TPU v7x, 32 devices: a whole 2x2x4 slice. The times are simulated.
32 devices in a mesh: batch: 8 (over y, x, core), head: 4 (over z).
Axes of the slice: x: 2, y: 2, z: 4, core: 2. Of those that a mesh axis runs over, the one named last changes fastest.
Arguments:
- tokens: bfloat16 [16384, 1152], P('batch'), may hold values from -6 to 6
- segments: int32 [16384], P('batch'), may hold values from 0 to 39, as said below
- item_cond: int32 [40], replicated, may hold values from 0 to 63
- condition: bfloat16 [64, 1152], replicated, may hold values from -6 to 6
- ada_weight: bfloat16 [1152, 6912], P(None, 'head'), may hold values from -0.1875 to 0.1875
- ada_bias: bfloat16 [6912], P('head'), may hold values from -3 to 3
- qkv_weight: bfloat16 [1152, 3456], P(None, 'head'), may hold values from -0.1875 to 0.1875
- qv_bias: bfloat16 [2304], P('head'), may hold values from -2 to 2
- proj_weight: bfloat16 [1152, 1152], P('head'), may hold values from -1.5 to 1.5
- proj_bias: bfloat16 [1152], replicated, may hold values from -2 to 2
- in_weight: bfloat16 [1152, 4608], P(None, 'head'), may hold values from -0.1875 to 0.1875
- in_bias: bfloat16 [4608], P('head'), may hold values from -2 to 2
- out_weight: bfloat16 [4608, 1152], P('head'), may hold values from -0.09375 to 0.09375
- out_bias: bfloat16 [1152], replicated, may hold values from -3 to 3
- cotangent: bfloat16 [16384, 1152], P('batch'), may hold values from -6 to 6
Outputs:
- block_out: bfloat16 [16384, 1152], P('batch', 'head')
- tokens_grad: bfloat16 [16384, 1152], P('batch', 'head')
- condition_grad: float32 [64, 1152], replicated
- ada_weight_grad: float32 [1152, 6912], P(None, 'head')
- ada_bias_grad: float32 [6912], P('head')
- qkv_weight_grad: float32 [1152, 3456], P(None, 'head')
- qv_bias_grad: float32 [2304], P('head')
- proj_weight_grad: float32 [1152, 1152], P('head')
- proj_bias_grad: float32 [1152], replicated
- in_weight_grad: float32 [1152, 4608], P(None, 'head')
- in_bias_grad: float32 [4608], P('head')
- out_weight_grad: float32 [4608, 1152], P('head')
- out_bias_grad: float32 [1152], replicated
Inputs may be any that keep to these rules, and one draw needn't show every extreme that they name: Tokens come in packed rows of 1024; each row holds either one segment or four segments of 256 tokens, and the 2 rows of each batch index hold 1 of each kind. Segment numbers never fall along the tokens and every number occurs.
All inputs are finite; a program needn't handle non-finite values.
Results may differ from a plain program's by a relative error of at most 0.02.
Values may be sent and summed in bfloat16 or wider, within the bound.
No kernel may reach another device: no remote copies, remote signals or barrier semaphores. Data moves between devices by JAX's collectives and lax.ppermute only.
A program may use at most 256 MiB of HBM per device.

v0:
```python
import math

import jax
import jax.numpy as jnp
from jax import lax
from jax.sharding import PartitionSpec as P

HEAD_DIM = 72
SEQ = 1024


norm_eps = 1e-06
neg_large = -1e30
gelu_coeff = 0.7978845608028654


def row_norm(values):
    center = jnp.mean(values, axis=-1, keepdims=True)
    shifted = values - center
    spread = jnp.mean(shifted * shifted, axis=-1, keepdims=True)
    inverse = lax.rsqrt(spread + norm_eps)
    return (shifted * inverse, inverse)


def norm_back(normed, inverse, grad_normed):
    first_mean = jnp.mean(grad_normed, axis=-1, keepdims=True)
    second_mean = jnp.mean(grad_normed * normed, axis=-1, keepdims=True)
    return inverse * (grad_normed - first_mean - normed * second_mean)


def gelu_tanh(values):
    inner = gelu_coeff * (values + 0.044715 * values * values * values)
    return 0.5 * values * (1.0 + jnp.tanh(inner))


def silu_act(values):
    return values / (1.0 + jnp.exp(-values))


def column_share(values, offset, share_width):
    return lax.dynamic_slice_in_dim(values, offset, share_width, 1)


def contract_rows(left_side, right_side):
    return lax.dot_general(
        left_side, right_side, (((0,), (0,)), ((), ())), preferred_element_type=jnp.float32
    )


def times_transpose(left_side, right_side):
    return lax.dot_general(
        left_side, right_side, (((1,), (1,)), ((), ())), preferred_element_type=jnp.float32
    )


def attend(block_data):
    queries, key_rows, value_rows, seg_row = block_data
    same_segment = seg_row[:, None] == seg_row[None, :]
    raw_scores = jnp.einsum("qhd,khd->hqk", queries, key_rows, preferred_element_type=jnp.float32)
    scores = jnp.where(
        same_segment[None], raw_scores * (1.0 / math.sqrt(queries.shape[-1])), neg_large
    )
    row_peak = jnp.max(scores, axis=-1, keepdims=True)
    exp_scores = jnp.exp(scores - row_peak)
    totals = jnp.sum(exp_scores, axis=-1, keepdims=True)
    probs_low = (exp_scores / totals).astype(jnp.bfloat16)
    mixed_heads = jnp.einsum(
        "hqk,khd->qhd", probs_low, value_rows, preferred_element_type=jnp.float32
    )
    log_totals = (row_peak + jnp.log(totals))[:, :, 0]
    return (mixed_heads.astype(jnp.bfloat16).reshape(queries.shape[0], -1), log_totals)


def attend_back(block_data):
    queries, key_rows, value_rows, seg_row, log_totals, grad_mixed = block_data
    key_scale = 1.0 / math.sqrt(queries.shape[-1])
    same_segment = seg_row[:, None] == seg_row[None, :]
    raw_scores = jnp.einsum("qhd,khd->hqk", queries, key_rows, preferred_element_type=jnp.float32)
    scores = jnp.where(same_segment[None], raw_scores * key_scale, neg_large)
    probs = jnp.exp(scores - log_totals[:, :, None])
    probs_low = probs.astype(jnp.bfloat16)
    grad_values = jnp.einsum(
        "hqk,qhd->khd", probs_low, grad_mixed, preferred_element_type=jnp.float32
    )
    grad_probs = jnp.einsum(
        "qhd,khd->hqk", grad_mixed, value_rows, preferred_element_type=jnp.float32
    )
    inner_sum = jnp.sum(probs * grad_probs, axis=-1, keepdims=True)
    grad_raw = (key_scale * (probs * (grad_probs - inner_sum))).astype(jnp.bfloat16)
    grad_queries = jnp.einsum(
        "hqk,khd->qhd", grad_raw, key_rows, preferred_element_type=jnp.float32
    )
    grad_keys = jnp.einsum("hqk,qhd->khd", grad_raw, queries, preferred_element_type=jnp.float32)
    stacked = jnp.stack([grad_queries, grad_keys, grad_values], axis=2)
    return stacked.astype(jnp.bfloat16).reshape(queries.shape[0], -1)


def shards(
    tokens,
    segments,
    item_cond,
    condition,
    ada_weight,
    ada_bias,
    qkv_weight,
    qv_bias,
    proj_weight,
    proj_bias,
    in_weight,
    in_bias,
    out_weight,
    out_bias,
    cotangent,
):
    token_count = tokens.shape[0]
    feature_width = tokens.shape[1]
    head_size = HEAD_DIM
    heads_here = qv_bias.shape[0] // (2 * head_size)
    feature_share = feature_width // lax.axis_size("head")
    offset = lax.axis_index("head") * feature_share
    packed_rows = token_count // SEQ
    quarter = SEQ // 4
    block_total = token_count // quarter
    cond_float = condition.astype(jnp.float32)
    cond_low = silu_act(cond_float).astype(jnp.bfloat16)
    table_part = jnp.dot(
        cond_low, ada_weight, preferred_element_type=jnp.float32
    ) + ada_bias.astype(jnp.float32)
    mod_table = lax.all_gather(table_part, "head", axis=1, tiled=True)
    block_class = jnp.take(item_cond, segments.reshape(block_total, quarter)[:, 0], axis=0)
    class_count = mod_table.shape[0]
    block_onehot = (
        block_class[:, None] == lax.broadcasted_iota(jnp.int32, (block_total, class_count), 1)
    ).astype(jnp.float32)
    block_mods = jnp.dot(
        block_onehot, mod_table, precision=lax.Precision.HIGHEST, preferred_element_type=jnp.float32
    )

    def spread_rows(block_rows):
        width = block_rows.shape[1]
        return jnp.broadcast_to(block_rows[:, None, :], (block_total, quarter, width)).reshape(
            token_count, width
        )

    def modulation(group):
        return spread_rows(block_mods[:, group * feature_width : (group + 1) * feature_width])

    def modulation_share(group):
        return spread_rows(column_share(block_mods, group * feature_width + offset, feature_share))

    def class_sum(row_grads):
        block_sums = jnp.sum(row_grads.reshape(block_total, quarter, row_grads.shape[1]), axis=1)
        return jnp.dot(
            block_onehot.T,
            block_sums,
            precision=lax.Precision.HIGHEST,
            preferred_element_type=jnp.float32,
        )

    tokens_f = tokens.astype(jnp.float32)
    tokens_share = column_share(tokens_f, offset, feature_share)
    normed_one, inverse_one = row_norm(tokens_f)
    scale_one = modulation(1)
    attn_in = (normed_one * (1.0 + scale_one) + modulation(0)).astype(jnp.bfloat16)
    bias_pairs = qv_bias.astype(jnp.float32).reshape(heads_here, 2, head_size)
    zero_keys = jnp.zeros((heads_here, 1, head_size), jnp.float32)
    full_bias = jnp.concatenate([bias_pairs[:, :1], zero_keys, bias_pairs[:, 1:]], axis=1).reshape(
        -1
    )
    projected = (
        jnp.dot(attn_in, qkv_weight, preferred_element_type=jnp.float32) + full_bias
    ).astype(jnp.bfloat16)
    grouped = projected.reshape(packed_rows, SEQ, heads_here, 3, head_size)
    seg_rows = segments.reshape(packed_rows, SEQ)
    head_rows, log_totals = lax.map(
        attend, (grouped[:, :, :, 0], grouped[:, :, :, 1], grouped[:, :, :, 2], seg_rows)
    )
    mixed = head_rows.reshape(token_count, -1)
    attn_part = jnp.dot(mixed, proj_weight, preferred_element_type=jnp.float32).astype(jnp.bfloat16)
    attn_share = lax.psum_scatter(attn_part, "head", scatter_dimension=1, tiled=True).astype(
        jnp.float32
    ) + column_share(proj_bias.astype(jnp.float32)[None, :], offset, feature_share)
    stream_share = tokens_share + modulation_share(2) * attn_share
    stream_low = lax.all_gather(stream_share.astype(jnp.bfloat16), "head", axis=1, tiled=True)
    normed_two, inverse_two = row_norm(stream_low.astype(jnp.float32))
    scale_two = modulation(4)
    mlp_in = (normed_two * (1.0 + scale_two) + modulation(3)).astype(jnp.bfloat16)
    pre_act = jnp.dot(mlp_in, in_weight, preferred_element_type=jnp.float32) + in_bias.astype(
        jnp.float32
    )
    hidden = gelu_tanh(pre_act).astype(jnp.bfloat16)
    mlp_part = jnp.dot(hidden, out_weight, preferred_element_type=jnp.float32).astype(jnp.bfloat16)
    mlp_share = lax.psum_scatter(mlp_part, "head", scatter_dimension=1, tiled=True).astype(
        jnp.float32
    ) + column_share(out_bias.astype(jnp.float32)[None, :], offset, feature_share)
    block_out = (stream_share + modulation_share(5) * mlp_share).astype(jnp.bfloat16)

    def through_norm(grad_partial, normed, inverse, scale_rows):
        grad_normed = grad_partial * (1.0 + scale_rows)
        norm_term = norm_back(normed, inverse, grad_normed)
        share_grad = lax.psum_scatter(
            norm_term.astype(jnp.bfloat16), "head", scatter_dimension=1, tiled=True
        ).astype(jnp.float32)
        return (share_grad, class_sum(grad_partial), class_sum(grad_partial * normed), 0)

    grad_out = cotangent.astype(jnp.float32)
    grad_out_share = column_share(grad_out, offset, feature_share)
    grad_mlp = (grad_out * modulation(5)).astype(jnp.bfloat16)
    out_bias_part = jnp.sum(grad_mlp.astype(jnp.float32), axis=0)
    out_weight_part = contract_rows(hidden, grad_mlp)
    grad_hidden = times_transpose(grad_mlp, out_weight)
    grad_pre = jax.vjp(gelu_tanh, pre_act)[1](grad_hidden)[0].astype(jnp.bfloat16)
    in_bias_part = jnp.sum(grad_pre.astype(jnp.float32), axis=0)
    in_weight_part = contract_rows(mlp_in, grad_pre)
    grad_mlp_in = times_transpose(grad_pre, in_weight)
    stream_part, shift_two_sum, scale_two_sum, start_two = through_norm(
        grad_mlp_in, normed_two, inverse_two, scale_two
    )
    stream_grad = grad_out_share + stream_part
    stream_grad_low = stream_grad.astype(jnp.bfloat16)
    stream_grad_rows = lax.all_gather(stream_grad_low, "head", axis=1, tiled=True)
    gate_one_sum = class_sum(stream_grad_low.astype(jnp.float32) * attn_share)
    gate_two_sum = class_sum(grad_out_share * mlp_share)
    grad_attn = (stream_grad_rows.astype(jnp.float32) * modulation(2)).astype(jnp.bfloat16)
    proj_bias_part = jnp.sum(grad_attn.astype(jnp.float32), axis=0)
    proj_weight_part = contract_rows(mixed, grad_attn)
    grad_mixed = (
        times_transpose(grad_attn, proj_weight)
        .astype(jnp.bfloat16)
        .reshape(packed_rows, SEQ, heads_here, head_size)
    )
    grad_rows = lax.map(
        attend_back,
        (
            grouped[:, :, :, 0],
            grouped[:, :, :, 1],
            grouped[:, :, :, 2],
            seg_rows,
            log_totals,
            grad_mixed,
        ),
    )
    grad_projected = grad_rows.reshape(token_count, -1)
    qkv_weight_part = contract_rows(attn_in, grad_projected)
    column_sums = jnp.sum(grad_projected.astype(jnp.float32), axis=0).reshape(
        heads_here, 3, head_size
    )
    qv_bias_part = jnp.concatenate([column_sums[:, :1], column_sums[:, 2:]], axis=1).reshape(-1)
    grad_attn_in = times_transpose(grad_projected, qkv_weight)
    input_part, shift_one_sum, scale_one_sum, start_one = through_norm(
        grad_attn_in, normed_one, inverse_one, scale_one
    )
    tokens_grad = (stream_grad + input_part).astype(jnp.bfloat16)
    mod_total = jnp.zeros((class_count, 6 * feature_width), jnp.float32)
    mod_total = lax.dynamic_update_slice(mod_total, shift_one_sum, (0, start_one))
    mod_total = lax.dynamic_update_slice(mod_total, scale_one_sum, (0, feature_width + start_one))
    mod_total = lax.dynamic_update_slice(mod_total, gate_one_sum, (0, 2 * feature_width + offset))
    mod_total = lax.dynamic_update_slice(
        mod_total, shift_two_sum, (0, 3 * feature_width + start_two)
    )
    mod_total = lax.dynamic_update_slice(
        mod_total, scale_two_sum, (0, 4 * feature_width + start_two)
    )
    mod_total = lax.dynamic_update_slice(mod_total, gate_two_sum, (0, 5 * feature_width + offset))
    mod_grad = lax.psum(mod_total, ("batch", "head")).astype(jnp.bfloat16)
    ada_columns = ada_weight.shape[1]
    mod_share = column_share(mod_grad, lax.axis_index("head") * ada_columns, ada_columns)
    ada_weight_grad = contract_rows(cond_low, mod_share)
    ada_bias_grad = jnp.sum(mod_share.astype(jnp.float32), axis=0)
    cond_part = times_transpose(mod_share, ada_weight)
    cond_total = lax.psum(cond_part.astype(jnp.bfloat16), "head").astype(jnp.float32)
    condition_grad = jax.vjp(silu_act, cond_float)[1](cond_total)[0]
    summed = (
        lax.psum(qkv_weight_part.astype(jnp.bfloat16), "batch").astype(jnp.float32),
        lax.psum(qv_bias_part.astype(jnp.bfloat16), "batch").astype(jnp.float32),
        lax.psum(proj_weight_part.astype(jnp.bfloat16), "batch").astype(jnp.float32),
        lax.psum(proj_bias_part.astype(jnp.bfloat16), "batch").astype(jnp.float32),
        lax.psum(in_weight_part.astype(jnp.bfloat16), "batch").astype(jnp.float32),
        lax.psum(in_bias_part.astype(jnp.bfloat16), "batch").astype(jnp.float32),
        lax.psum(out_weight_part.astype(jnp.bfloat16), "batch").astype(jnp.float32),
        lax.psum(out_bias_part.astype(jnp.bfloat16), "batch").astype(jnp.float32),
    )
    return (
        block_out,
        tokens_grad,
        condition_grad,
        ada_weight_grad,
        ada_bias_grad,
        summed[0],
        summed[1],
        summed[2],
        summed[3],
        summed[4],
        summed[5],
        summed[6],
        summed[7],
    )


def solution(mesh):
    in_specs = (
        P("batch", None),
        P("batch"),
        P(),
        P(),
        P(None, "head"),
        P("head"),
        P(None, "head"),
        P("head"),
        P("head", None),
        P(),
        P(None, "head"),
        P("head"),
        P("head", None),
        P(),
        P("batch", None),
    )
    out_specs = (
        P("batch", "head"),
        P("batch", "head"),
        P(),
        P(None, "head"),
        P("head"),
        P(None, "head"),
        P("head"),
        P("head", None),
        P(),
        P(None, "head"),
        P("head"),
        P("head", None),
        P(),
    )
    return jax.shard_map(shards, mesh=mesh, in_specs=in_specs, out_specs=out_specs, check_vma=False)
```

profile of v0, /device:TPU:9, one launch (start us, length us, event | category | flops | bytes accessed | tf_op | source)
XLA Modules:
  0.0 1206.9 jit_solution(18172485665829859361)
XLA Ops:
  25.8 27.9 %all-gather.9.cloned.1.call-done = f32[4,1728,64]{1,2,0:T(8,128)} async-done(((f32[1,1728,64]{1,2,0:T(8,128)}), f32[4,1728,64]{1,2,0:T(8,128)}) %all-gather.9.cloned.1.call-update) | async-done | bytes 1769488 | tf_op jit(solution)/shard_map/all_gather | solution.py:129
  83.7 14.8 %copy.140 = f32[144,8,8,256]{3,1,2,0:T(8,128)} copy(f32[144,8,8,256]{3,2,1,0:T(8,128)} %bitcast.213) | data formatting | bytes 18874368
  129.2 33.1 %while.22 = (s32[]{:T(128)}, bf16[2,1024,288]{1,2,0:T(8,128)(2,1)}, f32[2,4,1024]{2,1,0:T(4,128)S(1)}, bf16[2,1024,4,72]{1,3,2,0:T(8,128)(2,1)}, s32[2,1024]{1,0...) while((s32[]{:T(128)}, bf16[2,1024,288]{1,2,0:T(8,128)(2,1)}, ...), condition=%wide.region_5.6_spmd, body=%wide.region_2.0_spmd.sunk | while | flops 1259630592 | bytes 67646632 | solution.py:175
  182.6 73.2 %reduce-scatter.5.cloned.1.call-done = bf16[2048,288]{0,1:T(8,128)(2,1)} async-done(((bf16[2048,1152]{0,1:T(8,128)(2,1)}), bf16[2048,288]{0,1:T(8,128)(2,1)}) %reduce-scatter.5.cloned.1.call-update) | async-done | bytes 1179664 | tf_op jit(solution)/shard_map/reduce_scatter | solution.py:180
  300.2 12.1 fusion.128
  324.1 23.4 %all-gather.5.cloned.1.call-done = bf16[2048,1152]{0,1:T(8,128)(2,1)} async-done(((bf16[2048,288]{0,1:T(8,128)(2,1)}), bf16[2048,1152]{0,1:T(8,128)(2,1)}) %all-gather.5.cloned.1.call-update) | async-done | bytes 4718608 | tf_op jit(solution)/shard_map/all_gather | solution.py:184
  361.7 17.3 %fusion.129 = (bf16[1152]{0:T(1024)(128)(2,1)}, bf16[2048,1152]{1,0:T(8,128)(2,1)S(1)}, f32[2048,1152]{1,0:T(8,128)}) fusion(f32[2048,1152]{1,0:T(8,128)S(1)} %bitcast.244, f32[1152]{0:T(1024)S(1)} %convert_element_type.195, bf16[2048,1152]{0,1:T(8,128)(2,1)S(1)} %fusion.77, bf16[1152,1152]{1,0:T(8,128)(2,1)S(1)} %copy-done), kind=kOutput, calls=%fused_computation.186 | convolution fusion | flops 5497158656 | bytes 30972672 | tf_op jit(solution)/shard_map/dot_general | solution.py:188
  398.4 17.3 %fusion.127 = (f32[2048]{0:T(1024)S(1)}, f32[2048]{0:T(1024)S(1)}, f32[2048,1152]{0,1:T(8,128)}, f32[2048,1152]{0,1:T(8,128)}) fusion(f32[2048]{0:T(1024)S(1)} %add_rsqrt_fusion, f32[2048]{0:T(1024)S(1)} %broadcast_multiply_fusion.4, bf16[2048,1152]{0,1:T(8,128)(2,1)} %all-gather.5.cloned.1.call-done, f32[2048,1152]{0,1:T(8,128)} %copy.123, ...), kind=kLoop, calls=%fused_computation.184 | loop fusion | flops 18870272 | bytes 42500096 | tf_op jit(solution)/shard_map/reduce_sum | solution.py:26
  424.0 86.5 %reduce-scatter.9.cloned.1.call-done = bf16[2048,288]{0,1:T(8,128)(2,1)} async-done(((bf16[2048,1152]{0,1:T(8,128)(2,1)}), bf16[2048,288]{0,1:T(8,128)(2,1)}) %reduce-scatter.9.cloned.1.call-update) | async-done | bytes 1179664 | tf_op jit(solution)/shard_map/reduce_scatter | solution.py:201
  536.2 14.9 %convolution_convert_fusion.2 = bf16[1152,1152]{1,0:T(8,128)(2,1)} fusion(bf16[2048,1152]{0,1:T(8,128)(2,1)} %get-tuple-element.171, f32[2048,1152]{1,0:T(8,128)} %get-tuple-element.205), kind=kOutput, calls=%fused_computation.106 | convolution fusion | flops 5458378752 | bytes 16809984 | tf_op jit(solution)/shard_map/dot_general | solution.py:45
  551.1 51.5 %all-gather.7.cloned.1.call-done = bf16[2048,1152]{0,1:T(8,128)(2,1)} async-done(((bf16[2048,288]{0,1:T(8,128)(2,1)}), bf16[2048,1152]{0,1:T(8,128)(2,1)}) %all-gather.7.cloned.1.call-update) | async-done | bytes 4718608 | tf_op jit(solution)/shard_map/all_gather | solution.py:221
  616.0 159.3 %while.23 = (s32[]{:T(128)}, bf16[2,1024,864]{1,2,0:T(8,128)(2,1)}, bf16[2,1024,4,72]{1,3,2,0:T(8,128)(2,1)}, s32[2,1024]{1,0:T(2,128)S(1)}, bf16[2,1024,4,72]{1...) while((s32[]{:T(128)}, bf16[2,1024,864]{1,2,0:T(8,128)(2,1)}, ...), condition=%wide.region_15.16_spmd, body=%wide.region_13.15_spmd.sunk | while | flops 3082332160 | bytes 236255440 | solution.py:232
  646.8 22.1 %fusion.206 = bf16[1024,4,1,72]{0,3,1,2:T(8,128)(2,1)S(1)} fusion(f32[4,1024,1024]{1,2,0:T(8,128)} %subtract_exponential_fusion.3, f32[4,1024,1024]{1,2,0:T(8,128)} %fusion.204, bf16[2,1024,4,72]{1,3,2,0:T(8,128)(2,1)S(1)} %copy-done.22, s32[]{:T(128)S(6)} %copy.170), kind=kOutput, calls=%fused_computation.39.clone.1 | convolution fusion | flops 625251328 | bytes 68288512 | tf_op jit(solution)/shard_map/while/body/eval_jaxpr/hqk,khd->qhd/dot_general | solution.py:90
  669.0 22.8 %fusion.205 = bf16[1024,4,1,72]{0,3,1,2:T(8,128)(2,1)S(1)} fusion(f32[4,1024,1024]{1,2,0:T(8,128)} %subtract_exponential_fusion.3, f32[4,1024,1024]{1,2,0:T(8,128)} %fusion.204, bf16[2,1024,4,72]{1,3,2,0:T(8,128)(2,1)} %get-tuple-element.354, s32[]{:T(128)S(6)} %copy.170), kind=kOutput, calls=%fused_computation.38.clone.1 | convolution fusion | flops 625251328 | bytes 68288512 | tf_op jit(solution)/shard_map/while/body/eval_jaxpr/hqk,qhd->khd/dot_general | solution.py:93
  726.1 22.1 %fusion.206 = bf16[1024,4,1,72]{0,3,1,2:T(8,128)(2,1)S(1)} fusion(f32[4,1024,1024]{1,2,0:T(8,128)} %subtract_exponential_fusion.3, f32[4,1024,1024]{1,2,0:T(8,128)} %fusion.204, bf16[2,1024,4,72]{1,3,2,0:T(8,128)(2,1)S(1)} %copy-done.22, s32[]{:T(128)S(6)} %copy.170), kind=kOutput, calls=%fused_computation.39.clone.1 | convolution fusion | flops 625251328 | bytes 68288512 | tf_op jit(solution)/shard_map/while/body/eval_jaxpr/hqk,khd->qhd/dot_general | solution.py:90
  748.3 22.8 %fusion.205 = bf16[1024,4,1,72]{0,3,1,2:T(8,128)(2,1)S(1)} fusion(f32[4,1024,1024]{1,2,0:T(8,128)} %subtract_exponential_fusion.3, f32[4,1024,1024]{1,2,0:T(8,128)} %fusion.204, bf16[2,1024,4,72]{1,3,2,0:T(8,128)(2,1)} %get-tuple-element.354, s32[]{:T(128)S(6)} %copy.170), kind=kOutput, calls=%fused_computation.38.clone.1 | convolution fusion | flops 625251328 | bytes 68288512 | tf_op jit(solution)/shard_map/while/body/eval_jaxpr/hqk,qhd->khd/dot_general | solution.py:93
  824.1 17.3 %fusion.126 = (f32[2048]{0:T(1024)S(1)}, f32[2048]{0:T(1024)S(1)}, f32[2048,1152]{0,1:T(8,128)}, f32[2048,1152]{0,1:T(8,128)}) fusion(f32[2048]{0:T(1024)S(1)} %copy-done.35, f32[2048]{0:T(1024)S(1)} %copy-done.27, bf16[2048,1152]{0,1:T(8,128)(2,1)} %copy.108, f32[2048,1152]{0,1:T(8,128)} %copy.127, f32[2048,1152]{0,1:T(8,128)} %bitcast.206), kind=kLoop, calls=%fused_computation.183 | loop fusion | flops 18870272 | bytes 42500096 | tf_op jit(solution)/shard_map/reduce_sum | solution.py:26
  853.7 11.9 copy.148
  878.2 22.8 %all-reduce.1 = (bf16[576]{0:T(1024)(128)(2,1)S(1)}, bf16[1152]{0:T(1024)(128)(2,1)S(1)}, bf16[1152]{0:T(1024)(128)(2,1)S(1)}, bf16[1152]{0:T(1024)(128)(2,1)S(1)}) all-reduce(bf16[576]{0:T(1024)(128)(2,1)S(1)} %convert_element_type.221, bf16[1152]{0:T(1024)(128)(2,1)S(1)} %copy-done.43, ...), channel_id=1, replica_groups=mesh['batch'=8,'head'=4] {'batch'}, use_global_device_ids=true, to_apply=%region_30.31 | all-reduce | flops 4032 | bytes 16128 | tf_op jit(solution)/shard_map/psum | solution.py:275
  903.9 12.1 %copy.146 = f32[144,8,8,256]{3,2,1,0:T(8,128)} copy(f32[144,8,8,256]{3,1,2,0:T(8,128)} %bitcast.221) | data formatting | bytes 18874368
  935.9 68.1 %reduce-scatter.7.cloned.1.call-done = bf16[2048,288]{0,1:T(8,128)(2,1)} async-done(((bf16[2048,1152]{0,1:T(8,128)(2,1)}), bf16[2048,288]{0,1:T(8,128)(2,1)}) %reduce-scatter.7.cloned.1.call-update) | async-done | bytes 1179664 | tf_op jit(solution)/shard_map/reduce_scatter | solution.py:193
  1004.0 88.2 %reduce-scatter.11.cloned.1.call-done = bf16[2048,288]{0,1:T(8,128)(2,1)} async-done(((bf16[2048,1152]{0,1:T(8,128)(2,1)}), bf16[2048,288]{0,1:T(8,128)(2,1)}) %reduce-scatter.11.cloned.1.call-update) | async-done | bytes 1179664 | tf_op jit(solution)/shard_map/reduce_scatter | solution.py:201
  1103.5 56.6 %all-reduce.10 = bf16[64,6912]{1,0:T(8,128)(2,1)S(1)} all-reduce(f32[64,6912]{1,0:T(8,128)} %dynamic_update_slice.35), channel_id=1, replica_groups=mesh['batch'=8,'head'=4] {'batch','head'}, use_global_device_ids=true, to_apply=%region_25.26 | all-reduce | flops 442368 | bytes 2654208 | tf_op jit(solution)/shard_map/psum | solution.py:265
  1169.0 29.4 %all-reduce.7.cloned.1.call-done = bf16[64,1152]{1,0:T(8,128)(2,1)} async-done(((bf16[64,1152]{1,0:T(8,128)(2,1)}), bf16[64,1152]{1,0:T(8,128)(2,1)}) %all-reduce.7.cloned.1.call-update) | async-done | bytes 147472 | tf_op jit(solution)/shard_map/psum | solution.py:271
  (317 shorter events, 455.7 us)
Async XLA Ops:
  7.2 354.4 %copy-start = (bf16[1152,1152]{1,0:T(8,128)(2,1)S(1)}, bf16[1152,1152]{1,0:T(8,128)(2,1)}, u32[]{:S(2)}) copy-start(bf16[1152,1152]{1,0:T(8,128)(2,1)} %param.29) | copy-start | bytes 7962628
  7.2 46.5 %all-gather.9.cloned.1.call-start = ((), (), s32[]{:S(2)}) async-start(), calls=%async_computation.11 | async-start | bytes 2293760 | tf_op jit(solution)/shard_map/all_gather | solution.py:129
  12.4 243.4 %reduce-scatter.5.cloned.1.call-start = ((), (), s32[]{:S(2)}) async-start(), calls=%async_computation.4 | async-start | bytes 5898240 | tf_op jit(solution)/shard_map/reduce_scatter | solution.py:180
  20.4 40.5 %copy-start.38 = (s32[8]{0:T(128)}, s32[8]{0:T(128)S(1)}, u32[]{:S(2)}) copy-start(s32[8]{0:T(128)S(1)} %select_reduce_fusion) | copy-start | bytes 100
  24.5 74.0 %copy-start.26 = (f32[2048]{0:T(1024)}, f32[2048]{0:T(1024)S(1)}, u32[]{:S(2)}) copy-start(f32[2048]{0:T(1024)S(1)} %broadcast_multiply_fusion.5) | copy-start | bytes 24580
  25.8 72.7 %copy-start.34 = (f32[2048]{0:T(1024)}, f32[2048]{0:T(1024)S(1)}, u32[]{:S(2)}) copy-start(f32[2048]{0:T(1024)S(1)} %add_rsqrt_fusion.1) | copy-start | bytes 24580
  78.7 19.7 %copy-start.5 = (f32[144,8,8,256]{3,1,2,0:T(8,128)}, f32[144,8,8,256]{3,1,2,0:T(8,128)S(1)}, u32[]{:S(2)}) copy-start(f32[144,8,8,256]{3,1,2,0:T(8,128)S(1)} %copy.139) | copy-start | bytes 28311556
  78.8 19.7 %slice-start = ((s8[4718592]{0:T(1024)(128)(4,1)}), s8[4194304]{0:T(1024)(128)(4,1)S(1)}, s32[]{:S(2)}) async-start(s8[4718592]{0:T(1024)(128)(4,1)} %bitcast.198), calls=%async_computation.13 | async-start | bytes 8388608
  170.0 177.4 %all-gather.5.cloned.1.call-start = ((), (), s32[]{:S(2)}) async-start(), calls=%async_computation.5 | async-start | bytes 5898240 | tf_op jit(solution)/shard_map/all_gather | solution.py:184
  178.2 332.3 %copy-start.41 = (f32[288]{0:T(512)}, f32[288]{0:T(512)S(1)}, u32[]{:S(2)}) copy-start(f32[288]{0:T(512)S(1)} %dynamic-slice_convert_fusion.2) | copy-start | bytes 3460
  182.6 77.5 %copy-start.45 = (bf16[1152]{0:T(1024)(128)(2,1)S(1)}, bf16[1152]{0:T(1024)(128)(2,1)}, u32[]{:S(2)}) copy-start(bf16[1152]{0:T(1024)(128)(2,1)} %param.30) | copy-start | bytes 6916
  260.0 250.5 %reduce-scatter.9.cloned.1.call-start = ((), (), s32[]{:S(2)}) async-start(), calls=%async_computation.7 | async-start | bytes 5898240 | tf_op jit(solution)/shard_map/reduce_scatter | solution.py:201
  388.8 26.9 %slice-start.4 = ((s8[4718592]{0:T(1024)(128)(4,1)}), s8[524288]{0:T(1024)(128)(4,1)S(1)}, s32[]{:S(2)}) async-start(s8[4718592]{0:T(1024)(128)(4,1)} %bitcast.203), calls=%async_computation.17 | async-start | bytes 1048576
  424.0 86.6 %copy-start.9 = (bf16[2048,288]{0,1:T(8,128)(2,1)S(1)}, bf16[2048,288]{0,1:T(8,128)(2,1)}, u32[]{:S(2)}) copy-start(bf16[2048,288]{0,1:T(8,128)(2,1)} %reduce-scatter.5.cloned.1.call-done) | copy-start | bytes 3538948
  424.0 178.6 %all-gather.7.cloned.1.call-start = ((), (), s32[]{:S(2)}) async-start(), calls=%async_computation.8 | async-start | bytes 5898240 | tf_op jit(solution)/shard_map/all_gather | solution.py:221
  515.1 408.6 %all-reduce.9.cloned.1.call-start = ((), (), s32[]{:S(2)}) async-start(), calls=%async_computation.12 | async-start | bytes 15925248 | tf_op jit(solution)/shard_map/psum | solution.py:274
  790.9 213.2 %reduce-scatter.7.cloned.1.call-start = ((), (), s32[]{:S(2)}) async-start(), calls=%async_computation.6 | async-start | bytes 5898240 | tf_op jit(solution)/shard_map/reduce_scatter | solution.py:193
  803.3 288.9 %reduce-scatter.11.cloned.1.call-start = ((), (), s32[]{:S(2)}) async-start(), calls=%async_computation.9 | async-start | bytes 5898240 | tf_op jit(solution)/shard_map/reduce_scatter | solution.py:201
  814.3 27.1 %slice-start.2 = ((s8[4718592]{0:T(1024)(128)(4,1)}), s8[524288]{0:T(1024)(128)(4,1)S(1)}, s32[]{:S(2)}) async-start(s8[4718592]{0:T(1024)(128)(4,1)} %bitcast.200), calls=%async_computation.15 | async-start | bytes 1048576
  849.8 348.6 %all-reduce.7.cloned.1.call-start = ((), (), s32[]{:S(2)}) async-start(), calls=%async_computation.10 | async-start | bytes 294912 | tf_op jit(solution)/shard_map/psum | solution.py:271
  933.1 159.1 %copy-start.6 = (f32[36,8,8,256]{3,1,2,0:T(8,128)S(1)}, f32[36,8,8,256]{3,1,2,0:T(8,128)}, u32[]{:S(2)}) copy-start(f32[36,8,8,256]{3,1,2,0:T(8,128)} %copy.138) | copy-start | bytes 7077892
  933.1 159.1 %copy-start.42 = (f32[288]{0:T(512)S(1)}, f32[288]{0:T(512)}, u32[]{:S(2)}) copy-start(f32[288]{0:T(512)} %copy-done.41) | copy-start | bytes 3460
  1100.9 63.5 %copy-start.17 = (bf16[64,1152]{1,0:T(8,128)(2,1)S(1)}, bf16[64,1152]{1,0:T(8,128)(2,1)}, u32[]{:S(2)}) copy-start(bf16[64,1152]{1,0:T(8,128)(2,1)} %param.22) | copy-start | bytes 442372
  1164.5 35.7 %copy-start.1 = (bf16[1152,1152]{1,0:T(8,128)(2,1)S(1)}, bf16[1152,1152]{1,0:T(8,128)(2,1)}, u32[]{:S(2)}) copy-start(bf16[1152,1152]{1,0:T(8,128)(2,1)} %param.29) | copy-start | bytes 7962628
  (54 other events, 348.8 us)
Sparse Core Ops, SparseCore 0:
  12.5 41.1 all-gather.8
  170.2 85.5 reduce-scatter.4
  260.1 87.2 all-gather.4
  424.1 86.3 reduce-scatter.8
  515.3 87.2 all-gather.6
  791.0 124.3 all-reduce.8
  918.4 85.5 reduce-scatter.6
  1006.4 85.7 reduce-scatter.10
  1164.6 33.7 all-reduce.6
where the time goes:
time: 1220 us; the launch traced here: 1210 us
  waiting for transfers between devices  448 us (37%)
  matrix products  298 us (24%)
  local copies, waits for them, and re-layouts  201 us (16%)
  other arithmetic  163 us (13%)
  blocking collectives  79.3 us (6%)
  between operations  14.9 us (1%)
    reduce_scatter x2, waiting for transfers between devices, through_norm(): lax.psum_scatter(norm_term.astype(jnp.bfloat16), 'head', scatter_dimensio...  175 us
    unnamed x134, local copies, waits for them, and re-layouts  115 us
    reduce_scatter x1, waiting for transfers between devices, shards(): lax.psum_scatter(attn_part, 'head', scatter_dimension=1, tiled=True)  73.2 us
    reduce_scatter x1, waiting for transfers between devices, shards(): lax.psum_scatter(mlp_part, 'head', scatter_dimension=1, tiled=True)  68.1 us
    psum x1, blocking collectives, shards(): mod_grad = lax.psum(mod_total, ('batch', 'head')).astype(jnp.bfloat16)  56.6 us
    all_gather x1, waiting for transfers between devices, shards(): lax.all_gather(stream_grad_low, 'head', axis=1, tiled=True)  51.5 us
    dot_general x2, matrix products, attend_back(): jnp.einsum('hqk,qhd->khd', grad_raw, queries, preferred_element_type=jnp....  45.6 us
    dot_general x2, matrix products, attend_back(): jnp.einsum('hqk,khd->qhd', grad_raw, key_rows, preferred_element_type=jnp...  44.3 us
  transfers between devices with their start and end apart: 9, of which 8 were waited for; matrix products, arithmetic and copies ran while one was open for 21% of the time, Pallas kernels for 0%

commit v1 on v0

v1 whole, which is shorter than its diff:
```python
import functools
import math

import jax
import jax.numpy as jnp
from jax import lax
from jax.experimental import pallas as pl
from jax.experimental.pallas import tpu as pltpu
from jax.sharding import PartitionSpec as P

HEAD_DIM = 72
SEQ = 1024
LOG2E = 1.4426950408889634
KEY_SCALE = 1.0 / math.sqrt(HEAD_DIM)


def nt(a, b):
    return lax.dot_general(a, b, (((1,), (1,)), ((), ())), preferred_element_type=jnp.float32)


def nn(a, b):
    return lax.dot_general(a, b, (((1,), (0,)), ((), ())), preferred_element_type=jnp.float32)


def attend_kernel(heads, chunk, groups, split, proj_ref, mixed_ref, lse_ref):
    seq = proj_ref.shape[1]
    home = seq // groups
    group = lax.axis_index("head")
    width = 3 * HEAD_DIM
    key_count = chunk if split else seq

    def part(head, start):
        at = head * width
        rows = pl.ds(start, chunk)
        keys = pl.ds(start if split else 0, key_count)
        queries = proj_ref[0, rows, at : at + HEAD_DIM]
        key_rows = proj_ref[0, keys, at + HEAD_DIM : at + 2 * HEAD_DIM]
        value_rows = proj_ref[0, keys, at + 2 * HEAD_DIM : at + 3 * HEAD_DIM]
        scores = nt(key_rows, queries)
        peak = jnp.max(scores, axis=0, keepdims=True)
        weights = jnp.exp2((scores - peak) * (KEY_SCALE * LOG2E))
        total = jnp.sum(weights, axis=0, keepdims=True)
        mixed_t = nn(value_rows.T, weights.astype(jnp.bfloat16)) / total
        lse_ref[0, head : head + 1, rows] = peak * (KEY_SCALE * LOG2E) + jnp.log2(total)
        return mixed_t.T

    def step(index, _):
        start = pl.multiple_of(index * chunk, chunk)
        outs = [part(head, start) for head in range(heads)]
        outs = jnp.concatenate(outs, axis=1).astype(jnp.bfloat16)
        for spot in range(chunk // home):
            target = index * (chunk // home) + spot
            mixed_ref[(group - target + groups) % groups, 0] = outs[spot * home : (spot + 1) * home]
        return 0

    lax.fori_loop(0, seq // chunk, step, 0)


def attend(projected, row, heads, chunk, groups, order):
    seq, width = projected.shape[1:]
    split = row == 0
    return call(
        functools.partial(attend_kernel, heads, chunk, groups, split),
        [
            shape_of((groups, 1, seq // groups, heads * HEAD_DIM), jnp.bfloat16),
            shape_of((1, heads, seq), jnp.float32),
        ],
        [pl.BlockSpec((1, seq, width), lambda i: (row, 0, 0))],
        [
            pl.BlockSpec((groups, 1, seq // groups, heads * HEAD_DIM), lambda i: (0, 0, 0, 0)),
            pl.BlockSpec((1, heads, seq), lambda i: (0, 0, 0)),
        ],
        grid=(1,),
        name="attend_split" if split else "attend_whole",
        micros=6 if split else 16,
        order=order,
    )(projected)


def attend_back_kernel(heads, chunk, groups, split, proj_ref, lse_ref, pieces_ref, out_ref, dk_ref, dv_ref, grad_ref):
    seq = proj_ref.shape[1]
    home = seq // groups
    group = lax.axis_index("head")
    width = 3 * HEAD_DIM
    key_count = chunk if split else seq
    for spot in range(groups):
        grad_ref[spot * home : (spot + 1) * home, :] = pieces_ref[(group - spot + groups) % groups, 0]

    def part(head, start):
        at = head * width
        rows = pl.ds(start, chunk)
        keys = pl.ds(start if split else 0, key_count)
        queries = proj_ref[0, rows, at : at + HEAD_DIM]
        key_rows = proj_ref[0, keys, at + HEAD_DIM : at + 2 * HEAD_DIM]
        value_rows = proj_ref[0, keys, at + 2 * HEAD_DIM : at + 3 * HEAD_DIM]
        grads = grad_ref[rows, head * HEAD_DIM : (head + 1) * HEAD_DIM]
        scores = nt(key_rows, queries)
        probs = jnp.exp2(scores * (KEY_SCALE * LOG2E) - lse_ref[0, head : head + 1, rows])
        grad_probs = nt(value_rows, grads)
        inner = jnp.sum(probs * grad_probs, axis=0, keepdims=True)
        grad_raw = (probs * (grad_probs - inner) * KEY_SCALE).astype(jnp.bfloat16)
        grad_values = nn(probs.astype(jnp.bfloat16), grads)
        grad_keys = nn(grad_raw, queries)
        grad_queries = nn(key_rows.T, grad_raw).T
        return grad_queries, grad_keys, grad_values

    if not split:
        for head in range(heads):
            at = head * width
            dk_ref[...] = jnp.zeros_like(dk_ref)
            dv_ref[...] = jnp.zeros_like(dv_ref)

            def step(index, _):
                start = pl.multiple_of(index * chunk, chunk)
                dq, dk, dv = part(head, start)
                out_ref[0, pl.ds(start, chunk), at : at + HEAD_DIM] = dq.astype(jnp.bfloat16)
                dk_ref[...] += dk
                dv_ref[...] += dv
                return 0

            lax.fori_loop(0, seq // chunk, step, 0)
            both = jnp.concatenate([dk_ref[...], dv_ref[...]], axis=1).astype(jnp.bfloat16)
            out_ref[0, :, at + HEAD_DIM : at + 3 * HEAD_DIM] = both
    else:

        def step(index, _):
            start = pl.multiple_of(index * chunk, chunk)
            outs = [t for head in range(heads) for t in part(head, start)]
            out_ref[0, pl.ds(start, chunk), :] = jnp.concatenate(outs, axis=1).astype(jnp.bfloat16)
            return 0

        lax.fori_loop(0, seq // chunk, step, 0)


def attend_back(projected, row, lse, grads, heads, chunk, groups, order):
    seq, width = projected.shape[1:]
    split = row == 0

    return call(
        functools.partial(attend_back_kernel, heads, chunk, groups, split),
        shape_of((1, seq, width), jnp.bfloat16),
        [
            pl.BlockSpec((1, seq, width), lambda i: (row, 0, 0)),
            pl.BlockSpec((1, heads, seq), lambda i: (0, 0, 0)),
            pl.BlockSpec((groups, 1, seq // groups, heads * HEAD_DIM), lambda i: (0, 0, 0, 0)),
        ],
        pl.BlockSpec((1, seq, width), lambda i: (0, 0, 0)),
        grid=(1,),
        scratch=[pltpu.VMEM((seq, HEAD_DIM), jnp.float32)] * 2
        + [pltpu.VMEM((seq, heads * HEAD_DIM), jnp.bfloat16)],
        name="attend_back_split" if split else "attend_back_whole",
        micros=8 if split else 24,
        order=order,
    )(projected, lse, grads)


norm_eps = 1e-06
gelu_coeff = 0.7978845608028654
VMEM_BYTES = 58 * 1024 * 1024
UNIT_TILE = 384


def tn(left_side, right_side):
    return lax.dot_general(
        left_side, right_side, (((0,), (0,)), ((), ())), preferred_element_type=jnp.float32
    )


def row_norm(values):
    center = jnp.mean(values, axis=-1, keepdims=True)
    shifted = values - center
    spread = jnp.mean(shifted * shifted, axis=-1, keepdims=True)
    inverse = lax.rsqrt(spread + norm_eps)
    return (shifted * inverse, inverse)


def norm_back(normed, inverse, grad_normed):
    first_mean = jnp.mean(grad_normed, axis=-1, keepdims=True)
    second_mean = jnp.mean(grad_normed * normed, axis=-1, keepdims=True)
    return inverse * (grad_normed - first_mean - normed * second_mean)


def silu_act(values):
    return values / (1.0 + jnp.exp(-values))


def weight_of(micros):
    return pl.CostEstimate(flops=0, bytes_accessed=int(micros * 3.3e6), transcendentals=0)


def call(kernel, out_shape, in_specs, out_specs, grid=(), prefetch=0, scratch=(), name=None, micros=1, order=()):
    first = prefetch + len(in_specs)

    def ordered(*refs):
        kernel(*refs[:first], *refs[first + len(order) :])

    run = pl.pallas_call(
        ordered if order else kernel,
        grid_spec=pltpu.PrefetchScalarGridSpec(
            num_scalar_prefetch=prefetch,
            grid=grid,
            in_specs=list(in_specs) + [pl.BlockSpec(memory_space=pl.ANY)] * len(order),
            out_specs=out_specs,
            scratch_shapes=scratch,
        ),
        out_shape=out_shape,
        compiler_params=pltpu.CompilerParams(vmem_limit_bytes=VMEM_BYTES),
        cost_estimate=weight_of(micros),
        name=name,
    )
    return lambda *arrays: run(*arrays, *order)


def hold(values, *order):
    run = pl.pallas_call(
        lambda *refs: None,
        in_specs=[pl.BlockSpec(memory_space=pl.ANY)] * (1 + len(order)),
        out_specs=pl.BlockSpec(memory_space=pl.ANY),
        out_shape=shape_of(values.shape, values.dtype),
        input_output_aliases={0: 0},
        name="hold",
    )
    return run(values, *order)


def whole(shape):
    return pl.BlockSpec(shape, lambda *_: (0,) * len(shape))


SCALARS = pl.BlockSpec(memory_space=pltpu.SMEM)
shape_of = jax.ShapeDtypeStruct


class Links:
    def __init__(self, heads, batches):
        self.heads = heads
        self.batches = batches
        bits = batches.bit_length() - 1
        self.levels = bits - 1
        first = list(range(bits - 1, 0, -1))
        self.orders = (first, first[1:] + first[:1])

    def fetch(self, values, distance):
        count = self.heads
        return lax.ppermute(values, "head", [((i + distance) % count, i) for i in range(count)])

    def send(self, values, distance):
        count = self.heads
        return lax.ppermute(values, "head", [(i, (i + distance) % count) for i in range(count)])

    def core_swap(self, values):
        return lax.ppermute(values, "batch", [(i, i ^ 1) for i in range(self.batches)])

    def link_swap(self, values, level):
        pairs = [(i, i ^ (1 << self.orders[i & 1][level])) for i in range(self.batches)]
        return lax.ppermute(values, "batch", pairs)

    def owner(self, spot):
        batch = lax.axis_index("batch")
        half = spot >> self.levels
        masks = [
            sum(1 << order[level] for level in range(self.levels) if spot >> level & 1)
            for order in self.orders
        ]
        mask = jnp.where(batch % 2 == half, masks[0], masks[1])
        return (batch ^ half) ^ mask

    def place(self, index):
        batch = lax.axis_index("batch")
        way = batch ^ index
        half = way & 1
        spots = [
            sum(((way >> order[level]) & 1) << level for level in range(self.levels))
            for order in self.orders
        ]
        return (half << self.levels) + jnp.where((batch & 1) == half, spots[0], spots[1])

    def gather_levels(self, values, order=()):
        pieces = [values]
        for level in range(self.levels):
            joined = pieces[0] if level == 0 else jnp.concatenate(pieces, axis=0)
            more = self.link_swap(joined, level)
            if level == 0 and order:
                more = hold(more, *order)
            pieces = [joined, more]
        return pieces

    def gather_batch(self, values):
        own = jnp.concatenate(self.gather_levels(values), axis=0)
        return jnp.concatenate([own, self.core_swap(own)], axis=0)

    def reduce_levels(self, kept, orders=()):
        low = jnp.bfloat16
        steps = []
        for level in reversed(range(self.levels)):
            more = self.link_swap(kept[1], level)
            if len(orders) > len(steps):
                more = hold(more, orders[len(steps)])
            total = (kept[0].astype(jnp.float32) + more.astype(jnp.float32)).astype(low)
            half = total.shape[0] // 2
            kept = [total[:half], total[half:]]
            steps.append(total)
        return steps

    def by_owner(self, values):
        return jnp.concatenate(
            [lax.dynamic_index_in_dim(values, self.owner(i), 0) for i in range(self.batches)]
        )

    def by_index(self, values):
        return jnp.concatenate(
            [lax.dynamic_index_in_dim(values, self.place(i), 0) for i in range(self.batches)]
        )

    def at_head(self, distance):
        return (lax.axis_index("head") + distance) % self.heads


def mod_kernel(quarter, units_here, seg_ref, item_ref, cond_ref, ada_ref, bias_ref, in_bias_ref, table_ref, info_ref):
    starts = [[seg_ref[row * SEQ + spot * quarter] for spot in range(4)] for row in range(2)]
    first_splits = starts[0][0] != starts[0][3]
    ids = [jnp.where(first_splits, starts[1][0], starts[0][0])] + [
        jnp.where(first_splits, starts[0][spot], starts[1][spot]) for spot in range(4)
    ]
    classes = [item_ref[one] for one in ids]
    info_ref[0] = jnp.where(first_splits, 0, 1)
    info_ref[1] = lax.axis_index("head")
    info_ref[2] = 0
    for spot in range(5):
        info_ref[3 + spot] = classes[spot]
    cond_low = silu_act(cond_ref[...].astype(jnp.float32)).astype(jnp.bfloat16)
    count = cond_low.shape[0]
    row_spot = lax.broadcasted_iota(jnp.int32, (8, count), 0)
    wanted = jnp.full((8, count), count, jnp.int32)
    for spot in range(5):
        wanted = jnp.where(row_spot == spot, classes[spot], wanted)
    hits = (lax.broadcasted_iota(jnp.int32, (8, count), 1) == wanted).astype(jnp.float32)
    rows = nn(hits.astype(jnp.bfloat16), cond_low).astype(jnp.bfloat16)
    table_ref[...] = nt(rows, ada_ref[...]) + bias_ref[...]
    table_ref[5:6, :units_here] = in_bias_ref[...]


def project_kernel(heads, quarter, info_ref, table_rel_ref, tokens_ref, weight_ref, bias_ref, attn_in_ref, projected_ref, table_ref):
    block = pl.program_id(0)
    width = tokens_ref.shape[1]
    columns = table_rel_ref.shape[2]

    @pl.when(block == 0)
    def _():
        for head in range(heads):
            spot = (head - lax.axis_index("head") + heads) % heads
            table_ref[:, head * columns : (head + 1) * columns] = table_rel_ref[spot]

    row = jnp.where(block < 4, 1 + block % 4, 0)
    normed, _ = row_norm(tokens_ref[...].astype(jnp.float32))
    shift = table_ref[pl.ds(row, 1), :width]
    scale = table_ref[pl.ds(row, 1), width : 2 * width]
    attn_in = (normed * (1.0 + scale) + shift).astype(jnp.bfloat16)
    attn_in_ref[...] = attn_in
    projected_ref[...] = (nt(attn_in, weight_ref[...]) + bias_ref[...]).astype(jnp.bfloat16)


def home_row(info_ref, row, home, quarter):
    return jnp.where(row == 0, 1 + info_ref[1] * home // quarter, 0)


def enter_kernel(link, quarter, info_ref, table_ref, split_ref, single_ref, proj_ref, tokens_ref, grad_ref, bias_ref,
                 attn_ref, stream_ref, mlp_in_ref, grad_mlp_ref, mixed_home_ref, proj_true_ref, grad_sum_ref):
    row = pl.program_id(0)
    heads = link.heads
    home, width = tokens_ref.shape[1:]
    share = width // heads
    slice_rows = proj_ref.shape[2]
    head = lax.axis_index("head")

    @pl.when(row == 0)
    def _():
        grad_sum_ref[...] = jnp.zeros_like(grad_sum_ref)
        for index in range(link.batches):
            first = index * slice_rows
            count = min(slice_rows, share - first)
            if count > 0:
                place = link.place(index)
                for spot in range(heads):
                    piece = proj_ref[place, (spot - head + heads) % heads]
                    at = spot * share + first
                    proj_true_ref[at : at + count, :] = piece[:count]

    for at_row, mixed_ref in enumerate((split_ref, single_ref)):

        @pl.when(row == at_row)
        def _(mixed_ref=mixed_ref):
            for spot in range(heads):
                piece = mixed_ref[(spot - head + heads) % heads, 0]
                mixed_home_ref[0, :, spot * share : (spot + 1) * share] = piece

    spot = home_row(info_ref, row, home, quarter)

    def mod(group):
        return table_ref[pl.ds(spot, 1), group * width : (group + 1) * width]

    attn = nn(mixed_home_ref[0], proj_true_ref[...]) + bias_ref[...]
    attn_ref[0] = attn
    stream = tokens_ref[0].astype(jnp.float32) + mod(2) * attn
    stream_ref[0] = stream
    normed, _ = row_norm(stream.astype(jnp.bfloat16).astype(jnp.float32))
    mlp_in_ref[0] = (normed * (1.0 + mod(4)) + mod(3)).astype(jnp.bfloat16)
    grad_mlp = (grad_ref[0].astype(jnp.float32) * mod(5)).astype(jnp.bfloat16)
    grad_mlp_ref[0] = grad_mlp
    grad_sum_ref[...] += jnp.sum(grad_mlp.astype(jnp.float32), axis=0, keepdims=True)


def expand_kernel(steps, mlp_in_ref, bias_ref, *refs):
    pieces, (hidden_ref, slope_ref) = refs[:-2], refs[-2:]
    step = pl.program_id(0)
    for spot, piece_ref in enumerate(pieces):

        @pl.when(step // steps == spot)
        def _(piece_ref=piece_ref):
            pre = nt(mlp_in_ref[...], piece_ref[...]) + bias_ref[...]
            square = pre * pre
            bent = jnp.tanh(gelu_coeff * (pre + 0.044715 * square * pre))
            half = 0.5 * (1.0 + bent)
            hidden_ref[...] = (pre * half).astype(jnp.bfloat16)
            inner = gelu_coeff * (1.0 + (3.0 * 0.044715) * square)
            slope_ref[...] = (half + 0.5 * pre * (1.0 - bent * bent) * inner).astype(jnp.bfloat16)


def contract_kernel(link, quarter, steps, info_ref, table_ref, grad_mlp_ref, hidden_ref, slope_ref, out_bias_ref,
                    tokens_grad_ref, stream_ref, attn_ref, proj_ref, *refs):
    count = 4
    ins, outs = refs[:count], refs[count : 2 * count]
    (grad_pre_ref, pre_sum_ref, block_ref, stream_grad_ref, grad_attn_ref, split_ref, single_ref, sums_ref, attn_sum_ref,
     mlp_acc, grad_acc) = refs[2 * count :]
    grad_mixed_refs = (split_ref, single_ref)
    step = pl.program_id(0)
    heads = link.heads
    rows, home, width = stream_ref.shape
    share = width // heads

    @pl.when(step == 0)
    def _():
        mlp_acc[...] = jnp.zeros_like(mlp_acc)
        grad_acc[...] = jnp.zeros_like(grad_acc)

    for spot in range(count):

        @pl.when(step // steps == spot)
        def _(in_ref=ins[spot], out_ref=outs[spot]):
            grad_pre = (nt(grad_mlp_ref[...], out_ref[...]) * slope_ref[...].astype(jnp.float32)).astype(jnp.bfloat16)
            grad_pre_ref[...] = grad_pre
            pre_sum_ref[...] = jnp.sum(grad_pre.astype(jnp.float32), axis=0, keepdims=True)
            grad_acc[...] += nn(grad_pre, in_ref[...])
            mlp_acc[...] += nn(hidden_ref[...], out_ref[...])

    @pl.when(step == count * steps - 1)
    def _():
        head = lax.axis_index("head")
        attn_sum = jnp.zeros((1, width), jnp.float32)
        for row in range(rows):
            spot = home_row(info_ref, row, home, quarter)

            def mod(group):
                return table_ref[pl.ds(spot, 1), group * width : (group + 1) * width]

            here = slice(row * home, (row + 1) * home)
            grad_out = tokens_grad_ref[row_at(row, info_ref)].astype(jnp.float32)
            stream = stream_ref[row]
            mlp = mlp_acc[here, :] + out_bias_ref[...]
            block = (stream + mod(5) * mlp).astype(jnp.bfloat16)
            for other in range(heads):
                block_ref[(other - head + heads) % heads, row] = block[:, other * share : (other + 1) * share]
            normed, inverse = row_norm(stream.astype(jnp.bfloat16).astype(jnp.float32))
            grad_in = grad_acc[here, :]
            sums_ref[row, 1:2] = jnp.sum(grad_in, axis=0, keepdims=True)
            sums_ref[row, 2:3] = jnp.sum(grad_in * normed, axis=0, keepdims=True)
            sums_ref[row, 3:4] = jnp.sum(grad_out * mlp, axis=0, keepdims=True)
            stream_grad = grad_out + norm_back(normed, inverse, grad_in * (1.0 + mod(4)))
            stream_grad_ref[row] = stream_grad
            rounded = stream_grad.astype(jnp.bfloat16).astype(jnp.float32)
            sums_ref[row, 0:1] = jnp.sum(rounded * attn_ref[row], axis=0, keepdims=True)
            grad_attn = (rounded * mod(2)).astype(jnp.bfloat16)
            grad_attn_ref[row] = grad_attn
            attn_sum += jnp.sum(grad_attn.astype(jnp.float32), axis=0, keepdims=True)
            grad_mixed = nt(grad_attn, proj_ref[...]).astype(jnp.bfloat16)
            for other in range(heads):
                grad_mixed_refs[row][(other - head + heads) % heads, 0] = grad_mixed[:, other * share : (other + 1) * share]
        attn_sum_ref[...] = attn_sum


def row_at(spot, info_ref):
    return jnp.where(spot == 0, info_ref[0], 1 - info_ref[0])


def leave_kernel(link, quarter, at_row, info_ref, table_ref, grad_ref, weight_ref, tokens_ref, stream_grad_ref,
                 shares_ref, sums_ref, term_ref):
    block = pl.program_id(0)
    heads = link.heads
    width = tokens_ref.shape[1]
    share = width // heads
    home = stream_grad_ref.shape[1]
    spot = 1 + block if at_row == 0 else 0
    scale = table_ref[pl.ds(spot, 1), width : 2 * width]
    grad_in = nn(grad_ref[...], weight_ref[...])
    normed, inverse = row_norm(tokens_ref[...].astype(jnp.float32))
    sums_ref[0, 0:1] = jnp.sum(grad_in, axis=0, keepdims=True)
    sums_ref[0, 1:2] = jnp.sum(grad_in * normed, axis=0, keepdims=True)
    term_ref[...] = norm_back(normed, inverse, grad_in * (1.0 + scale))
    start = info_ref[1] * home

    @pl.when(start // quarter == block)
    def _():
        rows = pl.ds(pl.multiple_of(start % quarter, 8), home)
        term_ref[rows, :] += stream_grad_ref[0]

    low = term_ref[...].astype(jnp.bfloat16)
    for head in range(heads):
        shares_ref[head] = low[:, head * share : (head + 1) * share]


def unit_grads_kernel(steps, left_ref, right_ref, *refs):
    more, outs = refs[:2], refs[2:]
    for spot in range(2):

        @pl.when(pl.program_id(0) // steps == spot)
        def _(spot=spot):
            total = tn(left_ref[...], right_ref[...])
            total = total + more[spot][...].astype(jnp.float32)
            outs[spot][...] = total.astype(jnp.bfloat16)


def unit_grads(left, right, half, more=(), order=()):
    count, total = left.shape
    width = right.shape[1]
    piece = total // 4
    steps = piece // UNIT_TILE

    def spec(spot):
        return pl.BlockSpec((UNIT_TILE, width), lambda i: (jnp.clip(i - spot * steps, 0, steps - 1), 0))

    kernel = functools.partial(unit_grads_kernel, steps)
    if not more:
        kernel = lambda l, r, *outs: unit_grads_plain(steps, l, r, *outs)
    return call(
        kernel,
        [shape_of((piece, width), jnp.bfloat16)] * 2,
        [pl.BlockSpec((count, UNIT_TILE), lambda i: (0, i + half * 2 * steps)), whole((count, width))]
        + [spec(i) for i in range(len(more))],
        [spec(0), spec(1)],
        grid=(2 * steps,),
        name="unit_grads", micros=6,
        order=order,
    )(left, right, *more)


def unit_grads_plain(steps, left_ref, right_ref, *outs):
    for spot in range(2):

        @pl.when(pl.program_id(0) // steps == spot)
        def _(spot=spot):
            outs[spot][...] = tn(left_ref[...], right_ref[...]).astype(jnp.bfloat16)


def place_rows_kernel(link, slices_ref, out_ref):
    rows = slices_ref.shape[1]
    for index in range(link.batches):
        count = min(rows, out_ref.shape[0] - index * rows)
        if count > 0:
            piece = slices_ref[link.place(index)].astype(jnp.float32)
            out_ref[index * rows : index * rows + count, :] = piece[:count]


def place_rows(link, slices, rows):
    width = slices.shape[2]
    tile = 384
    return call(
        functools.partial(place_rows_kernel, link),
        shape_of((rows, width), jnp.float32),
        [pl.BlockSpec(slices.shape[:2] + (tile,), lambda i: (0, 0, i))],
        pl.BlockSpec((rows, tile), lambda i: (0, i)),
        grid=(width // tile,),
        name="place_rows", micros=4,
    )(slices)


def place_columns_kernel(link, slices_ref, out_ref, rows_ref):
    rows = slices_ref.shape[1]
    for index in range(link.batches):
        rows_ref[index * rows : (index + 1) * rows, :] = slices_ref[link.place(index)].astype(jnp.float32)
    out_ref[...] = rows_ref[...].T


def place_columns(link, slices):
    batches, rows, width = slices.shape
    tile = 128
    return call(
        functools.partial(place_columns_kernel, link),
        shape_of((width, batches * rows), jnp.float32),
        [pl.BlockSpec((batches, rows, tile), lambda i: (0, 0, i))],
        pl.BlockSpec((tile, batches * rows), lambda i: (i, 0)),
        grid=(width // tile,),
        scratch=[pltpu.VMEM((batches * rows, tile), jnp.float32)],
        name="place_columns", micros=8,
    )(slices)


def lay_home_kernel(heads, info_ref, blocks_ref, out_ref):
    home = blocks_ref.shape[2]
    head = lax.axis_index("head")
    for spot in range(heads):
        for row in range(2):
            out_ref[row_at(row, info_ref), spot * home : (spot + 1) * home, :] = blocks_ref[(head - spot + heads) % heads, row]


def shards(
    tokens,
    segments,
    item_cond,
    condition,
    ada_weight,
    ada_bias,
    qkv_weight,
    qv_bias,
    proj_weight,
    proj_bias,
    in_weight,
    in_bias,
    out_weight,
    out_bias,
    cotangent,
):
    low = jnp.bfloat16
    full = jnp.float32
    heads, batches = lax.axis_size("head"), lax.axis_size("batch")
    link = Links(heads, batches)
    batch = lax.axis_index("batch")
    token_count, width = tokens.shape
    rows = token_count // SEQ
    quarter = SEQ // 4
    home = SEQ // heads
    home_count = rows * home
    share = width // heads
    heads_here = qv_bias.shape[0] // (2 * HEAD_DIM)
    qkv_here = 3 * heads_here * HEAD_DIM
    units_here = in_weight.shape[1]
    units = units_here // batches
    ada_here = ada_weight.shape[1]
    cond_count = condition.shape[0]

    ada_t = ada_weight.T
    qkv_t = qkv_weight.T
    table_part, info = call(
        functools.partial(mod_kernel, quarter, units_here),
        [shape_of((8, ada_here), full), shape_of((8,), jnp.int32)],
        [SCALARS, SCALARS] + [whole(s) for s in ((cond_count, width), (ada_here, width), (1, ada_here), (1, units_here))],
        [whole((8, ada_here)), SCALARS],
        name="modulation", micros=5,
    )(segments, item_cond, condition, ada_t, ada_bias.astype(full)[None], in_bias.astype(full)[None])
    table_rel = jnp.stack([table_part] + [link.fetch(table_part, j) for j in range(1, heads)])

    slice_rows = -(-share // (8 * batches)) * 8
    proj_pad = jnp.pad(proj_weight, ((0, slice_rows * batches - share), (0, 0)))
    proj_slice = lax.dynamic_slice_in_dim(proj_pad, batch * slice_rows, slice_rows, 0)
    in_slice = lax.dynamic_slice_in_dim(in_weight, batch * units, units, 1).T
    out_slice = lax.dynamic_slice_in_dim(out_weight, batch * units, units, 0)
    proj_rel = jnp.stack([proj_slice] + [link.fetch(proj_slice, j) for j in range(1, heads)])
    in_gathered = lax.all_gather(in_slice, "head", axis=0, tiled=True)
    out_gathered = lax.all_gather(out_slice, "head", axis=0, tiled=True)
    def tokens_block(i, info_ref):
        return (4 * row_at(i // 4, info_ref) + i % 4, 0)

    bias_pairs = qv_bias.astype(full).reshape(heads_here, 2, HEAD_DIM)
    full_bias = jnp.concatenate(
        [bias_pairs[:, :1], jnp.zeros((heads_here, 1, HEAD_DIM), full), bias_pairs[:, 1:]], axis=1
    ).reshape(1, -1)
    attn_in, projected, table = call(
        functools.partial(project_kernel, heads, quarter),
        [
            shape_of((token_count, width), low),
            shape_of((token_count, qkv_here), low),
            shape_of((8, 6 * width), full),
        ],
        [
            whole((heads, 8, ada_here)),
            pl.BlockSpec((quarter, width), tokens_block),
            whole((qkv_here, width)),
            whole((1, qkv_here)),
        ],
        [
            pl.BlockSpec((quarter, width), lambda i, _: (i, 0)),
            pl.BlockSpec((quarter, qkv_here), lambda i, _: (i, 0)),
            whole((8, 6 * width)),
        ],
        grid=(4 * rows,),
        prefetch=1,
        name="project", micros=13,
        order=[proj_rel],
    )(info, table_rel, tokens, qkv_t, full_bias)
    projected = projected.reshape(rows, SEQ, qkv_here)
    mixed_rows = []
    mixed_here_rows = []
    log_totals = []
    proj_own = jnp.concatenate(link.gather_levels(proj_rel[None]), axis=0)
    orders = [[proj_own]]
    for row in range(rows):
        mixed, log_total = attend(projected, row, heads_here, quarter, heads, orders[row])
        mixed_rows.append(jnp.stack([mixed[0]] + [link.fetch(mixed[j], j) for j in range(1, heads)]))
        mixed_here_rows.append(mixed)
        if row == 0:
            in_gathered = hold(in_gathered, mixed)
            orders.append([in_gathered])
        log_totals.append(log_total)

    proj_all = jnp.concatenate([proj_own, link.core_swap(proj_own)], axis=0)
    in_held = link.gather_levels(in_gathered, [mixed_here_rows[1]])
    out_held = link.gather_levels(out_gathered)
    out_pieces = out_held + [link.core_swap(piece) for piece in out_held]
    tokens_rows = tokens.reshape(rows, SEQ, width)
    grad_rows = cotangent.reshape(rows, SEQ, width)
    home_spec = pl.BlockSpec((1, home, width), lambda i, info_ref: (row_at(i, info_ref), info_ref[1], 0))
    row_spec = pl.BlockSpec((1, home, width), lambda i, _: (i, 0, 0))
    attn, stream, mlp_in, grad_mlp, mixed_home, proj_true, grad_sum = call(
        functools.partial(enter_kernel, link, quarter),
        [
            shape_of((rows, home, width), full),
            shape_of((rows, home, width), full),
            shape_of((rows, home, width), low),
            shape_of((rows, home, width), low),
            shape_of((rows, home, width), low),
            shape_of((width, width), low),
            shape_of((1, width), full),
        ],
        [
            whole((8, 6 * width)),
            whole((heads, 1, home, share)),
            whole((heads, 1, home, share)),
            whole(proj_all.shape),
            home_spec,
            home_spec,
            whole((1, width)),
        ],
        [row_spec] * 5 + [whole((width, width)), whole((1, width))],
        grid=(rows,),
        prefetch=1,
        name="enter", micros=9,
        order=[in_held[0], out_gathered],
    )(info, table, *mixed_rows, proj_all, tokens_rows, grad_rows, proj_bias.astype(full)[None])

    in_held[1] = hold(in_held[1], mlp_in)
    in_pieces = in_held + [link.core_swap(piece) for piece in in_held]
    mlp_in = mlp_in.reshape(home_count, width)
    grad_mlp = grad_mlp.reshape(home_count, width)
    in_bias_all = table[5].reshape(heads, -1)[:, :units_here]
    in_bias_all = in_bias_all.reshape(heads, batches, units)
    in_bias_all = link.by_owner(in_bias_all.transpose(1, 0, 2)).reshape(1, -1)
    piece_rows = in_pieces[0].shape[0]
    unit_count = 4 * piece_rows
    steps = piece_rows // UNIT_TILE

    def piece_spec(spot):
        return pl.BlockSpec((UNIT_TILE, width), lambda i, *_: (jnp.clip(i - spot * steps, 0, steps - 1), 0))

    tile_spec = pl.BlockSpec((home_count, UNIT_TILE), lambda i, *_: (0, i))
    bias_spec = pl.BlockSpec((1, UNIT_TILE), lambda i, *_: (0, i))
    hidden, slope = call(
        functools.partial(expand_kernel, steps),
        [shape_of((home_count, unit_count), low)] * 2,
        [whole((home_count, width)), bias_spec] + [piece_spec(spot) for spot in range(4)],
        [tile_spec, tile_spec],
        grid=(4 * steps,),
        name="expand", micros=20,
        order=[out_held[0]],
    )(mlp_in, in_bias_all, *in_pieces)

    out_far = unit_grads(hidden, grad_mlp, 1)
    out_near = unit_grads(hidden, grad_mlp, 0, [link.core_swap(piece) for piece in out_far])

    stay = pl.BlockSpec((rows, home, width), lambda *_: (0, 0, 0))
    by_head = whole((heads, rows, home, share))
    one_row = whole((heads, 1, home, share))
    grad_pre, pre_sum, block_home, stream_grad, grad_attn, mixed_split, mixed_single, home_sums, attn_sum = call(
        functools.partial(contract_kernel, link, quarter, steps),
        [
            shape_of((home_count, unit_count), low),
            shape_of((1, unit_count), full),
            shape_of((heads, rows, home, share), low),
            shape_of((rows, home, width), full),
            shape_of((rows, home, width), low),
            shape_of((heads, 1, home, share), low),
            shape_of((heads, 1, home, share), low),
            shape_of((rows, 4, width), full),
            shape_of((1, width), full),
        ],
        [
            whole((8, 6 * width)),
            whole((home_count, width)),
            tile_spec,
            tile_spec,
            whole((1, width)),
            pl.BlockSpec((rows, home, width), lambda i, info_ref: (0, info_ref[1], 0)),
            stay,
            stay,
            whole((width, width)),
        ]
        + [piece_spec(spot) for spot in range(4)] * 2,
        [tile_spec, bias_spec, by_head, stay, stay, one_row, one_row, whole((rows, 4, width)), whole((1, width))],
        grid=(4 * steps,),
        prefetch=1,
        scratch=[pltpu.VMEM((home_count, width), full)] * 2,
        name="contract", micros=44,
        order=list(out_near),
    )(info, table, grad_mlp, hidden, slope, out_bias.astype(full)[None], grad_rows, stream, attn, proj_true,
      *in_pieces, *out_pieces)
    grad_mixed_rows = [
        jnp.stack([piece[0]] + [link.send(piece[j], j) for j in range(1, heads)])
        for piece in (mixed_split, mixed_single)
    ]
    out_sums = link.reduce_levels(list(out_near))
    in_far = unit_grads(grad_pre, mlp_in, 1, order=[out_sums[0]])
    in_near = unit_grads(
        grad_pre, mlp_in, 0, [link.core_swap(piece) for piece in in_far], order=[grad_mixed_rows[0]]
    )
    proj_grad = tn(mixed_home.reshape(home_count, width), grad_attn.reshape(home_count, width)).astype(low)

    grad_rows_low = []
    block_sums = []
    shares = []
    for row in range(rows):
        grad_row = attend_back(
            projected, row, log_totals[row], grad_mixed_rows[row], heads_here, quarter, heads,
            [in_near[0], out_sums[-1]] if row == 0 else [sums_row],
        )[0]
        share_row, sums_row = call(
            functools.partial(leave_kernel, link, quarter, row),
            [shape_of((heads, SEQ, share), low), shape_of((4, 2, width), full)],
            [
                whole((8, 6 * width)),
                pl.BlockSpec((quarter, qkv_here), lambda i, _: (i, 0)),
                whole((qkv_here, width)),
                pl.BlockSpec((quarter, width), lambda i, info_ref, row=row: tokens_block(i + 4 * row, info_ref)),
                pl.BlockSpec((1, home, width), lambda i, _, row=row: (row, 0, 0)),
            ],
            [
                pl.BlockSpec((heads, quarter, share), lambda i, _: (0, i, 0)),
                pl.BlockSpec((1, 2, width), lambda i, _: (i, 0, 0)),
            ],
            grid=(4,),
            prefetch=1,
            scratch=[pltpu.VMEM((quarter, width), full)],
            name="leave", micros=9,
            order=shares,
        )(info, table, grad_row, qkv_t, tokens, stream_grad)
        grad_rows_low.append(grad_row)
        block_sums.append(sums_row)
        shares.append(lax.psum_scatter(share_row, "head", scatter_dimension=0, tiled=True)[0] if row == 0 else share_row)
    grad_projected = jnp.concatenate(grad_rows_low, axis=0)
    in_sums = link.reduce_levels(list(in_near), [grad_rows_low[1], shares[1]])

    def head_sum(values):
        return lax.psum_scatter(values, "head", scatter_dimension=0, tiled=True)

    out_slice_sum = head_sum(out_sums[-1])
    in_slice_sum = head_sum(hold(in_sums[-1], shares[0]))
    shares[1] = head_sum(hold(shares[1], in_slice_sum))[0]
    tokens_grad = jnp.where(
        info[0] == 0, jnp.concatenate(shares, axis=0), jnp.concatenate(shares[::-1], axis=0)
    )

    block_home = jnp.stack([block_home[0]] + [link.send(block_home[j], j) for j in range(1, heads)])
    block_out = call(
        functools.partial(lay_home_kernel, heads),
        shape_of((rows, SEQ, share), low),
        [whole((heads, rows, home, share))],
        whole((rows, SEQ, share)),
        prefetch=1,
        name="lay_home", micros=3,
        order=[grad_rows_low[1]],
    )(info, block_home).reshape(token_count, share)

    home_quarter = lax.axis_index("head") * home // quarter
    seg_spots = lax.broadcasted_iota(jnp.int32, (5, 1), 0)

    def seg_home(sums):
        placed = jnp.where(seg_spots == 1 + home_quarter, sums[0][None, :], 0.0)
        return jnp.where(seg_spots == 0, sums[1][None, :], placed)

    seg_blocks = jnp.concatenate([jnp.sum(block_sums[1], axis=0, keepdims=True), block_sums[0]], axis=0)
    seg_grads = jnp.concatenate(
        [seg_blocks[:, 0], seg_blocks[:, 1]] + [seg_home(home_sums[:, i]) for i in range(4)], axis=1
    )
    in_bias_part = link.by_index(pre_sum.reshape(batches, heads, units)).transpose(1, 0, 2)
    bias_grads = jnp.concatenate(
        [
            in_bias_part.reshape(heads, -1),
            grad_sum.reshape(heads, -1),
            attn_sum.reshape(heads, -1),
        ],
        axis=1,
    ).reshape(1, -1)
    sent = jnp.concatenate([seg_grads, bias_grads, jnp.zeros((2, 6 * width), full)], axis=0)
    sent = sent.reshape(8, heads, ada_here)

    def sent_block(distance):
        return lax.dynamic_index_in_dim(sent, link.at_head(distance), 1, keepdims=False)

    held = sent_block(0)
    for j in range(1, heads):
        held = held + link.send(sent_block(j), j)
    column_sums = jnp.sum(grad_projected.astype(full), axis=0).reshape(heads_here, 3, HEAD_DIM)
    qv_bias_part = jnp.concatenate([column_sums[:, :1], column_sums[:, 2:]], axis=1).reshape(-1)
    held = jnp.concatenate(
        [
            held[:6],
            jnp.pad(qv_bias_part, (0, ada_here - qv_bias_part.shape[0]))[None],
            jnp.pad(info[3:].astype(full), (0, ada_here - 5))[None],
        ],
        axis=0,
    )
    all_held = link.gather_batch(held[None])
    all_classes = (all_held[:, 7, :5] + 0.5).astype(jnp.int32).reshape(-1)
    class_hits = (
        lax.broadcasted_iota(jnp.int32, (cond_count, 1), 0) == all_classes[None, :]
    ).astype(full)
    mod_low = jnp.dot(
        class_hits,
        all_held[:, :5].reshape(-1, ada_here),
        precision=lax.Precision.HIGHEST,
        preferred_element_type=full,
    ).astype(low)
    bias_total = jnp.sum(all_held[:, 5], axis=0)
    qv_bias_grad = jnp.sum(all_held[:, 6, : qv_bias.shape[0]], axis=0)
    in_bias_grad = bias_total[:units_here]
    cond_f = condition.astype(full)
    ada_weight_grad = tn(mod_low, silu_act(cond_f).astype(low)).T
    ada_bias_grad = jnp.sum(mod_low.astype(full), axis=0)
    cond_part = nn(mod_low, ada_t)
    shared = jnp.pad(bias_total[units_here:], (0, width - 2 * share))
    last = jnp.concatenate([cond_part, shared[None], jnp.zeros((7, width), full)]).astype(low)
    last = jnp.stack([last] + [link.fetch(last, j) for j in range(1, heads)]).astype(full)
    cond_total = jnp.sum(last[:, :cond_count], axis=0)
    condition_grad = jax.vjp(silu_act, cond_f)[1](cond_total)[0]
    shared = last[:, cond_count]
    head = lax.axis_index("head")
    shared = jnp.concatenate(
        [lax.dynamic_index_in_dim(shared, (j - head + heads) % heads, 0) for j in range(heads)]
    )
    out_bias_grad = shared[:, :share].reshape(-1)
    proj_bias_grad = shared[:, share : 2 * share].reshape(-1)

    out_weight_grad = place_rows(link, link.gather_batch(out_slice_sum[None]), units_here)
    in_weight_grad = place_columns(link, link.gather_batch(in_slice_sum[None]))

    qkv_rows = -(-qkv_here // (16 * batches)) * 16
    qkv_grad = tn(grad_projected, attn_in.reshape(token_count, width)).astype(low)
    qkv_grad = jnp.pad(qkv_grad, ((0, qkv_rows * batches - qkv_here), (0, 0))).reshape(batches, qkv_rows, width)
    proj_grad = jnp.pad(
        proj_grad.reshape(heads, share, width), ((0, 0), (0, slice_rows * batches - share), (0, 0))
    ).reshape(heads, batches, slice_rows, width)
    proj_grad = proj_grad.transpose(1, 0, 2, 3).reshape(batches, heads * slice_rows, width)
    both = link.by_owner(jnp.concatenate([qkv_grad, proj_grad], axis=1))
    both = both.reshape(2, 2, -1, width)
    got = [link.core_swap(piece) for piece in both[1]]
    both = [(mine.astype(full) + more.astype(full)).astype(low) for mine, more in zip(both[0], got)]
    both = link.reduce_levels(both)[-1]
    proj_blocks = both[qkv_rows:].reshape(heads, slice_rows, width)

    def proj_block(distance):
        return lax.dynamic_index_in_dim(proj_blocks, link.at_head(distance), 0, keepdims=False)

    proj_sum = proj_block(0).astype(full)
    for j in range(1, heads):
        proj_sum = proj_sum + link.send(proj_block(j), j).astype(full)
    both = jnp.concatenate([both[:qkv_rows], proj_sum.astype(low)], axis=0)
    both = link.gather_batch(both[None])
    qkv_weight_grad = place_rows(link, both[:, :qkv_rows], qkv_here).T
    proj_weight_grad = place_rows(link, both[:, qkv_rows:], share)

    return (
        block_out,
        tokens_grad,
        condition_grad,
        ada_weight_grad,
        ada_bias_grad,
        qkv_weight_grad,
        qv_bias_grad,
        proj_weight_grad,
        proj_bias_grad,
        in_weight_grad,
        in_bias_grad,
        out_weight_grad,
        out_bias_grad,
    )


def solution(mesh):
    in_specs = (
        P("batch", None),
        P("batch"),
        P(),
        P(),
        P(None, "head"),
        P("head"),
        P(None, "head"),
        P("head"),
        P("head", None),
        P(),
        P(None, "head"),
        P("head"),
        P("head", None),
        P(),
        P("batch", None),
    )
    out_specs = (
        P("batch", "head"),
        P("batch", "head"),
        P(),
        P(None, "head"),
        P("head"),
        P(None, "head"),
        P("head"),
        P("head", None),
        P(),
        P(None, "head"),
        P("head"),
        P("head", None),
        P(),
    )
    return jax.shard_map(shards, mesh=mesh, in_specs=in_specs, out_specs=out_specs, check_vma=False)
```

time: 1220 us -> 636 us (0.52)
  matrix products: 298 us -> 18.8 us
  waiting for transfers between devices: 448 us -> 181 us
  Pallas kernels: 0 us -> 225 us
  local copies, waits for them, and re-layouts: 201 us -> 51.3 us
  other arithmetic: 163 us -> 57.9 us
  blocking collectives: 79.3 us -> 0 us
  starting transfers between devices: 0.59 us -> 77.1 us
    reduce_scatter x4, waiting for transfers between devices: 316 us -> 10.6 us  [the longest x3 10.5 us: head_sum(): return lax.psum_scatter(values, 'head', scatter_dimension=0, tiled=True)]
    dot_general x36 -> x5, matrix products: 298 us -> 18.8 us  [the longest x3 13.9 us: tn(): lax.dot_general(left_side, right_side, (((0,), (0,)), ((), ())), preferre...]
    pallas_call x0 -> x27, Pallas kernels: none -> 225 us  [the longest x20 225 us: call(): return lambda *arrays: run(*arrays, *order)]
    ppermute x0 -> x65, waiting for transfers between devices: none -> 170 us  [the longest x15 89.3 us: fetch(): lax.ppermute(values, 'head', [((i + distance) % count, i) for i in range(...]
    all_gather x3 -> x2, waiting for transfers between devices: 103 us -> 0.01 us  [the longest x1 0.01 us: shards(): in_gathered = lax.all_gather(in_slice, 'head', axis=0, tiled=True)]
    unnamed x134 -> x162, local copies, waits for them, and re-layouts: 115 us -> 22.2 us
    reduce_sum x16 -> x5, other arithmetic: 85.5 us -> 2.9 us  [the longest x1 2.12 us: shards(): jnp.sum(grad_projected.astype(full), axis=0)]
    psum x2 -> x0, blocking collectives: 79.3 us -> none  [the longest x1 56.6 us: shards(): mod_grad = lax.psum(mod_total, ('batch', 'head')).astype(jnp.bfloat16)]
  transfers between devices with their start and end apart: 9 -> 71, of which waited for: 8 -> 32; matrix products, arithmetic and copies ran while one was open for 21% -> 16% of each run, Pallas kernels for 0% -> 35%
where the time goes in v1:
time: 636 us; the launch traced here: 627 us
  Pallas kernels  225 us (35%)
  waiting for transfers between devices  181 us (28%)
  starting transfers between devices  77.1 us (12%)
  other arithmetic  57.9 us (9%)
  local copies, waits for them, and re-layouts  51.3 us (8%)
  matrix products  18.8 us (3%)
  between operations  15.7 us (2%)
    pallas_call x20, Pallas kernels, call(): return lambda *arrays: run(*arrays, *order)  225 us
    ppermute x15, waiting for transfers between devices, fetch(): lax.ppermute(values, 'head', [((i + distance) % count, i) for i in range(...  89.3 us
    ppermute x20, waiting for transfers between devices, link_swap(): return lax.ppermute(values, 'batch', pairs)  55.1 us
    ppermute x15, starting transfers between devices, send(): lax.ppermute(values, 'head', [(i, (i + distance) % count) for i in range(...  25.1 us
    ppermute x20, starting transfers between devices, link_swap(): return lax.ppermute(values, 'batch', pairs)  23.3 us
    unnamed x162, local copies, waits for them, and re-layouts  22.2 us
    ppermute x15, waiting for transfers between devices, send(): lax.ppermute(values, 'head', [(i, (i + distance) % count) for i in range(...  16.1 us
    ppermute x15, starting transfers between devices, core_swap(): lax.ppermute(values, 'batch', [(i, i ^ 1) for i in range(self.batches)])  14.4 us
  transfers between devices with their start and end apart: 71, of which 32 were waited for; matrix products, arithmetic and copies ran while one was open for 16% of the time, Pallas kernels for 35%

profile of v1, /device:TPU:9, one launch (start us, length us, event | category | flops | bytes accessed | tf_op | source)
XLA Modules:
  0.0 627.0 jit_solution(16834479883678318176)
XLA Ops:
  51.1 12.8 %project.1 = (bf16[2048,1152]{1,0:T(8,128)(2,1)}, bf16[2048,864]{1,0:T(8,128)(2,1)}, f32[8,6912]{1,0:T(8,128)}) custom-call(s32[8]{0:T(128)} %get-tuple-element.52.refs_0_.info_ref, f32[4,8,1728]{2,1,0:T(8,128)} %pad_maximum_fusion.27.refs_1_, bf16[2048,1152]{1,0:T(8,128)(2,1)} %refs_4_.1, bf16[864,1152]{1,0:T(8,128)(2,1)} %bitcast.200, ...), custom_call_target="tpu_custom_call" | custom-call | bytes 42900000 | tf_op jit(solution)/shard_map/project/pallas_call | solution.py:211
  65.3 8.4 %attend_split.1 = (bf16[4,1,256,288]{3,2,1,0:T(8,128)(2,1)}, f32[1,4,1024]{2,1,0:T(4,128)}) custom-call(bf16[2,1024,864]{2,1,0:T(8,128)(2,1)} %bitcast.182, bf16[4,4,40,1152]{3,2,1,0:T(8,128)(2,1)} %pad_maximum_fusion.8.refs_1_), custom_call_target="tpu_custom_call" | custom-call | bytes 19800000 | tf_op jit(solution)/shard_map/attend_split/pallas_call | solution.py:211
  74.0 14.9 %attend_whole.1 = (bf16[4,1,256,288]{3,2,1,0:T(8,128)(2,1)}, f32[1,4,1024]{2,1,0:T(4,128)}) custom-call(bf16[2,1024,864]{2,1,0:T(8,128)(2,1)} %bitcast.183, bf16[576,1152]{1,0:T(8,128)(2,1)} %hold.7.refs_1_), custom_call_target="tpu_custom_call" | custom-call | bytes 52800000 | tf_op jit(solution)/shard_map/attend_whole/pallas_call | solution.py:211
  107.1 18.3 %collective-permute-done.9 = bf16[1,256,288]{2,1,0:T(8,128)(2,1)S(1)} collective-permute-done((bf16[1,256,288]{2,1,0:T(8,128)(2,1)S(1)}, bf16[1,256,288]{2,1,0:T(8,128)(2,1)S(1)}, u32[]{:S(2)}, u32[]{:S(2)}) %collective-permute-start.9) | collective-permute-done | bytes 147488 | tf_op jit(solution)/shard_map/ppermute | solution.py:245
  129.1 17.1 %collective-permute-done.8 = bf16[1,256,288]{2,1,0:T(8,128)(2,1)S(1)} collective-permute-done((bf16[1,256,288]{2,1,0:T(8,128)(2,1)S(1)}, bf16[1,256,288]{2,1,0:T(8,128)(2,1)S(1)}, u32[]{:S(2)}, u32[]{:S(2)}) %collective-permute-start.8) | collective-permute-done | bytes 147488 | tf_op jit(solution)/shard_map/ppermute | solution.py:245
  148.0 7.5 %collective-permute-done.12 = bf16[1,256,288]{2,1,0:T(8,128)(2,1)S(1)} collective-permute-done((bf16[1,256,288]{2,1,0:T(8,128)(2,1)S(1)}, bf16[1,256,288]{2,1,0:T(8,128)(2,1)S(1)}, u32[]{:S(2)}, u32[]{:S(2)}) %collective-permute-start.12) | collective-permute-done | bytes 147488 | tf_op jit(solution)/shard_map/ppermute | solution.py:245
  160.4 9.7 %enter.1 = (f32[2,256,1152]{2,1,0:T(8,128)}, f32[2,256,1152]{2,1,0:T(8,128)}, bf16[2,256,1152]{2,1,0:T(8,128)(2,1)}, bf16[2,256,1152]{2,1,0:T(8,128)(2,1)}, bf16...) custom-call(s32[8]{0:T(128)} %get-tuple-element.52.refs_0_.info_ref, ...), custom_call_target="tpu_custom_call" | custom-call | bytes 29700000 | tf_op jit(solution)/shard_map/enter/pallas_call | solution.py:211
  174.9 13.9 %collective-permute-done.19 = bf16[576,1152]{1,0:T(8,128)(2,1)} collective-permute-done((bf16[576,1152]{1,0:T(8,128)(2,1)}, bf16[576,1152]{1,0:T(8,128)(2,1)}, u32[]{:S(2)}, u32[]{:S(2)}) %collective-permute-start.19) | collective-permute-done | bytes 1327136 | tf_op jit(solution)/shard_map/ppermute | solution.py:256
  191.9 19.6 %expand.1 = (bf16[512,4608]{1,0:T(8,128)(2,1)}, bf16[512,4608]{1,0:T(8,128)(2,1)}) custom-call(bf16[512,1152]{1,0:T(8,128)(2,1)} %bitcast.195, f32[1,4608]{1,0:T(1,128)} %reshape.225.refs_1_, bf16[1152,1152]{1,0:T(8,128)(2,1)} %copy-done.3, bf16[1152,1152]{1,0:T(8,128)(2,1)} %hold.9.refs_3_.refs_11_, ...), custom_call_target="tpu_custom_call" | custom-call | bytes 66000000 | tf_op jit(solution)/shard_map/expand/pallas_call | solution.py:211
  211.5 8.4 %unit_grads.4 = (bf16[1152,1152]{1,0:T(8,128)(2,1)}, bf16[1152,1152]{1,0:T(8,128)(2,1)}) custom-call(bf16[512,4608]{1,0:T(8,128)(2,1)} %get-tuple-element.60.l.left_ref.refs_3_, bf16[512,1152]{1,0:T(8,128)(2,1)} %bitcast.208), custom_call_target="tpu_custom_call" | custom-call | bytes 19800000 | tf_op jit(solution)/shard_map/unit_grads/pallas_call | solution.py:211
  226.2 7.6 %collective-permute-done.24.refs_1_ = bf16[1152,1152]{1,0:T(8,128)(2,1)} collective-permute-done((bf16[1152,1152]{1,0:T(8,128)(2,1)}, bf16[1152,1152]{1,0:T(8,128)(2,1)}, u32[]{:S(2)}, u32[]{:S(2)}) %collective-permute-start.24) | collective-permute-done | bytes 2654240 | tf_op jit(solution)/shard_map/ppermute | solution.py:252
  233.8 9.7 %unit_grads.5 = (bf16[1152,1152]{1,0:T(8,128)(2,1)}, bf16[1152,1152]{1,0:T(8,128)(2,1)}) custom-call(bf16[512,4608]{1,0:T(8,128)(2,1)} %get-tuple-element.60.l.left_ref.refs_3_, bf16[512,1152]{1,0:T(8,128)(2,1)} %bitcast.209, bf16[1152,1152]{1,0:T(8,128)(2,1)} %collective-permute-done.23.refs_0_, bf16[1152,1152]{1,0:T(8,128)(2,1)} %collective-permute-done.24.refs_1_), custom_call_target="tpu_custom_call" | custom-call | bytes 19800000 | tf_op jit(solution)/shard_map/unit_grads/pallas_call | solution.py:211
  245.2 44.1 %contract.1 = (bf16[512,4608]{1,0:T(8,128)(2,1)}, f32[1,4608]{1,0:T(1,128)}, bf16[4,2,256,288]{3,2,1,0:T(8,128)(2,1)}, f32[2,256,1152]{2,1,0:T(8,128)}, bf16[2,2...) custom-call(s32[8]{0:T(128)} %get-tuple-element.52.refs_0_.info_ref,, ...), custom_call_target="tpu_custom_call" | custom-call | bytes 145200000 | tf_op jit(solution)/shard_map/contract/pallas_call | solution.py:211
  293.3 8.4 %unit_grads.6 = (bf16[1152,1152]{1,0:T(8,128)(2,1)}, bf16[1152,1152]{1,0:T(8,128)(2,1)}) custom-call(bf16[512,4608]{1,0:T(8,128)(2,1)} %get-tuple-element.74.refs_0_, bf16[512,1152]{1,0:T(8,128)(2,1)} %bitcast.196, bf16[1152,1152]{1,0:T(8,128)(2,1)} %add_convert_fusion.1.refs_2_), custom_call_target="tpu_custom_call" | custom-call | bytes 19800000 | tf_op jit(solution)/shard_map/unit_grads/pallas_call | solution.py:211
  349.1 9.9 %unit_grads.7 = (bf16[1152,1152]{1,0:T(8,128)(2,1)}, bf16[1152,1152]{1,0:T(8,128)(2,1)}) custom-call(bf16[512,4608]{1,0:T(8,128)(2,1)} %get-tuple-element.74.refs_0_, bf16[512,1152]{1,0:T(8,128)(2,1)} %bitcast.197, bf16[1152,1152]{1,0:T(8,128)(2,1)} %collective-permute-done.35.refs_2_, bf16[1152,1152]{1,0:T(8,128)(2,1)} %collective-permute-done.36.refs_3_, ...), custom_call_target="tpu_custom_call" | custom-call | bytes 19800000 | tf_op jit(solution)/shard_map/unit_grads/pallas_call | solution.py:211
  359.0 9.4 %attend_back_split.1 = bf16[1,1024,864]{2,1,0:T(8,128)(2,1)} custom-call(bf16[2,1024,864]{2,1,0:T(8,128)(2,1)} %bitcast.184, f32[1,4,1024]{2,1,0:T(4,128)} %get-tuple-element.72.refs_1_, bf16[4,1,256,288]{3,2,1,0:T(8,128)(2,1)} %pad_maximum_fusion.19.refs_4_.refs_2_, bf16[1152,1152]{1,0:T(8,128)(2,1)} %get-tuple-element.77.refs_3_, ...), custom_call_target="tpu_custom_call" | custom-call | bytes 26400000 | tf_op jit(solution)/shard_map/attend_back_split/pallas_call | solution.py:211
  368.4 9.9 %leave.2 = (bf16[4,1024,288]{2,1,0:T(8,128)(2,1)}, f32[4,2,1152]{2,1,0:T(2,128)}) custom-call(s32[8]{0:T(128)} %get-tuple-element.52.refs_0_.info_ref, f32[8,6912]{1,0:T(8,128)} %get-tuple-element.54.refs_1_.table_ref, bf16[1024,864]{1,0:T(8,128)(2,1)} %bitcast.203, bf16[864,1152]{1,0:T(8,128)(2,1)} %bitcast.201, bf16[2048,1152]{1,0:T(8,128)(2,1)} %refs_4_.1, ...), custom_call_target="tpu_custom_call" | custom-call | bytes 29700000 | tf_op jit(solution)/shard_map/leave/pallas_call | solution.py:211
  378.3 23.0 %attend_back_whole.1 = bf16[1,1024,864]{2,1,0:T(8,128)(2,1)} custom-call(bf16[2,1024,864]{2,1,0:T(8,128)(2,1)} %bitcast.185, f32[1,4,1024]{2,1,0:T(4,128)} %get-tuple-element.70.refs_1_, bf16[4,1,256,288]{3,2,1,0:T(8,128)(2,1)} %pad_maximum_fusion.18.refs_2_, f32[4,2,1152]{2,1,0:T(2,128)} %get-tuple-element.79.refs_3_), custom_call_target="tpu_custom_call" | custom-call | bytes 79200000 | tf_op jit(solution)/shard_map/attend_back_whole/pallas_call | solution.py:211
  401.3 7.7 %convolution_convert_fusion = bf16[864,1152]{1,0:T(8,128)(2,1)S(1)} fusion(bf16[2048,1152]{1,0:T(8,128)(2,1)} %get-tuple-element.88, bf16[1024,864]{1,0:T(8,128)(2,1)} %bitcast.186, bf16[1024,864]{1,0:T(8,128)(2,1)S(1)} %bitcast.205), kind=kOutput, calls=%fused_computation.22 | convolution fusion | flops 4084936704 | bytes 10248192 | tf_op jit(solution)/shard_map/dot_general | solution.py:164
  438.1 23.1 %collective-permute-done.51 = bf16[544,1152]{1,0:T(8,128)(2,1)} collective-permute-done((bf16[544,1152]{1,0:T(8,128)(2,1)}, bf16[544,1152]{1,0:T(8,128)(2,1)}, u32[]{:S(2)}, u32[]{:S(2)}) %collective-permute-start.51) | collective-permute-done | bytes 1253408 | tf_op jit(solution)/shard_map/ppermute | solution.py:256
  488.2 10.2 %leave.3 = (bf16[4,1024,288]{2,1,0:T(8,128)(2,1)}, f32[4,2,1152]{2,1,0:T(2,128)}) custom-call(s32[8]{0:T(128)} %get-tuple-element.52.refs_0_.info_ref, f32[8,6912]{1,0:T(8,128)} %get-tuple-element.54.refs_1_.table_ref, bf16[1024,864]{1,0:T(8,128)(2,1)} %bitcast.189, bf16[864,1152]{1,0:T(8,128)(2,1)} %bitcast.202, bf16[2048,1152]{1,0:T(8,128)(2,1)} %refs_4_.1, ...), custom_call_target="tpu_custom_call" | custom-call | bytes 29700000 | tf_op jit(solution)/shard_map/leave/pallas_call | solution.py:211
  556.8 18.0 %collective-permute-done.47 = bf16[72,1152]{1,0:T(8,128)(2,1)S(1)} collective-permute-done((bf16[72,1152]{1,0:T(8,128)(2,1)S(1)}, bf16[72,1152]{1,0:T(8,128)(2,1)S(1)}, u32[]{:S(2)}, u32[]{:S(2)}) %collective-permute-start.47) | collective-permute-done | bytes 165920 | tf_op jit(solution)/shard_map/ppermute | solution.py:245
  598.5 7.5 %place_columns.1 = f32[1152,1152]{1,0:T(8,128)} custom-call(bf16[8,144,1152]{2,1,0:T(8,128)(2,1)} %pad_maximum_fusion.4.slices_ref), custom_call_target="tpu_custom_call" | custom-call | bytes 26400000 | tf_op jit(solution)/shard_map/place_columns/pallas_call | solution.py:211
  606.0 8.1 %reduce-scatter.9.cloned.1.call-done = bf16[1,1024,288]{2,1,0:T(8,128)(2,1)} async-done(((bf16[4,1024,288]{2,1,0:T(8,128)(2,1)}), bf16[1,1024,288]{2,1,0:T(8,128)(2,1)}) %reduce-scatter.9.cloned.1.call-update) | async-done | bytes 589840 | tf_op jit(solution)/shard_map/reduce_scatter | solution.py:860
  (452 shorter events, 284.0 us)
Async XLA Ops:
  7.2 66.5 %all-gather.3.cloned.1.call-start = ((), (), s32[]{:S(2)}) async-start(), calls=%async_computation.4 | async-start | bytes 1658880 | tf_op jit(solution)/shard_map/all_gather | solution.py:667
  15.3 145.1 %all-gather.5.cloned.1.call-start = ((), (), s32[]{:S(2)}) async-start(), calls=%async_computation.5 | async-start | bytes 1658880 | tf_op jit(solution)/shard_map/all_gather | solution.py:668
  28.5 35.5 %collective-permute-start.7 = (bf16[2,4,40,1152]{3,2,1,0:T(8,128)(2,1)S(1)}, bf16[2,4,40,1152]{3,2,1,0:T(8,128)(2,1)S(1)}, u32[]{:S(2)}, u32[]{:S(2)}) collective-permute-start(bf16[2,4,40,1152]{3,2,1,0:T(8,128)(2,1)S(1)} %pad_maximum_fusion.21), channel_id=1, source_target_pairs={{0,8},{4,20},{8,0},{12,28},{16,24},{20,4},{24,16},{28,12},{1,9},{5... | collective-permute-start | bytes 2211848 | tf_op jit(solution)/shard_map/ppermute | solution.py:256
  93.9 76.2 %collective-permute-start.16 = (bf16[1152,1152]{1,0:T(8,128)(2,1)S(1)}, bf16[1152,1152]{1,0:T(8,128)(2,1)}, u32[]{:S(2)}, u32[]{:S(2)}) collective-permute-start(bf16[1152,1152]{1,0:T(8,128)(2,1)S(1)} %pad_maximum_fusion.3.refs_8_.refs_2_.refs_10_), channel_id=1, source_target_pairs={{0,8},{4,20},{8,0},{12,28},{16,24},{20,4},{24,16},{28,12},{1,9},{5... | collective-permute-start | bytes 7962632 | tf_op jit(solution)/shard_map/ppermute | solution.py:256
  96.0 330.5 %reduce-scatter.11.cloned.1.call-start = ((), (), s32[]{:S(2)}) async-start(), calls=%async_computation.9 | async-start | bytes 1658880 | tf_op jit(solution)/shard_map/reduce_scatter | solution.py:860
  96.0 62.1 %collective-permute-start.14 = (bf16[4,4,40,1152]{3,2,1,0:T(8,128)(2,1)}, bf16[4,4,40,1152]{3,2,1,0:T(8,128)(2,1)S(1)}, u32[]{:S(2)}, u32[]{:S(2)}) collective-permute-start(bf16[4,4,40,1152]{3,2,1,0:T(8,128)(2,1)} %pad_maximum_fusion.8.refs_1_), channel_id=1, source_target_pairs={{0,4},{4,0},{8,12},{12,8},{16,20},{20,16},{24,28},{28,24},{1,5},{5... | collective-permute-start | bytes 4423688 | tf_op jit(solution)/shard_map/ppermute | solution.py:252
  100.8 45.3 %collective-permute-start.8 = (bf16[1,256,288]{2,1,0:T(8,128)(2,1)S(1)}, bf16[1,256,288]{2,1,0:T(8,128)(2,1)S(1)}, u32[]{:S(2)}, u32[]{:S(2)}) collective-permute-start(bf16[1,256,288]{2,1,0:T(8,128)(2,1)S(1)} %get-tuple-element.152), channel_id=1, source_target_pairs={{1,0},{2,1},{3,2},{0,3},{5,4},{6,5},{7,6},{4,7},{9,8},{10,9},{11,1... | collective-permute-start | bytes 442376 | tf_op jit(solution)/shard_map/ppermute | solution.py:245
  107.1 40.9 %collective-permute-start.13 = (bf16[1,256,288]{2,1,0:T(8,128)(2,1)S(1)}, bf16[1,256,288]{2,1,0:T(8,128)(2,1)S(1)}, u32[]{:S(2)}, u32[]{:S(2)}) collective-permute-start(bf16[1,256,288]{2,1,0:T(8,128)(2,1)S(1)} %get-tuple-element.146), channel_id=1, source_target_pairs={{3,0},{0,1},{1,2},{2,3},{7,4},{4,5},{5,6},{6,7},{11,8},{8,9},{9,10... | collective-permute-start | bytes 442376 | tf_op jit(solution)/shard_map/ppermute | solution.py:245
  243.5 45.8 %collective-permute-start.34 = (bf16[1152,1152]{1,0:T(8,128)(2,1)}, bf16[1152,1152]{1,0:T(8,128)(2,1)}, u32[]{:S(2)}, u32[]{:S(2)}) collective-permute-start(bf16[1152,1152]{1,0:T(8,128)(2,1)} %get-tuple-element.68.refs_19_), channel_id=1, source_target_pairs={{0,8},{4,20},{8,0},{12,28},{16,24},{20,4},{24,16},{28,12},{1,9},{5... | collective-permute-start | bytes 7962632 | tf_op jit(solution)/shard_map/ppermute | solution.py:256
  301.6 47.4 %collective-permute-start.35 = (bf16[1152,1152]{1,0:T(8,128)(2,1)}, bf16[1152,1152]{1,0:T(8,128)(2,1)}, u32[]{:S(2)}, u32[]{:S(2)}) collective-permute-start(bf16[1152,1152]{1,0:T(8,128)(2,1)} %get-tuple-element.75), channel_id=1, source_target_pairs={{0,4},{4,0},{8,12},{12,8},{16,20},{20,16},{24,28},{28,24},{1,5},{5... | collective-permute-start | bytes 7962632 | tf_op jit(solution)/shard_map/ppermute | solution.py:252
  302.4 46.7 %collective-permute-start.36 = (bf16[1152,1152]{1,0:T(8,128)(2,1)}, bf16[1152,1152]{1,0:T(8,128)(2,1)}, u32[]{:S(2)}, u32[]{:S(2)}) collective-permute-start(bf16[1152,1152]{1,0:T(8,128)(2,1)} %get-tuple-element.76), channel_id=1, source_target_pairs={{0,4},{4,0},{8,12},{12,8},{16,20},{20,16},{24,28},{28,24},{1,5},{5... | collective-permute-start | bytes 7962632 | tf_op jit(solution)/shard_map/ppermute | solution.py:252
  311.3 34.1 %collective-permute-start.37 = (bf16[576,1152]{1,0:T(8,128)(2,1)S(1)}, bf16[576,1152]{1,0:T(8,128)(2,1)S(1)}, u32[]{:S(2)}, u32[]{:S(2)}) collective-permute-start(bf16[576,1152]{1,0:T(8,128)(2,1)S(1)} %slice.274), channel_id=1, source_target_pairs={{0,16},{4,12},{8,24},{12,4},{16,0},{20,28},{24,8},{28,20},{1,17},{... | collective-permute-start | bytes 3981320 | tf_op jit(solution)/shard_map/ppermute | solution.py:256
  340.1 77.8 %collective-permute-start.27 = (bf16[2,256,288]{2,1,0:T(8,128)(2,1)}, bf16[2,256,288]{2,1,0:T(8,128)(2,1)}, u32[]{:S(2)}, u32[]{:S(2)}) collective-permute-start(bf16[2,256,288]{2,1,0:T(8,128)(2,1)} %get-tuple-element.134), channel_id=1, source_target_pairs={{0,3},{1,0},{2,1},{3,2},{4,7},{5,4},{6,5},{7,6},{8,11},{9,8},{10,9... | collective-permute-start | bytes 884744 | tf_op jit(solution)/shard_map/ppermute | solution.py:249
  344.3 75.7 %collective-permute-start.26 = (bf16[2,256,288]{2,1,0:T(8,128)(2,1)}, bf16[2,256,288]{2,1,0:T(8,128)(2,1)}, u32[]{:S(2)}, u32[]{:S(2)}) collective-permute-start(bf16[2,256,288]{2,1,0:T(8,128)(2,1)} %get-tuple-element.135), channel_id=1, source_target_pairs={{0,2},{1,3},{2,0},{3,1},{4,6},{5,7},{6,4},{7,5},{8,10},{9,11},{10,... | collective-permute-start | bytes 884744 | tf_op jit(solution)/shard_map/ppermute | solution.py:249
  345.4 74.6 %collective-permute-start.25 = (bf16[2,256,288]{2,1,0:T(8,128)(2,1)}, bf16[2,256,288]{2,1,0:T(8,128)(2,1)}, u32[]{:S(2)}, u32[]{:S(2)}) collective-permute-start(bf16[2,256,288]{2,1,0:T(8,128)(2,1)} %get-tuple-element.136), channel_id=1, source_target_pairs={{0,1},{1,2},{2,3},{3,0},{4,5},{5,6},{6,7},{7,4},{8,9},{9,10},{10,1... | collective-permute-start | bytes 884744 | tf_op jit(solution)/shard_map/ppermute | solution.py:249
  349.0 139.2 %reduce-scatter.5.cloned.1.call-start = ((), (), s32[]{:S(2)}) async-start(), calls=%async_computation.6 | async-start | bytes 3932160 | tf_op jit(solution)/shard_map/reduce_scatter | solution.py:855
  412.7 52.7 %collective-permute-start.38 = (bf16[1152,1152]{1,0:T(8,128)(2,1)}, bf16[1152,1152]{1,0:T(8,128)(2,1)}, u32[]{:S(2)}, u32[]{:S(2)}) collective-permute-start(bf16[1152,1152]{1,0:T(8,128)(2,1)} %get-tuple-element.82), channel_id=1, source_target_pairs={{0,8},{4,20},{8,0},{12,28},{16,24},{20,4},{24,16},{28,12},{1,9},{5... | collective-permute-start | bytes 7962632 | tf_op jit(solution)/shard_map/ppermute | solution.py:256
  417.9 43.2 %collective-permute-start.51 = (bf16[544,1152]{1,0:T(8,128)(2,1)}, bf16[544,1152]{1,0:T(8,128)(2,1)}, u32[]{:S(2)}, u32[]{:S(2)}) collective-permute-start(bf16[544,1152]{1,0:T(8,128)(2,1)} %fusion.1), channel_id=1, source_target_pairs={{0,8},{4,20},{8,0},{12,28},{16,24},{20,4},{24,16},{28,12},{1,9},{5... | collective-permute-start | bytes 3760136 | tf_op jit(solution)/shard_map/ppermute | solution.py:256
  422.7 115.3 %reduce-scatter.7.cloned.1.call-start = ((), (), s32[]{:S(2)}) async-start(), calls=%async_computation.7 | async-start | bytes 1658880 | tf_op jit(solution)/shard_map/reduce_scatter | solution.py:860
  437.6 45.3 %collective-permute-start.63 = (bf16[2,144,1152]{2,1,0:T(8,128)(2,1)}, bf16[2,144,1152]{2,1,0:T(8,128)(2,1)}, u32[]{:S(2)}, u32[]{:S(2)}) collective-permute-start(bf16[2,144,1152]{2,1,0:T(8,128)(2,1)} %pad_maximum_fusion.24), channel_id=1, source_target_pairs={{0,8},{4,20},{8,0},{12,28},{16,24},{20,4},{24,16},{28,12},{1,9},{5... | collective-permute-start | bytes 1990664 | tf_op jit(solution)/shard_map/ppermute | solution.py:256
  485.3 37.3 %collective-permute-start.64 = (bf16[4,144,1152]{2,1,0:T(8,128)(2,1)}, bf16[4,144,1152]{2,1,0:T(8,128)(2,1)}, u32[]{:S(2)}, u32[]{:S(2)}) collective-permute-start(bf16[4,144,1152]{2,1,0:T(8,128)(2,1)} %pad_maximum_fusion.11), channel_id=1, source_target_pairs={{0,4},{4,0},{8,12},{12,8},{16,20},{20,16},{24,28},{28,24},{1,5},{5... | collective-permute-start | bytes 3981320 | tf_op jit(solution)/shard_map/ppermute | solution.py:252
  504.0 110.2 %reduce-scatter.9.cloned.1.call-start = ((), (), s32[]{:S(2)}) async-start(), calls=%async_computation.8 | async-start | bytes 3932160 | tf_op jit(solution)/shard_map/reduce_scatter | solution.py:860
  534.7 51.4 %collective-permute-start.58 = (bf16[4,152,1152]{2,1,0:T(8,128)(2,1)}, bf16[4,152,1152]{2,1,0:T(8,128)(2,1)S(1)}, u32[]{:S(2)}, u32[]{:S(2)}) collective-permute-start(bf16[4,152,1152]{2,1,0:T(8,128)(2,1)} %pad_maximum_fusion.9), channel_id=1, source_target_pairs={{0,4},{4,0},{8,12},{12,8},{16,20},{20,16},{24,28},{28,24},{1,5},{5... | collective-permute-start | bytes 4202504 | tf_op jit(solution)/shard_map/ppermute | solution.py:252
  547.7 32.8 %collective-permute-start.46 = (bf16[72,1152]{1,0:T(8,128)(2,1)S(1)}, bf16[72,1152]{1,0:T(8,128)(2,1)S(1)}, u32[]{:S(2)}, u32[]{:S(2)}) collective-permute-start(bf16[72,1152]{1,0:T(8,128)(2,1)S(1)} %maximum_maximum_fusion.1), channel_id=1, source_target_pairs={{1,0},{2,1},{3,2},{0,3},{5,4},{6,5},{7,6},{4,7},{9,8},{10,9},{11,1... | collective-permute-start | bytes 497672 | tf_op jit(solution)/shard_map/ppermute | solution.py:245
  (117 other events, 1302.4 us)
Sparse Core Ops, SparseCore 0:
  15.4 35.6 all-gather.2
  96.1 58.3 all-gather.4
  349.1 50.7 reduce-scatter.10
  422.9 60.9 reduce-scatter.4
  504.1 33.9 reduce-scatter.6
  540.2 73.8 reduce-scatter.8

commit v2 on v1

--- a/solution.py
+++ b/solution.py
@@ -56,25 +56,28 @@
     lax.fori_loop(0, seq // chunk, step, 0)
 
 
-def attend(projected, row, heads, chunk, groups, order):
+def attend(projected, row, mixed, heads, chunk, groups, order):
     seq, width = projected.shape[1:]
     split = row == 0
+    kernel = functools.partial(attend_kernel, heads, chunk, groups, split)
+    earlier = [] if mixed is None else [mixed]
     return call(
-        functools.partial(attend_kernel, heads, chunk, groups, split),
-        [
-            shape_of((groups, 1, seq // groups, heads * HEAD_DIM), jnp.bfloat16),
+        kernel if mixed is None else lambda p, _, *refs: kernel(p, *refs),
+        [
+            shape_of((groups, 2, seq // groups, heads * HEAD_DIM), jnp.bfloat16),
             shape_of((1, heads, seq), jnp.float32),
         ],
-        [pl.BlockSpec((1, seq, width), lambda i: (row, 0, 0))],
-        [
-            pl.BlockSpec((groups, 1, seq // groups, heads * HEAD_DIM), lambda i: (0, 0, 0, 0)),
+        [pl.BlockSpec((1, seq, width), lambda i: (row, 0, 0))] + [pl.BlockSpec(memory_space=pl.ANY)] * len(earlier),
+        [
+            pl.BlockSpec((groups, 1, seq // groups, heads * HEAD_DIM), lambda i: (0, row, 0, 0)),
             pl.BlockSpec((1, heads, seq), lambda i: (0, 0, 0)),
         ],
         grid=(1,),
         name="attend_split" if split else "attend_whole",
         micros=6 if split else 16,
         order=order,
-    )(projected)
+        aliases={} if mixed is None else {1: 0},
+    )(projected, *earlier)
 
 
 def attend_back_kernel(heads, chunk, groups, split, proj_ref, lse_ref, pieces_ref, out_ref, dk_ref, dv_ref, grad_ref):
@@ -142,7 +145,7 @@
         [
             pl.BlockSpec((1, seq, width), lambda i: (row, 0, 0)),
             pl.BlockSpec((1, heads, seq), lambda i: (0, 0, 0)),
-            pl.BlockSpec((groups, 1, seq // groups, heads * HEAD_DIM), lambda i: (0, 0, 0, 0)),
+            pl.BlockSpec((groups, 1, seq // groups, heads * HEAD_DIM), lambda i: (0, row, 0, 0)),
         ],
         pl.BlockSpec((1, seq, width), lambda i: (0, 0, 0)),
         grid=(1,),
@@ -185,10 +188,10 @@
 
 
 def weight_of(micros):
-    return pl.CostEstimate(flops=0, bytes_accessed=int(micros * 3.3e6), transcendentals=0)
-
-
-def call(kernel, out_shape, in_specs, out_specs, grid=(), prefetch=0, scratch=(), name=None, micros=1, order=()):
+    return pl.CostEstimate(flops=int(micros * 2.2e10), bytes_accessed=int(micros * 6.6e7), transcendentals=0)
+
+
+def call(kernel, out_shape, in_specs, out_specs, grid=(), prefetch=0, scratch=(), name=None, micros=1, order=(), aliases={}):
     first = prefetch + len(in_specs)
 
     def ordered(*refs):
@@ -204,6 +207,7 @@
             scratch_shapes=scratch,
         ),
         out_shape=out_shape,
+        input_output_aliases=aliases,
         compiler_params=pltpu.CompilerParams(vmem_limit_bytes=VMEM_BYTES),
         cost_estimate=weight_of(micros),
         name=name,
@@ -211,13 +215,14 @@
     return lambda *arrays: run(*arrays, *order)
 
 
-def hold(values, *order):
+def hold(values, *order, micros=0):
     run = pl.pallas_call(
         lambda *refs: None,
         in_specs=[pl.BlockSpec(memory_space=pl.ANY)] * (1 + len(order)),
         out_specs=pl.BlockSpec(memory_space=pl.ANY),
         out_shape=shape_of(values.shape, values.dtype),
         input_output_aliases={0: 0},
+        cost_estimate=weight_of(micros),
         name="hold",
     )
     return run(values, *order)
@@ -247,6 +252,28 @@
     def send(self, values, distance):
         count = self.heads
         return lax.ppermute(values, "head", [(i, (i + distance) % count) for i in range(count)])
+
+    def head_swap(self, values, bit):
+        return lax.ppermute(values, "head", [(i, i ^ (1 << bit)) for i in range(self.heads)])
+
+    def head_cube(self, values, orders):
+        for bit in range(self.heads.bit_length() - 1):
+            more = self.head_swap(values, bit)
+            if bit < len(orders):
+                more = hold(more, orders[bit])
+            values = jnp.concatenate([values, more], axis=0)
+        return values
+
+    def head_gather(self, values):
+        return [values] + [self.fetch(values, distance) for distance in range(1, self.heads)]
+
+    def by_head(self, pieces):
+        values = pieces[0]
+        rows = values.shape[0]
+        held = jnp.zeros((self.heads * rows,) + values.shape[1:], values.dtype)
+        for distance in range(self.heads):
+            held = lax.dynamic_update_slice_in_dim(held, pieces[distance], self.at_head(distance) * rows, 0)
+        return held
 
     def core_swap(self, values):
         return lax.ppermute(values, "batch", [(i, i ^ 1) for i in range(self.batches)])
@@ -289,18 +316,30 @@
         own = jnp.concatenate(self.gather_levels(values), axis=0)
         return jnp.concatenate([own, self.core_swap(own)], axis=0)
 
-    def reduce_levels(self, kept, orders=()):
-        low = jnp.bfloat16
-        steps = []
-        for level in reversed(range(self.levels)):
-            more = self.link_swap(kept[1], level)
-            if len(orders) > len(steps):
-                more = hold(more, orders[len(steps)])
-            total = (kept[0].astype(jnp.float32) + more.astype(jnp.float32)).astype(low)
+    def reduce_cores(self, pieces, *order):
+        sums = []
+        for mine, other in zip(pieces[:2], pieces[2:]):
+            more = self.core_swap(other)
+            if order:
+                more = hold(more, *order)
+            sums.append((mine.astype(jnp.float32) + more.astype(jnp.float32)).astype(jnp.bfloat16))
+        return sums
+
+    def reduce_first(self, kept, *order):
+        more = self.link_swap(kept[1], self.levels - 1)
+        if order:
+            more = hold(more, *order)
+        return (kept[0].astype(jnp.float32) + more.astype(jnp.float32)).astype(jnp.bfloat16)
+
+    def reduce_rest(self, total, *order):
+        for level in reversed(range(self.levels - 1)):
             half = total.shape[0] // 2
-            kept = [total[:half], total[half:]]
-            steps.append(total)
-        return steps
+            more = self.link_swap(total[half:], level)
+            if order:
+                more = hold(more, *order)
+                order = ()
+            total = (total[:half].astype(jnp.float32) + more.astype(jnp.float32)).astype(jnp.bfloat16)
+        return total
 
     def by_owner(self, values):
         return jnp.concatenate(
@@ -364,7 +403,7 @@
     return jnp.where(row == 0, 1 + info_ref[1] * home // quarter, 0)
 
 
-def enter_kernel(link, quarter, info_ref, table_ref, split_ref, single_ref, proj_ref, tokens_ref, grad_ref, bias_ref,
+def enter_kernel(link, quarter, info_ref, table_ref, mixed_ref, proj_ref, tokens_ref, grad_ref, bias_ref,
                  attn_ref, stream_ref, mlp_in_ref, grad_mlp_ref, mixed_home_ref, proj_true_ref, grad_sum_ref):
     row = pl.program_id(0)
     heads = link.heads
@@ -386,14 +425,9 @@
                     at = spot * share + first
                     proj_true_ref[at : at + count, :] = piece[:count]
 
-    for at_row, mixed_ref in enumerate((split_ref, single_ref)):
-
-        @pl.when(row == at_row)
-        def _(mixed_ref=mixed_ref):
-            for spot in range(heads):
-                piece = mixed_ref[(spot - head + heads) % heads, 0]
-                mixed_home_ref[0, :, spot * share : (spot + 1) * share] = piece
-
+    for spot in range(heads):
+        piece = mixed_ref[(spot - head + heads) % heads, 0]
+        mixed_home_ref[0, :, spot * share : (spot + 1) * share] = piece
     spot = home_row(info_ref, row, home, quarter)
 
     def mod(group):
@@ -430,9 +464,8 @@
                     tokens_grad_ref, stream_ref, attn_ref, proj_ref, *refs):
     count = 4
     ins, outs = refs[:count], refs[count : 2 * count]
-    (grad_pre_ref, pre_sum_ref, block_ref, stream_grad_ref, grad_attn_ref, split_ref, single_ref, sums_ref, attn_sum_ref,
+    (grad_pre_ref, pre_sum_ref, block_ref, stream_grad_ref, grad_attn_ref, grad_mixed_ref, sums_ref, attn_sum_ref,
      mlp_acc, grad_acc) = refs[2 * count :]
-    grad_mixed_refs = (split_ref, single_ref)
     step = pl.program_id(0)
     heads = link.heads
     rows, home, width = stream_ref.shape
@@ -484,7 +517,7 @@
             attn_sum += jnp.sum(grad_attn.astype(jnp.float32), axis=0, keepdims=True)
             grad_mixed = nt(grad_attn, proj_ref[...]).astype(jnp.bfloat16)
             for other in range(heads):
-                grad_mixed_refs[row][(other - head + heads) % heads, 0] = grad_mixed[:, other * share : (other + 1) * share]
+                grad_mixed_ref[(other - head + heads) % heads, row] = grad_mixed[:, other * share : (other + 1) * share]
         attn_sum_ref[...] = attn_sum
 
 
@@ -518,18 +551,15 @@
         shares_ref[head] = low[:, head * share : (head + 1) * share]
 
 
-def unit_grads_kernel(steps, left_ref, right_ref, *refs):
-    more, outs = refs[:2], refs[2:]
-    for spot in range(2):
+def unit_grads_kernel(steps, left_ref, right_ref, *outs):
+    for spot in range(4):
 
         @pl.when(pl.program_id(0) // steps == spot)
         def _(spot=spot):
-            total = tn(left_ref[...], right_ref[...])
-            total = total + more[spot][...].astype(jnp.float32)
-            outs[spot][...] = total.astype(jnp.bfloat16)
-
-
-def unit_grads(left, right, half, more=(), order=()):
+            outs[spot][...] = tn(left_ref[...], right_ref[...]).astype(jnp.bfloat16)
+
+
+def unit_grads(left, right, order=()):
     count, total = left.shape
     width = right.shape[1]
     piece = total // 4
@@ -538,27 +568,15 @@
     def spec(spot):
         return pl.BlockSpec((UNIT_TILE, width), lambda i: (jnp.clip(i - spot * steps, 0, steps - 1), 0))
 
-    kernel = functools.partial(unit_grads_kernel, steps)
-    if not more:
-        kernel = lambda l, r, *outs: unit_grads_plain(steps, l, r, *outs)
     return call(
-        kernel,
-        [shape_of((piece, width), jnp.bfloat16)] * 2,
-        [pl.BlockSpec((count, UNIT_TILE), lambda i: (0, i + half * 2 * steps)), whole((count, width))]
-        + [spec(i) for i in range(len(more))],
-        [spec(0), spec(1)],
-        grid=(2 * steps,),
-        name="unit_grads", micros=6,
+        functools.partial(unit_grads_kernel, steps),
+        [shape_of((piece, width), jnp.bfloat16)] * 4,
+        [pl.BlockSpec((count, UNIT_TILE), lambda i: (0, i)), whole((count, width))],
+        [spec(i) for i in range(4)],
+        grid=(4 * steps,),
+        name="unit_grads", micros=14,
         order=order,
-    )(left, right, *more)
-
-
-def unit_grads_plain(steps, left_ref, right_ref, *outs):
-    for spot in range(2):
-
-        @pl.when(pl.program_id(0) // steps == spot)
-        def _(spot=spot):
-            outs[spot][...] = tn(left_ref[...], right_ref[...]).astype(jnp.bfloat16)
+    )(left, right)
 
 
 def place_rows_kernel(link, slices_ref, out_ref):
@@ -579,7 +597,7 @@
         [pl.BlockSpec(slices.shape[:2] + (tile,), lambda i: (0, 0, i))],
         pl.BlockSpec((rows, tile), lambda i: (0, i)),
         grid=(width // tile,),
-        name="place_rows", micros=4,
+        name="place_rows", micros=0,
     )(slices)
 
 
@@ -600,7 +618,7 @@
         pl.BlockSpec((tile, batches * rows), lambda i: (i, 0)),
         grid=(width // tile,),
         scratch=[pltpu.VMEM((batches * rows, tile), jnp.float32)],
-        name="place_columns", micros=8,
+        name="place_columns", micros=0,
     )(slices)
 
 
@@ -660,10 +678,8 @@
 
     slice_rows = -(-share // (8 * batches)) * 8
     proj_pad = jnp.pad(proj_weight, ((0, slice_rows * batches - share), (0, 0)))
-    proj_slice = lax.dynamic_slice_in_dim(proj_pad, batch * slice_rows, slice_rows, 0)
     in_slice = lax.dynamic_slice_in_dim(in_weight, batch * units, units, 1).T
     out_slice = lax.dynamic_slice_in_dim(out_weight, batch * units, units, 0)
-    proj_rel = jnp.stack([proj_slice] + [link.fetch(proj_slice, j) for j in range(1, heads)])
     in_gathered = lax.all_gather(in_slice, "head", axis=0, tiled=True)
     out_gathered = lax.all_gather(out_slice, "head", axis=0, tiled=True)
     def tokens_block(i, info_ref):
@@ -694,25 +710,30 @@
         grid=(4 * rows,),
         prefetch=1,
         name="project", micros=13,
-        order=[proj_rel],
     )(info, table_rel, tokens, qkv_t, full_bias)
     projected = projected.reshape(rows, SEQ, qkv_here)
-    mixed_rows = []
-    mixed_here_rows = []
+    proj_slice = hold(lax.dynamic_slice_in_dim(proj_pad, batch * slice_rows, slice_rows, 0), table_rel)
+    proj_rel = jnp.stack(
+        [proj_slice] + [hold(link.fetch(proj_slice, j), projected) for j in range(1, heads)]
+    )[None]
+    mixed = None
     log_totals = []
-    proj_own = jnp.concatenate(link.gather_levels(proj_rel[None]), axis=0)
-    orders = [[proj_own]]
     for row in range(rows):
-        mixed, log_total = attend(projected, row, heads_here, quarter, heads, orders[row])
-        mixed_rows.append(jnp.stack([mixed[0]] + [link.fetch(mixed[j], j) for j in range(1, heads)]))
-        mixed_here_rows.append(mixed)
+        order = [in_gathered] if row == 1 else []
+        mixed, log_total = attend(projected, row, mixed, heads_here, quarter, heads, order)
+        log_totals.append(log_total)
+        if row < link.levels:
+            proj_rel = jnp.concatenate([proj_rel, hold(link.link_swap(proj_rel, row), log_total)], axis=0)
         if row == 0:
-            in_gathered = hold(in_gathered, mixed)
-            orders.append([in_gathered])
-        log_totals.append(log_total)
-
-    proj_all = jnp.concatenate([proj_own, link.core_swap(proj_own)], axis=0)
-    in_held = link.gather_levels(in_gathered, [mixed_here_rows[1]])
+            in_gathered = hold(in_gathered, log_total)
+    in_held = link.gather_levels(in_gathered, [log_totals[1]])
+    for level in range(rows, link.levels):
+        proj_rel = jnp.concatenate([proj_rel, link.link_swap(proj_rel, level)], axis=0)
+    proj_all = jnp.concatenate([proj_rel, link.core_swap(proj_rel)], axis=0)
+    out_gathered = hold(out_gathered, in_held[0])
+    mixed = hold(mixed, out_gathered, proj_all, micros=20)
+    mixed_all = jnp.stack([mixed[0]] + [link.fetch(mixed[j], j) for j in range(1, heads)])
+
     out_held = link.gather_levels(out_gathered)
     out_pieces = out_held + [link.core_swap(piece) for piece in out_held]
     tokens_rows = tokens.reshape(rows, SEQ, width)
@@ -732,8 +753,7 @@
         ],
         [
             whole((8, 6 * width)),
-            whole((heads, 1, home, share)),
-            whole((heads, 1, home, share)),
+            pl.BlockSpec((heads, 1, home, share), lambda i, _: (0, i, 0, 0)),
             whole(proj_all.shape),
             home_spec,
             home_spec,
@@ -743,8 +763,8 @@
         grid=(rows,),
         prefetch=1,
         name="enter", micros=9,
-        order=[in_held[0], out_gathered],
-    )(info, table, *mixed_rows, proj_all, tokens_rows, grad_rows, proj_bias.astype(full)[None])
+        order=[out_held[0]],
+    )(info, table, mixed_all, proj_all, tokens_rows, grad_rows, proj_bias.astype(full)[None])
 
     in_held[1] = hold(in_held[1], mlp_in)
     in_pieces = in_held + [link.core_swap(piece) for piece in in_held]
@@ -772,13 +792,11 @@
         order=[out_held[0]],
     )(mlp_in, in_bias_all, *in_pieces)
 
-    out_far = unit_grads(hidden, grad_mlp, 1)
-    out_near = unit_grads(hidden, grad_mlp, 0, [link.core_swap(piece) for piece in out_far])
+    out_parts = unit_grads(hidden, grad_mlp, order=[out_pieces[2]])
 
     stay = pl.BlockSpec((rows, home, width), lambda *_: (0, 0, 0))
     by_head = whole((heads, rows, home, share))
-    one_row = whole((heads, 1, home, share))
-    grad_pre, pre_sum, block_home, stream_grad, grad_attn, mixed_split, mixed_single, home_sums, attn_sum = call(
+    grad_pre, pre_sum, block_home, stream_grad, grad_attn, grad_mixed, home_sums, attn_sum = call(
         functools.partial(contract_kernel, link, quarter, steps),
         [
             shape_of((home_count, unit_count), low),
@@ -786,8 +804,7 @@
             shape_of((heads, rows, home, share), low),
             shape_of((rows, home, width), full),
             shape_of((rows, home, width), low),
-            shape_of((heads, 1, home, share), low),
-            shape_of((heads, 1, home, share), low),
+            shape_of((heads, rows, home, share), low),
             shape_of((rows, 4, width), full),
             shape_of((1, width), full),
         ],
@@ -803,78 +820,95 @@
             whole((width, width)),
         ]
         + [piece_spec(spot) for spot in range(4)] * 2,
-        [tile_spec, bias_spec, by_head, stay, stay, one_row, one_row, whole((rows, 4, width)), whole((1, width))],
+        [tile_spec, bias_spec, by_head, stay, stay, by_head, whole((rows, 4, width)), whole((1, width))],
         grid=(4 * steps,),
         prefetch=1,
         scratch=[pltpu.VMEM((home_count, width), full)] * 2,
         name="contract", micros=44,
-        order=list(out_near),
+        order=[out_parts[0]],
     )(info, table, grad_mlp, hidden, slope, out_bias.astype(full)[None], grad_rows, stream, attn, proj_true,
       *in_pieces, *out_pieces)
-    grad_mixed_rows = [
-        jnp.stack([piece[0]] + [link.send(piece[j], j) for j in range(1, heads)])
-        for piece in (mixed_split, mixed_single)
-    ]
-    out_sums = link.reduce_levels(list(out_near))
-    in_far = unit_grads(grad_pre, mlp_in, 1, order=[out_sums[0]])
-    in_near = unit_grads(
-        grad_pre, mlp_in, 0, [link.core_swap(piece) for piece in in_far], order=[grad_mixed_rows[0]]
-    )
+    mixed_sends = [link.send(grad_mixed[j], j) for j in range(1, heads)]
+    out_near = link.reduce_cores(out_parts, grad_pre)
+    out_sum = link.reduce_first(out_near)
+    in_parts = unit_grads(grad_pre, mlp_in, order=[out_near[1]])
+    grad_mixed = jnp.stack([grad_mixed[0]] + [hold(piece, in_parts[0]) for piece in mixed_sends])
+    out_slice = link.reduce_rest(out_sum)
+    in_near = link.reduce_cores(in_parts, grad_mixed)
     proj_grad = tn(mixed_home.reshape(home_count, width), grad_attn.reshape(home_count, width)).astype(low)
 
+    def head_sum(values):
+        return lax.psum_scatter(values, "head", scatter_dimension=0, tiled=True)
+
+    out_blocks = out_slice.reshape(heads, units, width)
+
+    def out_block(distance):
+        return lax.dynamic_index_in_dim(out_blocks, link.at_head(distance), 0, keepdims=False)
+
+    out_more = [link.send(out_block(j), j) for j in range(1, heads)]
     grad_rows_low = []
     block_sums = []
-    shares = []
+    shares = None
     for row in range(rows):
         grad_row = attend_back(
-            projected, row, log_totals[row], grad_mixed_rows[row], heads_here, quarter, heads,
-            [in_near[0], out_sums[-1]] if row == 0 else [sums_row],
+            projected, row, log_totals[row], grad_mixed, heads_here, quarter, heads,
+            [] if row == 0 else [sums_row, out_slice],
         )[0]
-        share_row, sums_row = call(
-            functools.partial(leave_kernel, link, quarter, row),
-            [shape_of((heads, SEQ, share), low), shape_of((4, 2, width), full)],
+        order = list(in_near) + [out_sum]
+        if row == 1:
+            in_sum = link.reduce_first(in_near, grad_row)
+            order = [in_sum]
+        earlier = [] if shares is None else [shares]
+        kernel = functools.partial(leave_kernel, link, quarter, row)
+        shares, sums_row = call(
+            kernel if row == 0 else lambda *refs: kernel(*refs[:6], *refs[7:]),
+            [shape_of((heads, token_count, share), low), shape_of((4, 2, width), full)],
             [
                 whole((8, 6 * width)),
                 pl.BlockSpec((quarter, qkv_here), lambda i, _: (i, 0)),
                 whole((qkv_here, width)),
                 pl.BlockSpec((quarter, width), lambda i, info_ref, row=row: tokens_block(i + 4 * row, info_ref)),
                 pl.BlockSpec((1, home, width), lambda i, _, row=row: (row, 0, 0)),
-            ],
+            ]
+            + [pl.BlockSpec(memory_space=pl.ANY)] * len(earlier),
             [
-                pl.BlockSpec((heads, quarter, share), lambda i, _: (0, i, 0)),
+                pl.BlockSpec((heads, quarter, share), lambda i, _, row=row: (0, i + 4 * row, 0)),
                 pl.BlockSpec((1, 2, width), lambda i, _: (i, 0, 0)),
             ],
             grid=(4,),
             prefetch=1,
             scratch=[pltpu.VMEM((quarter, width), full)],
             name="leave", micros=9,
-            order=shares,
-        )(info, table, grad_row, qkv_t, tokens, stream_grad)
+            aliases={6: 0} if earlier else {},
+            order=order,
+        )(info, table, grad_row, qkv_t, tokens, stream_grad, *earlier)
         grad_rows_low.append(grad_row)
         block_sums.append(sums_row)
-        shares.append(lax.psum_scatter(share_row, "head", scatter_dimension=0, tiled=True)[0] if row == 0 else share_row)
-    grad_projected = jnp.concatenate(grad_rows_low, axis=0)
-    in_sums = link.reduce_levels(list(in_near), [grad_rows_low[1], shares[1]])
-
-    def head_sum(values):
-        return lax.psum_scatter(values, "head", scatter_dimension=0, tiled=True)
-
-    out_slice_sum = head_sum(out_sums[-1])
-    in_slice_sum = head_sum(hold(in_sums[-1], shares[0]))
-    shares[1] = head_sum(hold(shares[1], in_slice_sum))[0]
+    in_slice = link.reduce_rest(in_sum, sums_row)
+    out_slice_sum = out_block(0).astype(full)
+    for more in out_more:
+        out_slice_sum = out_slice_sum + hold(more, grad_rows_low[1]).astype(full)
+    out_slice_sum = out_slice_sum.astype(low)
+    grad_projected = hold(jnp.concatenate(grad_rows_low, axis=0), in_slice)
+
+    in_slice_sum = head_sum(in_slice)
+    shares = head_sum(hold(shares, in_slice_sum))[0]
     tokens_grad = jnp.where(
-        info[0] == 0, jnp.concatenate(shares, axis=0), jnp.concatenate(shares[::-1], axis=0)
+        info[0] == 0, shares, jnp.concatenate([shares[SEQ:], shares[:SEQ]], axis=0)
     )
 
-    block_home = jnp.stack([block_home[0]] + [link.send(block_home[j], j) for j in range(1, heads)])
+    block_home = hold(block_home, grad_mixed)
+    block_home = jnp.stack(
+        [block_home[0]] + [hold(link.send(block_home[j], j), sums_row) for j in range(1, heads)]
+    )
     block_out = call(
         functools.partial(lay_home_kernel, heads),
         shape_of((rows, SEQ, share), low),
         [whole((heads, rows, home, share))],
         whole((rows, SEQ, share)),
         prefetch=1,
-        name="lay_home", micros=3,
-        order=[grad_rows_low[1]],
+        name="lay_home", micros=0,
+        order=[sums_row],
     )(info, block_home).reshape(token_count, share)
 
     home_quarter = lax.axis_index("head") * home // quarter
@@ -898,7 +932,7 @@
         axis=1,
     ).reshape(1, -1)
     sent = jnp.concatenate([seg_grads, bias_grads, jnp.zeros((2, 6 * width), full)], axis=0)
-    sent = sent.reshape(8, heads, ada_here)
+    sent = hold(sent, in_slice).reshape(8, heads, ada_here)
 
     def sent_block(distance):
         return lax.dynamic_index_in_dim(sent, link.at_head(distance), 1, keepdims=False)
@@ -916,7 +950,7 @@
         ],
         axis=0,
     )
-    all_held = link.gather_batch(held[None])
+    all_held = hold(link.gather_batch(held[None]), in_slice_sum)
     all_classes = (all_held[:, 7, :5] + 0.5).astype(jnp.int32).reshape(-1)
     class_hits = (
         lax.broadcasted_iota(jnp.int32, (cond_count, 1), 0) == all_classes[None, :]
@@ -961,7 +995,7 @@
     both = both.reshape(2, 2, -1, width)
     got = [link.core_swap(piece) for piece in both[1]]
     both = [(mine.astype(full) + more.astype(full)).astype(low) for mine, more in zip(both[0], got)]
-    both = link.reduce_levels(both)[-1]
+    both = link.reduce_rest(link.reduce_first(both))
     proj_blocks = both[qkv_rows:].reshape(heads, slice_rows, width)
 
     def proj_block(distance):

time: 636 us -> 615 us (0.967)
  waiting for transfers between devices: 181 us -> 113 us
  other arithmetic: 57.9 us -> 85.1 us
  starting transfers between devices: 77.1 us -> 101 us
  Pallas kernels: 225 us -> 218 us
    ppermute x15 -> x12, waiting for transfers between devices: 89.3 us -> 21 us  [fetch(): lax.ppermute(values, 'head', [((i + distance) % count, i) for i in range(...]
    ppermute x15, starting transfers between devices: 14.4 us -> 56.4 us  [core_swap(): lax.ppermute(values, 'batch', [(i, i ^ 1) for i in range(self.batches)])]
    ppermute x20, waiting for transfers between devices: 55.1 us -> 34.6 us  [link_swap(): return lax.ppermute(values, 'batch', pairs)]
    ppermute x15, waiting for transfers between devices: 16.1 us -> 36.4 us  [send(): lax.ppermute(values, 'head', [(i, (i + distance) % count) for i in range(...]
    convert_element_type x6 -> x9, other arithmetic: 13.8 us -> 26.2 us  [the longest x3 11.8 us: reduce_cores(): (mine.astype(jnp.float32) + more.astype(jnp.float32)).astype(jnp.bfloat16)]
    reduce_scatter x3 -> x2, waiting for transfers between devices: 10.5 us -> 19.9 us  [head_sum(): return lax.psum_scatter(values, 'head', scatter_dimension=0, tiled=True)]
    ppermute x15, starting transfers between devices: 25.1 us -> 16.1 us  [send(): lax.ppermute(values, 'head', [(i, (i + distance) % count) for i in range(...]
    ppermute x15, waiting for transfers between devices: 9.95 us -> 1.02 us  [core_swap(): lax.ppermute(values, 'batch', [(i, i ^ 1) for i in range(self.batches)])]
  transfers between devices with their start and end apart: 71 -> 66, of which waited for: 32 -> 25; matrix products, arithmetic and copies ran while one was open for 16% -> 23% of each run, Pallas kernels for 35% -> 36%
where the time goes in v2:
time: 615 us; the launch traced here: 605 us
  Pallas kernels  218 us (35%)
  waiting for transfers between devices  113 us (18%)
  starting transfers between devices  101 us (16%)
  other arithmetic  85.1 us (14%)
  local copies, waits for them, and re-layouts  51.5 us (8%)
  matrix products  21.3 us (3%)
  between operations  15.3 us (2%)
    pallas_call x18, Pallas kernels, call(): return lambda *arrays: run(*arrays, *order)  218 us
    ppermute x15, starting transfers between devices, core_swap(): lax.ppermute(values, 'batch', [(i, i ^ 1) for i in range(self.batches)])  56.4 us
    ppermute x15, waiting for transfers between devices, send(): lax.ppermute(values, 'head', [(i, (i + distance) % count) for i in range(...  36.4 us
    ppermute x20, waiting for transfers between devices, link_swap(): return lax.ppermute(values, 'batch', pairs)  34.6 us
    ppermute x12, waiting for transfers between devices, fetch(): lax.ppermute(values, 'head', [((i + distance) % count, i) for i in range(...  21 us
    reduce_scatter x2, waiting for transfers between devices, head_sum(): return lax.psum_scatter(values, 'head', scatter_dimension=0, tiled=True)  19.9 us
    dot_general x3, matrix products, tn(): lax.dot_general(left_side, right_side, (((0,), (0,)), ((), ())), preferre...  17.4 us
    unnamed x151, local copies, waits for them, and re-layouts  16.6 us
  transfers between devices with their start and end apart: 66, of which 25 were waited for; matrix products, arithmetic and copies ran while one was open for 23% of the time, Pallas kernels for 36%

profile of v2, /device:TPU:9, one launch (start us, length us, event | category | flops | bytes accessed | tf_op | source)
XLA Modules:
  0.0 605.4 jit_solution(11039239193200062681)
XLA Ops:
  30.8 12.9 %project.1 = (bf16[2048,1152]{1,0:T(8,128)(2,1)}, bf16[2048,864]{1,0:T(8,128)(2,1)}, f32[8,6912]{1,0:T(8,128)}) custom-call(s32[8]{0:T(128)} %get-tuple-element.51.info_ref.refs_0_, f32[4,8,1728]{2,1,0:T(8,128)} %pad_maximum_fusion.24.table_rel_ref.refs_1_, bf16[2048,1152]{1,0:T(8,128)(2,1)} %refs_4_.3, bf16[864,1152]{1,0:T(8,128)(2,1)} %bitcast.237, ...), custom_call_target="tpu_custom_call" | custom-call | flops 285999988736 | bytes 858000000 | tf_op jit(solution)/shard_map/project/pallas_call | solution.py:215
  51.4 8.4 %attend_split.1 = (bf16[4,2,256,288]{3,2,1,0:T(8,128)(2,1)}, f32[1,4,1024]{2,1,0:T(4,128)}) custom-call(bf16[2,1024,864]{2,1,0:T(8,128)(2,1)} %bitcast.187), custom_call_target="tpu_custom_call" | custom-call | flops 131999997952 | bytes 396000000 | tf_op jit(solution)/shard_map/attend_split/pallas_call | solution.py:215
  64.0 15.0 %attend_whole.1 = (bf16[4,2,256,288]{3,2,1,0:T(8,128)(2,1)}, f32[1,4,1024]{2,1,0:T(4,128)}) custom-call(bf16[2,1024,864]{2,1,0:T(8,128)(2,1)} %bitcast.188, bf16[4,2,256,288]{3,2,1,0:T(8,128)(2,1)} %get-tuple-element.55.refs_1_, bf16[576,1152]{1,0:T(8,128)(2,1)} %hold.31.refs_2_), custom_call_target="tpu_custom_call", output_to_operand_aliasing={{0}: (1, {})} | custom-call | flops 352000016384 | bytes 1056000000 | tf_op jit(solution)/shard_map/attend_whole/pallas_call | solution.py:215
  100.1 6.7 %collective-permute-done.10 = bf16[2,256,288]{2,1,0:T(8,128)(2,1)S(1)} collective-permute-done((bf16[2,256,288]{2,1,0:T(8,128)(2,1)S(1)}, bf16[2,256,288]{2,1,0:T(8,128)(2,1)S(1)}, u32[]{:S(2)}, u32[]{:S(2)}) %collective-permute-start.10) | collective-permute-done | bytes 294944 | tf_op jit(solution)/shard_map/ppermute | solution.py:250
  106.9 19.2 %collective-permute-start.15 = (bf16[1152,1152]{1,0:T(8,128)(2,1)}, bf16[1152,1152]{1,0:T(8,128)(2,1)}, u32[]{:S(2)}, u32[]{:S(2)}) collective-permute-start(bf16[1152,1152]{1,0:T(8,128)(2,1)} %pad_maximum_fusion.3.refs_1_.refs_2_.refs_10_), channel_id=1, source_target_pairs={{0,4},{4,0},{8,12},{12,8},{16,20},{20,16},{24,28},{28,24},{1,5},{5... | collective-permute-start | bytes 7962632 | tf_op jit(solution)/shard_map/ppermute | solution.py:279
  136.6 9.0 %enter.1 = (f32[2,256,1152]{2,1,0:T(8,128)}, f32[2,256,1152]{2,1,0:T(8,128)}, bf16[2,256,1152]{2,1,0:T(8,128)(2,1)}, bf16[2,256,1152]{2,1,0:T(8,128)(2,1)}, bf16...) custom-call(s32[8]{0:T(128)} %get-tuple-element.51.info_ref.refs_0_, ...), custom_call_target="tpu_custom_call" | custom-call | flops 198000001024 | bytes 594000000 | tf_op jit(solution)/shard_map/enter/pallas_call | solution.py:215
  153.5 14.1 %collective-permute-done.17.refs_15_ = bf16[1152,1152]{1,0:T(8,128)(2,1)} collective-permute-done((bf16[1152,1152]{1,0:T(8,128)(2,1)}, bf16[1152,1152]{1,0:T(8,128)(2,1)}, u32[]{:S(2)}, u32[]{:S(2)}) %collective-permute-start.17) | collective-permute-done | bytes 2654240 | tf_op jit(solution)/shard_map/ppermute | solution.py:283
  169.0 19.6 %expand.1 = (bf16[512,4608]{1,0:T(8,128)(2,1)}, bf16[512,4608]{1,0:T(8,128)(2,1)}) custom-call(bf16[512,1152]{1,0:T(8,128)(2,1)} %bitcast.214, f32[1,4608]{1,0:T(1,128)} %reshape.232.refs_1_, bf16[1152,1152]{1,0:T(8,128)(2,1)} %pad_maximum_fusion.3.refs_1_.refs_2_.refs_10_, bf16[1152,1152]{1,0:T(8,128)(2,1)} %hold.41.refs_3_.refs_11_, ...), custom_call_target="tpu_custom_call" | custom-call | flops 439999987712 | bytes 1320000000 | tf_op jit(solution)/shard_map/expand/pallas_call | solution.py:215
  188.7 15.0 %unit_grads.2 = (bf16[1152,1152]{1,0:T(8,128)(2,1)}, bf16[1152,1152]{1,0:T(8,128)(2,1)}, bf16[1152,1152]{1,0:T(8,128)(2,1)}, bf16[1152,1152]{1,0:T(8,128)(2,1)}) custom-call(bf16[512,4608]{1,0:T(8,128)(2,1)} %get-tuple-element.61.refs_0_.refs_3_, bf16[512,1152]{1,0:T(8,128)(2,1)} %bitcast.240, bf16[1152,1152]{1,0:T(8,128)(2,1)} %collective-permute-done.18.refs_2_.refs_16_), custom_call_target="tpu_custom_call" | custom-call | flops 307999997952 | bytes 924000000 | tf_op jit(solution)/shard_map/unit_grads/pallas_call | solution.py:215
  204.2 43.8 %contract.1 = (bf16[512,4608]{1,0:T(8,128)(2,1)}, f32[1,4608]{1,0:T(1,128)}, bf16[4,2,256,288]{3,2,1,0:T(8,128)(2,1)}, f32[2,256,1152]{2,1,0:T(8,128)}, bf16[2,2...) custom-call(s32[8]{0:T(128)} %get-tuple-element.51.info_ref.refs_0_, ...), custom_call_target="tpu_custom_call" | custom-call | flops 968000012288 | bytes 2904000000 | tf_op jit(solution)/shard_map/contract/pallas_call | solution.py:215
  262.5 14.9 %unit_grads.3 = (bf16[1152,1152]{1,0:T(8,128)(2,1)}, bf16[1152,1152]{1,0:T(8,128)(2,1)}, bf16[1152,1152]{1,0:T(8,128)(2,1)}, bf16[1152,1152]{1,0:T(8,128)(2,1)}) custom-call(bf16[512,4608]{1,0:T(8,128)(2,1)} %get-tuple-element.69.refs_1_.refs_0_, bf16[512,1152]{1,0:T(8,128)(2,1)} %bitcast.215, bf16[1152,1152]{1,0:T(8,128)(2,1)} %add_convert_fusion.5.refs_2_), custom_call_target="tpu_custom_call" | custom-call | flops 307999997952 | bytes 924000000 | tf_op jit(solution)/shard_map/unit_grads/pallas_call | solution.py:215
  279.1 7.9 %collective-permute-done.22.refs_0_ = bf16[2,256,288]{2,1,0:T(8,128)(2,1)} collective-permute-done((bf16[2,256,288]{2,1,0:T(8,128)(2,1)}, bf16[2,256,288]{2,1,0:T(8,128)(2,1)}, u32[]{:S(2)}, u32[]{:S(2)}) %collective-permute-start.22) | collective-permute-done | bytes 294944 | tf_op jit(solution)/shard_map/ppermute | solution.py:254
  291.9 9.3 %attend_back_split.1 = bf16[1,1024,864]{2,1,0:T(8,128)(2,1)} custom-call(bf16[2,1024,864]{2,1,0:T(8,128)(2,1)} %bitcast.189, f32[1,4,1024]{2,1,0:T(4,128)} %get-tuple-element.56.refs_1_.lse_ref, bf16[4,2,256,288]{3,2,1,0:T(8,128)(2,1)} %pad_maximum_fusion.8.refs_1_.pieces_ref.refs_2_), custom_call_target="tpu_custom_call" | custom-call | flops 176000008192 | bytes 528000000 | tf_op jit(solution)/shard_map/attend_back_split/pallas_call | solution.py:215
  319.9 10.0 %leave.2 = (bf16[4,2048,288]{2,1,0:T(8,128)(2,1)}, f32[4,2,1152]{2,1,0:T(2,128)}) custom-call(s32[8]{0:T(128)} %get-tuple-element.51.info_ref.refs_0_, f32[8,6912]{1,0:T(8,128)} %get-tuple-element.53.refs_1_, bf16[1024,864]{1,0:T(8,128)(2,1)} %bitcast.207, bf16[864,1152]{1,0:T(8,128)(2,1)} %bitcast.238, bf16[2048,1152]{1,0:T(8,128)(2,1)} %refs_4_.3, ...), custom_call_target="tpu_custom_call" | custom-call | flops 198000001024 | bytes 594000000 | tf_op jit(solution)/shard_map/leave/pallas_call | solution.py:215
  336.9 22.8 %attend_back_whole.1 = bf16[1,1024,864]{2,1,0:T(8,128)(2,1)} custom-call(bf16[2,1024,864]{2,1,0:T(8,128)(2,1)} %bitcast.190, f32[1,4,1024]{2,1,0:T(4,128)} %get-tuple-element.58.refs_1_, bf16[4,2,256,288]{3,2,1,0:T(8,128)(2,1)} %pad_maximum_fusion.8.refs_1_.pieces_ref.refs_2_, f32[4,2,1152]{2,1,0:T(2,128)} %get-tuple-element.78.refs_3_, ...), custom_call_target="tpu_custom_call" | custom-call | flops 527999991808 | bytes 1584000000 | tf_op jit(solution)/shard_map/attend_back_whole/pallas_call | solution.py:215
  391.7 10.3 %leave.3 = (bf16[4,2048,288]{2,1,0:T(8,128)(2,1)}, f32[4,2,1152]{2,1,0:T(2,128)}) custom-call(s32[8]{0:T(128)} %get-tuple-element.51.info_ref.refs_0_, f32[8,6912]{1,0:T(8,128)} %get-tuple-element.53.refs_1_, bf16[1024,864]{1,0:T(8,128)(2,1)} %bitcast.182, bf16[864,1152]{1,0:T(8,128)(2,1)} %bitcast.239, ...), custom_call_target="tpu_custom_call", output_to_operand_aliasing={{0}: (6, {})} | custom-call | flops 198000001024 | bytes 594000000 | tf_op jit(solution)/shard_map/leave/pallas_call | solution.py:215
  403.7 7.7 %collective-permute-done.31.refs_0_ = bf16[2,256,288]{2,1,0:T(8,128)(2,1)} collective-permute-done((bf16[2,256,288]{2,1,0:T(8,128)(2,1)}, bf16[2,256,288]{2,1,0:T(8,128)(2,1)}, u32[]{:S(2)}, u32[]{:S(2)}) %collective-permute-start.31) | collective-permute-done | bytes 294944 | tf_op jit(solution)/shard_map/ppermute | solution.py:254
  430.1 9.9 %convolution_convert_fusion = bf16[864,1152]{1,0:T(8,128)(2,1)} fusion(bf16[2048,864]{1,0:T(8,128)(2,1)} %hold.57, bf16[2048,1152]{1,0:T(8,128)(2,1)} %get-tuple-element.86), kind=kOutput, calls=%fused_computation.26 | convolution fusion | flops 4077858816 | bytes 10248192 | tf_op jit(solution)/shard_map/dot_general | solution.py:167
  450.6 7.0 %reduce-scatter.3.cloned.1.call-done.refs_1_ = bf16[144,1152]{1,0:T(8,128)(2,1)} async-done(((bf16[576,1152]{1,0:T(8,128)(2,1)}), bf16[144,1152]{1,0:T(8,128)(2,1)}) %reduce-scatter.3.cloned.1.call-update) | async-done | bytes 331792 | tf_op jit(solution)/shard_map/reduce_scatter | solution.py:841
  468.7 8.2 %collective-permute-done.38 = f32[2,8,1728]{2,1,0:T(8,128)S(1)} collective-permute-done((f32[2,8,1728]{2,1,0:T(8,128)S(1)}, f32[2,8,1728]{2,1,0:T(8,128)S(1)}, u32[]{:S(2)}, u32[]{:S(2)}) %collective-permute-start.38) | collective-permute-done | bytes 110624 | tf_op jit(solution)/shard_map/ppermute | solution.py:283
  498.9 11.3 %collective-permute-done.48 = bf16[40,1152]{1,0:T(8,128)(2,1)S(1)} collective-permute-done((bf16[40,1152]{1,0:T(8,128)(2,1)S(1)}, bf16[40,1152]{1,0:T(8,128)(2,1)S(1)}, u32[]{:S(2)}, u32[]{:S(2)}) %collective-permute-start.48) | collective-permute-done | bytes 92192 | tf_op jit(solution)/shard_map/ppermute | solution.py:254
  530.1 16.0 %collective-permute-start.55 = (bf16[4,144,1152]{2,1,0:T(8,128)(2,1)}, bf16[4,144,1152]{2,1,0:T(8,128)(2,1)}, u32[]{:S(2)}, u32[]{:S(2)}) collective-permute-start(bf16[4,144,1152]{2,1,0:T(8,128)(2,1)} %pad_maximum_fusion.12), channel_id=1, source_target_pairs={{0,4},{4,0},{8,12},{12,8},{16,20},{20,16},{24,28},{28,24},{1,5},{5... | collective-permute-start | bytes 3981320 | tf_op jit(solution)/shard_map/ppermute | solution.py:279
  559.9 7.4 %place_columns.1 = f32[1152,1152]{1,0:T(8,128)} custom-call(bf16[8,144,1152]{2,1,0:T(8,128)(2,1)} %pad_maximum_fusion.5.slices_ref), custom_call_target="tpu_custom_call" | custom-call | tf_op jit(solution)/shard_map/place_columns/pallas_call | solution.py:215
  579.5 12.9 %reduce-scatter.5.cloned.1.call-done = bf16[1,2048,288]{2,1,0:T(8,128)(2,1)} async-done(((bf16[4,2048,288]{2,1,0:T(8,128)(2,1)}), bf16[1,2048,288]{2,1,0:T(8,128)(2,1)}) %reduce-scatter.5.cloned.1.call-update) | async-done | bytes 1179664 | tf_op jit(solution)/shard_map/reduce_scatter | solution.py:841
  (456 shorter events, 270.5 us)
Async XLA Ops:
  7.2 56.5 %all-gather.3.cloned.1.call-start = ((), (), s32[]{:S(2)}) async-start(), calls=%async_computation.2 | async-start | bytes 1658880 | tf_op jit(solution)/shard_map/all_gather | solution.py:683
  10.2 81.8 %all-gather.5.cloned.1.call-start = ((), (), s32[]{:S(2)}) async-start(), calls=%async_computation.3 | async-start | bytes 1658880 | tf_op jit(solution)/shard_map/all_gather | solution.py:684
  22.0 435.6 %reduce-scatter.3.cloned.1.call-start = ((), (), s32[]{:S(2)}) async-start(), calls=%async_computation.4 | async-start | bytes 1658880 | tf_op jit(solution)/shard_map/reduce_scatter | solution.py:841
  91.9 41.3 %collective-permute-start.13 = (bf16[576,1152]{1,0:T(8,128)(2,1)}, bf16[576,1152]{1,0:T(8,128)(2,1)}, u32[]{:S(2)}, u32[]{:S(2)}) collective-permute-start(bf16[576,1152]{1,0:T(8,128)(2,1)} %hold.33.refs_1_), channel_id=1, source_target_pairs={{0,16},{4,12},{8,24},{12,4},{16,0},{20,28},{24,8},{28,20},{1,17},{... | collective-permute-start | bytes 3981320 | tf_op jit(solution)/shard_map/ppermute | solution.py:283
  98.2 33.4 %collective-permute-start.12 = (bf16[2,256,288]{2,1,0:T(8,128)(2,1)S(1)}, bf16[2,256,288]{2,1,0:T(8,128)(2,1)S(1)}, u32[]{:S(2)}, u32[]{:S(2)}) collective-permute-start(bf16[2,256,288]{2,1,0:T(8,128)(2,1)S(1)} %get-tuple-element.142), channel_id=1, source_target_pairs={{3,0},{0,1},{1,2},{2,3},{7,4},{4,5},{5,6},{6,7},{11,8},{8,9},{9,10... | collective-permute-start | bytes 884744 | tf_op jit(solution)/shard_map/ppermute | solution.py:250
  99.8 45.9 %collective-permute-start.14 = (bf16[1152,1152]{1,0:T(8,128)(2,1)}, bf16[1152,1152]{1,0:T(8,128)(2,1)}, u32[]{:S(2)}, u32[]{:S(2)}) collective-permute-start(bf16[1152,1152]{1,0:T(8,128)(2,1)} %pad_maximum_fusion.3.refs_1_.refs_2_.refs_10_), channel_id=1, source_target_pairs={{0,8},{4,20},{8,0},{12,28},{16,24},{20,4},{24,16},{28,12},{1,9},{5... | collective-permute-start | bytes 7962632 | tf_op jit(solution)/shard_map/ppermute | solution.py:283
  106.9 62.2 %collective-permute-start.15 = (bf16[1152,1152]{1,0:T(8,128)(2,1)}, bf16[1152,1152]{1,0:T(8,128)(2,1)}, u32[]{:S(2)}, u32[]{:S(2)}) collective-permute-start(bf16[1152,1152]{1,0:T(8,128)(2,1)} %pad_maximum_fusion.3.refs_1_.refs_2_.refs_10_), channel_id=1, source_target_pairs={{0,4},{4,0},{8,12},{12,8},{16,20},{20,16},{24,28},{28,24},{1,5},{5... | collective-permute-start | bytes 7962632 | tf_op jit(solution)/shard_map/ppermute | solution.py:279
  136.2 31.5 %collective-permute-start.17 = (bf16[1152,1152]{1,0:T(8,128)(2,1)}, bf16[1152,1152]{1,0:T(8,128)(2,1)}, u32[]{:S(2)}, u32[]{:S(2)}) collective-permute-start(bf16[1152,1152]{1,0:T(8,128)(2,1)} %pad_maximum_fusion.4.refs_7_.refs_6_.refs_14_), channel_id=1, source_target_pairs={{0,8},{4,20},{8,0},{12,28},{16,24},{20,4},{24,16},{28,12},{1,9},{5... | collective-permute-start | bytes 7962632 | tf_op jit(solution)/shard_map/ppermute | solution.py:283
  152.3 36.4 %collective-permute-start.18 = (bf16[1152,1152]{1,0:T(8,128)(2,1)}, bf16[1152,1152]{1,0:T(8,128)(2,1)}, u32[]{:S(2)}, u32[]{:S(2)}) collective-permute-start(bf16[1152,1152]{1,0:T(8,128)(2,1)} %pad_maximum_fusion.4.refs_7_.refs_6_.refs_14_), channel_id=1, source_target_pairs={{0,4},{4,0},{8,12},{12,8},{16,20},{20,16},{24,28},{28,24},{1,5},{5... | collective-permute-start | bytes 7962632 | tf_op jit(solution)/shard_map/ppermute | solution.py:279
  167.7 36.5 %collective-permute-start.19 = (bf16[1152,1152]{1,0:T(8,128)(2,1)}, bf16[1152,1152]{1,0:T(8,128)(2,1)}, u32[]{:S(2)}, u32[]{:S(2)}) collective-permute-start(bf16[1152,1152]{1,0:T(8,128)(2,1)} %collective-permute-done.17.refs_15_), channel_id=1, source_target_pairs={{0,4},{4,0},{8,12},{12,8},{16,20},{20,16},{24,28},{28,24},{1,5},{5... | collective-permute-start | bytes 7962632 | tf_op jit(solution)/shard_map/ppermute | solution.py:279
  203.7 97.6 %collective-permute-start.27 = (bf16[1152,1152]{1,0:T(8,128)(2,1)}, bf16[1152,1152]{1,0:T(8,128)(2,1)}, u32[]{:S(2)}, u32[]{:S(2)}) collective-permute-start(bf16[1152,1152]{1,0:T(8,128)(2,1)} %get-tuple-element.77), channel_id=1, source_target_pairs={{0,4},{4,0},{8,12},{12,8},{16,20},{20,16},{24,28},{28,24},{1,5},{5... | collective-permute-start | bytes 7962632 | tf_op jit(solution)/shard_map/ppermute | solution.py:279
  203.7 52.8 %collective-permute-start.21 = (bf16[1152,1152]{1,0:T(8,128)(2,1)}, bf16[1152,1152]{1,0:T(8,128)(2,1)}, u32[]{:S(2)}, u32[]{:S(2)}) collective-permute-start(bf16[1152,1152]{1,0:T(8,128)(2,1)} %get-tuple-element.71), channel_id=1, source_target_pairs={{0,4},{4,0},{8,12},{12,8},{16,20},{20,16},{24,28},{28,24},{1,5},{5... | collective-permute-start | bytes 7962632 | tf_op jit(solution)/shard_map/ppermute | solution.py:279
  252.8 34.1 %collective-permute-start.22 = (bf16[2,256,288]{2,1,0:T(8,128)(2,1)}, bf16[2,256,288]{2,1,0:T(8,128)(2,1)}, u32[]{:S(2)}, u32[]{:S(2)}) collective-permute-start(bf16[2,256,288]{2,1,0:T(8,128)(2,1)} %get-tuple-element.139), channel_id=1, source_target_pairs={{0,2},{1,3},{2,0},{3,1},{4,6},{5,7},{6,4},{7,5},{8,10},{9,11},{10,... | collective-permute-start | bytes 884744 | tf_op jit(solution)/shard_map/ppermute | solution.py:254
  255.2 34.0 %collective-permute-start.23 = (bf16[2,256,288]{2,1,0:T(8,128)(2,1)}, bf16[2,256,288]{2,1,0:T(8,128)(2,1)}, u32[]{:S(2)}, u32[]{:S(2)}) collective-permute-start(bf16[2,256,288]{2,1,0:T(8,128)(2,1)} %get-tuple-element.138), channel_id=1, source_target_pairs={{0,3},{1,0},{2,1},{3,2},{4,7},{5,4},{6,5},{7,6},{8,11},{9,8},{10,9... | collective-permute-start | bytes 884744 | tf_op jit(solution)/shard_map/ppermute | solution.py:254
  262.2 39.1 %collective-permute-start.28 = (bf16[1152,1152]{1,0:T(8,128)(2,1)}, bf16[1152,1152]{1,0:T(8,128)(2,1)}, u32[]{:S(2)}, u32[]{:S(2)}) collective-permute-start(bf16[1152,1152]{1,0:T(8,128)(2,1)} %add_convert_fusion.5.refs_2_), channel_id=1, source_target_pairs={{0,8},{4,20},{8,0},{12,28},{16,24},{20,4},{24,16},{28,12},{1,9},{5... | collective-permute-start | bytes 7962632 | tf_op jit(solution)/shard_map/ppermute | solution.py:283
  277.4 36.5 %collective-permute-start.26 = (bf16[1152,1152]{1,0:T(8,128)(2,1)}, bf16[1152,1152]{1,0:T(8,128)(2,1)}, u32[]{:S(2)}, u32[]{:S(2)}) collective-permute-start(bf16[1152,1152]{1,0:T(8,128)(2,1)} %get-tuple-element.76), channel_id=1, source_target_pairs={{0,4},{4,0},{8,12},{12,8},{16,20},{20,16},{24,28},{28,24},{1,5},{5... | collective-permute-start | bytes 7962632 | tf_op jit(solution)/shard_map/ppermute | solution.py:279
  319.6 68.2 %collective-permute-start.30 = (bf16[1152,1152]{1,0:T(8,128)(2,1)}, bf16[1152,1152]{1,0:T(8,128)(2,1)}, u32[]{:S(2)}, u32[]{:S(2)}) collective-permute-start(bf16[1152,1152]{1,0:T(8,128)(2,1)} %add_convert_fusion.3.refs_7_), channel_id=1, source_target_pairs={{0,8},{4,20},{8,0},{12,28},{16,24},{20,4},{24,16},{28,12},{1,9},{5... | collective-permute-start | bytes 7962632 | tf_op jit(solution)/shard_map/ppermute | solution.py:283
  378.2 33.1 %collective-permute-start.31 = (bf16[2,256,288]{2,1,0:T(8,128)(2,1)}, bf16[2,256,288]{2,1,0:T(8,128)(2,1)}, u32[]{:S(2)}, u32[]{:S(2)}) collective-permute-start(bf16[2,256,288]{2,1,0:T(8,128)(2,1)} %get-tuple-element.135), channel_id=1, source_target_pairs={{0,2},{1,3},{2,0},{3,1},{4,6},{5,7},{6,4},{7,5},{8,10},{9,11},{10,... | collective-permute-start | bytes 884744 | tf_op jit(solution)/shard_map/ppermute | solution.py:254
  378.2 34.8 %collective-permute-start.32 = (bf16[2,256,288]{2,1,0:T(8,128)(2,1)}, bf16[2,256,288]{2,1,0:T(8,128)(2,1)}, u32[]{:S(2)}, u32[]{:S(2)}) collective-permute-start(bf16[2,256,288]{2,1,0:T(8,128)(2,1)} %get-tuple-element.134), channel_id=1, source_target_pairs={{0,3},{1,0},{2,1},{3,2},{4,7},{5,4},{6,5},{7,6},{8,11},{9,8},{10,9... | collective-permute-start | bytes 884744 | tf_op jit(solution)/shard_map/ppermute | solution.py:254
  385.5 75.5 %collective-permute-start.61 = (bf16[4,144,1152]{2,1,0:T(8,128)(2,1)}, bf16[4,144,1152]{2,1,0:T(8,128)(2,1)}, u32[]{:S(2)}, u32[]{:S(2)}) collective-permute-start(bf16[4,144,1152]{2,1,0:T(8,128)(2,1)} %pad_maximum_fusion.13), channel_id=1, source_target_pairs={{0,4},{4,0},{8,12},{12,8},{16,20},{20,16},{24,28},{28,24},{1,5},{5... | collective-permute-start | bytes 3981320 | tf_op jit(solution)/shard_map/ppermute | solution.py:279
  425.7 166.8 %reduce-scatter.5.cloned.1.call-start = ((), (), s32[]{:S(2)}) async-start(), calls=%async_computation.5 | async-start | bytes 7864320 | tf_op jit(solution)/shard_map/reduce_scatter | solution.py:841
  494.6 57.5 %collective-permute-start.40 = (bf16[72,1152]{1,0:T(8,128)(2,1)S(1)}, bf16[72,1152]{1,0:T(8,128)(2,1)S(1)}, u32[]{:S(2)}, u32[]{:S(2)}) collective-permute-start(bf16[72,1152]{1,0:T(8,128)(2,1)S(1)} %maximum_maximum_fusion.1), channel_id=1, source_target_pairs={{1,0},{2,1},{3,2},{0,3},{5,4},{6,5},{7,6},{4,7},{9,8},{10,9},{11,1... | collective-permute-start | bytes 497672 | tf_op jit(solution)/shard_map/ppermute | solution.py:250
  496.3 55.9 %collective-permute-start.41 = (bf16[72,1152]{1,0:T(8,128)(2,1)S(1)}, bf16[72,1152]{1,0:T(8,128)(2,1)S(1)}, u32[]{:S(2)}, u32[]{:S(2)}) collective-permute-start(bf16[72,1152]{1,0:T(8,128)(2,1)S(1)} %maximum_maximum_fusion.1), channel_id=1, source_target_pairs={{2,0},{3,1},{0,2},{1,3},{6,4},{7,5},{4,6},{5,7},{10,8},{11,9},{8,1... | collective-permute-start | bytes 497672 | tf_op jit(solution)/shard_map/ppermute | solution.py:250
  498.0 54.1 %collective-permute-start.42 = (bf16[72,1152]{1,0:T(8,128)(2,1)S(1)}, bf16[72,1152]{1,0:T(8,128)(2,1)S(1)}, u32[]{:S(2)}, u32[]{:S(2)}) collective-permute-start(bf16[72,1152]{1,0:T(8,128)(2,1)S(1)} %maximum_maximum_fusion.1), channel_id=1, source_target_pairs={{3,0},{0,1},{1,2},{2,3},{7,4},{4,5},{5,6},{6,7},{11,8},{8,9},{9,10... | collective-permute-start | bytes 497672 | tf_op jit(solution)/shard_map/ppermute | solution.py:250
  (107 other events, 1138.0 us)
Sparse Core Ops, SparseCore 0:
  10.3 42.7 all-gather.2
  54.7 34.0 all-gather.4
  425.8 31.8 reduce-scatter.2
  459.8 132.6 reduce-scatter.4

commit v3 on v2

--- a/solution.py
+++ b/solution.py
@@ -53,7 +53,7 @@
             mixed_ref[(group - target + groups) % groups, 0] = outs[spot * home : (spot + 1) * home]
         return 0
 
-    lax.fori_loop(0, seq // chunk, step, 0)
+    lax.fori_loop(0, seq // chunk, step, 0, unroll=True)
 
 
 def attend(projected, row, mixed, heads, chunk, groups, order):
@@ -89,13 +89,14 @@
     for spot in range(groups):
         grad_ref[spot * home : (spot + 1) * home, :] = pieces_ref[(group - spot + groups) % groups, 0]
 
-    def part(head, start):
+    def part(head, start, key_turned=None):
         at = head * width
         rows = pl.ds(start, chunk)
         keys = pl.ds(start if split else 0, key_count)
         queries = proj_ref[0, rows, at : at + HEAD_DIM]
         key_rows = proj_ref[0, keys, at + HEAD_DIM : at + 2 * HEAD_DIM]
         value_rows = proj_ref[0, keys, at + 2 * HEAD_DIM : at + 3 * HEAD_DIM]
+        key_turned = key_rows.T if key_turned is None else key_turned
         grads = grad_ref[rows, head * HEAD_DIM : (head + 1) * HEAD_DIM]
         scores = nt(key_rows, queries)
         probs = jnp.exp2(scores * (KEY_SCALE * LOG2E) - lse_ref[0, head : head + 1, rows])
@@ -104,7 +105,7 @@
         grad_raw = (probs * (grad_probs - inner) * KEY_SCALE).astype(jnp.bfloat16)
         grad_values = nn(probs.astype(jnp.bfloat16), grads)
         grad_keys = nn(grad_raw, queries)
-        grad_queries = nn(key_rows.T, grad_raw).T
+        grad_queries = nn(key_turned, grad_raw).T
         return grad_queries, grad_keys, grad_values
 
     if not split:
@@ -112,16 +113,17 @@
             at = head * width
             dk_ref[...] = jnp.zeros_like(dk_ref)
             dv_ref[...] = jnp.zeros_like(dv_ref)
-
-            def step(index, _):
+            key_turned = proj_ref[0, :, at + HEAD_DIM : at + 2 * HEAD_DIM].T
+
+            def step(index, _, head=head, at=at, key_turned=key_turned):
                 start = pl.multiple_of(index * chunk, chunk)
-                dq, dk, dv = part(head, start)
+                dq, dk, dv = part(head, start, key_turned)
                 out_ref[0, pl.ds(start, chunk), at : at + HEAD_DIM] = dq.astype(jnp.bfloat16)
                 dk_ref[...] += dk
                 dv_ref[...] += dv
                 return 0
 
-            lax.fori_loop(0, seq // chunk, step, 0)
+            lax.fori_loop(0, seq // chunk, step, 0, unroll=True)
             both = jnp.concatenate([dk_ref[...], dv_ref[...]], axis=1).astype(jnp.bfloat16)
             out_ref[0, :, at + HEAD_DIM : at + 3 * HEAD_DIM] = both
     else:
@@ -132,7 +134,7 @@
             out_ref[0, pl.ds(start, chunk), :] = jnp.concatenate(outs, axis=1).astype(jnp.bfloat16)
             return 0
 
-        lax.fori_loop(0, seq // chunk, step, 0)
+        lax.fori_loop(0, seq // chunk, step, 0, unroll=True)
 
 
 def attend_back(projected, row, lse, grads, heads, chunk, groups, order):
@@ -390,13 +392,17 @@
             spot = (head - lax.axis_index("head") + heads) % heads
             table_ref[:, head * columns : (head + 1) * columns] = table_rel_ref[spot]
 
-    row = jnp.where(block < 4, 1 + block % 4, 0)
-    normed, _ = row_norm(tokens_ref[...].astype(jnp.float32))
-    shift = table_ref[pl.ds(row, 1), :width]
-    scale = table_ref[pl.ds(row, 1), width : 2 * width]
-    attn_in = (normed * (1.0 + scale) + shift).astype(jnp.bfloat16)
-    attn_in_ref[...] = attn_in
-    projected_ref[...] = (nt(attn_in, weight_ref[...]) + bias_ref[...]).astype(jnp.bfloat16)
+    quarter_rows = tokens_ref.shape[0] // 2
+    for half in range(2):
+        here = slice(half * quarter_rows, (half + 1) * quarter_rows)
+        spot = 2 * block + half
+        row = jnp.where(spot < 4, 1 + spot % 4, 0)
+        normed, _ = row_norm(tokens_ref[here, :].astype(jnp.float32))
+        shift = table_ref[pl.ds(row, 1), :width]
+        scale = table_ref[pl.ds(row, 1), width : 2 * width]
+        attn_in = (normed * (1.0 + scale) + shift).astype(jnp.bfloat16)
+        attn_in_ref[here, :] = attn_in
+        projected_ref[here, :] = (nt(attn_in, weight_ref[...]) + bias_ref[...]).astype(jnp.bfloat16)
 
 
 def home_row(info_ref, row, home, quarter):
@@ -460,65 +466,112 @@
             slope_ref[...] = (half + 0.5 * pre * (1.0 - bent * bent) * inner).astype(jnp.bfloat16)
 
 
-def contract_kernel(link, quarter, steps, info_ref, table_ref, grad_mlp_ref, hidden_ref, slope_ref, out_bias_ref,
+def contract_kernel(link, quarter, info_ref, table_ref, grad_mlp_ref, out_bias_ref, hidden_ref, slope_ref,
                     tokens_grad_ref, stream_ref, attn_ref, proj_ref, *refs):
     count = 4
     ins, outs = refs[:count], refs[count : 2 * count]
     (grad_pre_ref, pre_sum_ref, block_ref, stream_grad_ref, grad_attn_ref, grad_mixed_ref, sums_ref, attn_sum_ref,
-     mlp_acc, grad_acc) = refs[2 * count :]
-    step = pl.program_id(0)
+     mlp_acc, grad_acc, in_buf, out_buf, hidden_buf, slope_buf, pre_buf, tokens_buf, stream_buf, attn_buf, proj_buf,
+     piece_sems, pre_sems, late_sems) = refs[2 * count :]
     heads = link.heads
     rows, home, width = stream_ref.shape
     share = width // heads
-
-    @pl.when(step == 0)
-    def _():
-        mlp_acc[...] = jnp.zeros_like(mlp_acc)
-        grad_acc[...] = jnp.zeros_like(grad_acc)
-
-    for spot in range(count):
-
-        @pl.when(step // steps == spot)
-        def _(in_ref=ins[spot], out_ref=outs[spot]):
-            grad_pre = (nt(grad_mlp_ref[...], out_ref[...]) * slope_ref[...].astype(jnp.float32)).astype(jnp.bfloat16)
-            grad_pre_ref[...] = grad_pre
-            pre_sum_ref[...] = jnp.sum(grad_pre.astype(jnp.float32), axis=0, keepdims=True)
-            grad_acc[...] += nn(grad_pre, in_ref[...])
-            mlp_acc[...] += nn(hidden_ref[...], out_ref[...])
-
-    @pl.when(step == count * steps - 1)
-    def _():
-        head = lax.axis_index("head")
-        attn_sum = jnp.zeros((1, width), jnp.float32)
-        for row in range(rows):
-            spot = home_row(info_ref, row, home, quarter)
-
-            def mod(group):
-                return table_ref[pl.ds(spot, 1), group * width : (group + 1) * width]
-
-            here = slice(row * home, (row + 1) * home)
-            grad_out = tokens_grad_ref[row_at(row, info_ref)].astype(jnp.float32)
-            stream = stream_ref[row]
-            mlp = mlp_acc[here, :] + out_bias_ref[...]
-            block = (stream + mod(5) * mlp).astype(jnp.bfloat16)
-            for other in range(heads):
-                block_ref[(other - head + heads) % heads, row] = block[:, other * share : (other + 1) * share]
-            normed, inverse = row_norm(stream.astype(jnp.bfloat16).astype(jnp.float32))
-            grad_in = grad_acc[here, :]
-            sums_ref[row, 1:2] = jnp.sum(grad_in, axis=0, keepdims=True)
-            sums_ref[row, 2:3] = jnp.sum(grad_in * normed, axis=0, keepdims=True)
-            sums_ref[row, 3:4] = jnp.sum(grad_out * mlp, axis=0, keepdims=True)
-            stream_grad = grad_out + norm_back(normed, inverse, grad_in * (1.0 + mod(4)))
-            stream_grad_ref[row] = stream_grad
-            rounded = stream_grad.astype(jnp.bfloat16).astype(jnp.float32)
-            sums_ref[row, 0:1] = jnp.sum(rounded * attn_ref[row], axis=0, keepdims=True)
-            grad_attn = (rounded * mod(2)).astype(jnp.bfloat16)
-            grad_attn_ref[row] = grad_attn
-            attn_sum += jnp.sum(grad_attn.astype(jnp.float32), axis=0, keepdims=True)
-            grad_mixed = nt(grad_attn, proj_ref[...]).astype(jnp.bfloat16)
-            for other in range(heads):
-                grad_mixed_ref[(other - head + heads) % heads, row] = grad_mixed[:, other * share : (other + 1) * share]
-        attn_sum_ref[...] = attn_sum
+    units = ins[0].shape[0]
+    tile = UNIT_TILE
+
+    def piece_copies(piece):
+        slot = piece % 2
+        columns = pl.ds(piece * units, units)
+        pairs = (
+            (outs[piece], out_buf.at[slot]),
+            (slope_ref.at[:, columns], slope_buf.at[slot]),
+            (hidden_ref.at[:, columns], hidden_buf.at[slot]),
+            (ins[piece], in_buf.at[slot]),
+        )
+        return [
+            pltpu.make_async_copy(source, target, piece_sems.at[kind, slot])
+            for kind, (source, target) in enumerate(pairs)
+        ]
+
+    def pre_copy(piece):
+        slot = piece % 2
+        return pltpu.make_async_copy(
+            pre_buf.at[slot], grad_pre_ref.at[:, pl.ds(piece * units, units)], pre_sems.at[slot]
+        )
+
+    start = pl.multiple_of(info_ref[1] * home, 8)
+    late = [
+        pltpu.make_async_copy(tokens_grad_ref.at[:, pl.ds(start, home), :], tokens_buf, late_sems.at[0]),
+        pltpu.make_async_copy(stream_ref, stream_buf, late_sems.at[1]),
+        pltpu.make_async_copy(attn_ref, attn_buf, late_sems.at[2]),
+        pltpu.make_async_copy(proj_ref, proj_buf, late_sems.at[3]),
+    ]
+    for piece in range(2):
+        for copy in piece_copies(piece):
+            copy.start()
+    for copy in late:
+        copy.start()
+    for piece in range(count):
+        slot = piece % 2
+        copies = piece_copies(piece)
+        copies[0].wait()
+        copies[1].wait()
+        if piece >= 2:
+            pre_copy(piece - 2).wait()
+        for at in range(0, units, tile):
+            here = slice(at, at + tile)
+            grad_pre = nt(grad_mlp_ref[...], out_buf[slot, here, :]) * slope_buf[slot, :, here].astype(jnp.float32)
+            grad_pre = grad_pre.astype(jnp.bfloat16)
+            pre_buf[slot, :, here] = grad_pre
+            total = jnp.sum(grad_pre.astype(jnp.float32), axis=0, keepdims=True)
+            pre_sum_ref[:, piece * units + at : piece * units + at + tile] = total
+        pre_copy(piece).start()
+        copies[2].wait()
+        copies[3].wait()
+        for at in range(0, width, tile):
+            here = slice(at, at + tile)
+            mlp = nn(hidden_buf[slot], out_buf[slot, :, here])
+            grad = nn(pre_buf[slot], in_buf[slot, :, here])
+            mlp_acc[:, here] = mlp if piece == 0 else mlp_acc[:, here] + mlp
+            grad_acc[:, here] = grad if piece == 0 else grad_acc[:, here] + grad
+        if piece + 2 < count:
+            for copy in piece_copies(piece + 2):
+                copy.start()
+    for copy in late:
+        copy.wait()
+    head = lax.axis_index("head")
+    attn_sum = jnp.zeros((1, width), jnp.float32)
+    for row in range(rows):
+        spot = home_row(info_ref, row, home, quarter)
+
+        def mod(group):
+            return table_ref[pl.ds(spot, 1), group * width : (group + 1) * width]
+
+        here = slice(row * home, (row + 1) * home)
+        grad_out = tokens_buf[row_at(row, info_ref)].astype(jnp.float32)
+        stream = stream_buf[row]
+        mlp = mlp_acc[here, :] + out_bias_ref[...]
+        block = (stream + mod(5) * mlp).astype(jnp.bfloat16)
+        for other in range(heads):
+            block_ref[(other - head + heads) % heads, row] = block[:, other * share : (other + 1) * share]
+        normed, inverse = row_norm(stream.astype(jnp.bfloat16).astype(jnp.float32))
+        grad_in = grad_acc[here, :]
+        sums_ref[row, 1:2] = jnp.sum(grad_in, axis=0, keepdims=True)
+        sums_ref[row, 2:3] = jnp.sum(grad_in * normed, axis=0, keepdims=True)
+        sums_ref[row, 3:4] = jnp.sum(grad_out * mlp, axis=0, keepdims=True)
+        stream_grad = grad_out + norm_back(normed, inverse, grad_in * (1.0 + mod(4)))
+        stream_grad_ref[row] = stream_grad
+        rounded = stream_grad.astype(jnp.bfloat16).astype(jnp.float32)
+        sums_ref[row, 0:1] = jnp.sum(rounded * attn_buf[row], axis=0, keepdims=True)
+        grad_attn = (rounded * mod(2)).astype(jnp.bfloat16)
+        grad_attn_ref[row] = grad_attn
+        attn_sum += jnp.sum(grad_attn.astype(jnp.float32), axis=0, keepdims=True)
+        grad_mixed = nt(grad_attn, proj_buf[...]).astype(jnp.bfloat16)
+        for other in range(heads):
+            grad_mixed_ref[(other - head + heads) % heads, row] = grad_mixed[:, other * share : (other + 1) * share]
+    attn_sum_ref[...] = attn_sum
+    for piece in range(count - 2, count):
+        pre_copy(piece).wait()
 
 
 def row_at(spot, info_ref):
@@ -532,23 +585,28 @@
     width = tokens_ref.shape[1]
     share = width // heads
     home = stream_grad_ref.shape[1]
-    spot = 1 + block if at_row == 0 else 0
-    scale = table_ref[pl.ds(spot, 1), width : 2 * width]
-    grad_in = nn(grad_ref[...], weight_ref[...])
-    normed, inverse = row_norm(tokens_ref[...].astype(jnp.float32))
-    sums_ref[0, 0:1] = jnp.sum(grad_in, axis=0, keepdims=True)
-    sums_ref[0, 1:2] = jnp.sum(grad_in * normed, axis=0, keepdims=True)
-    term_ref[...] = norm_back(normed, inverse, grad_in * (1.0 + scale))
     start = info_ref[1] * home
-
-    @pl.when(start // quarter == block)
+    for half in range(2):
+        here = slice(half * quarter, (half + 1) * quarter)
+        spot = 2 * block + half
+        row = 1 + spot if at_row == 0 else 0
+        scale = table_ref[pl.ds(row, 1), width : 2 * width]
+        grad_in = nn(grad_ref[here, :], weight_ref[...])
+        normed, inverse = row_norm(tokens_ref[here, :].astype(jnp.float32))
+        sums_ref[half, 0:1] = jnp.sum(grad_in, axis=0, keepdims=True)
+        sums_ref[half, 1:2] = jnp.sum(grad_in * normed, axis=0, keepdims=True)
+        term_ref[here, :] = norm_back(normed, inverse, grad_in * (1.0 + scale))
+
+    @pl.when(start // (2 * quarter) == block)
     def _():
-        rows = pl.ds(pl.multiple_of(start % quarter, 8), home)
+        rows = pl.ds(pl.multiple_of(start % (2 * quarter), 8), home)
         term_ref[rows, :] += stream_grad_ref[0]
 
-    low = term_ref[...].astype(jnp.bfloat16)
-    for head in range(heads):
-        shares_ref[head] = low[:, head * share : (head + 1) * share]
+    for half in range(2):
+        here = slice(half * quarter, (half + 1) * quarter)
+        low = term_ref[here, :].astype(jnp.bfloat16)
+        for head in range(heads):
+            shares_ref[head, here, :] = low[:, head * share : (head + 1) * share]
 
 
 def unit_grads_kernel(steps, left_ref, right_ref, *outs):
@@ -683,7 +741,7 @@
     in_gathered = lax.all_gather(in_slice, "head", axis=0, tiled=True)
     out_gathered = lax.all_gather(out_slice, "head", axis=0, tiled=True)
     def tokens_block(i, info_ref):
-        return (4 * row_at(i // 4, info_ref) + i % 4, 0)
+        return (2 * row_at(i // 2, info_ref) + i % 2, 0)
 
     bias_pairs = qv_bias.astype(full).reshape(heads_here, 2, HEAD_DIM)
     full_bias = jnp.concatenate(
@@ -698,16 +756,16 @@
         ],
         [
             whole((heads, 8, ada_here)),
-            pl.BlockSpec((quarter, width), tokens_block),
+            pl.BlockSpec((2 * quarter, width), tokens_block),
             whole((qkv_here, width)),
             whole((1, qkv_here)),
         ],
         [
-            pl.BlockSpec((quarter, width), lambda i, _: (i, 0)),
-            pl.BlockSpec((quarter, qkv_here), lambda i, _: (i, 0)),
+            pl.BlockSpec((2 * quarter, width), lambda i, _: (i, 0)),
+            pl.BlockSpec((2 * quarter, qkv_here), lambda i, _: (i, 0)),
             whole((8, 6 * width)),
         ],
-        grid=(4 * rows,),
+        grid=(2 * rows,),
         prefetch=1,
         name="project", micros=13,
     )(info, table_rel, tokens, qkv_t, full_bias)
@@ -783,11 +841,12 @@
     tile_spec = pl.BlockSpec((home_count, UNIT_TILE), lambda i, *_: (0, i))
     bias_spec = pl.BlockSpec((1, UNIT_TILE), lambda i, *_: (0, i))
     hidden, slope = call(
-        functools.partial(expand_kernel, steps),
+        functools.partial(expand_kernel, 1),
         [shape_of((home_count, unit_count), low)] * 2,
-        [whole((home_count, width)), bias_spec] + [piece_spec(spot) for spot in range(4)],
-        [tile_spec, tile_spec],
-        grid=(4 * steps,),
+        [whole((home_count, width)), pl.BlockSpec((1, piece_rows), lambda i: (0, i))]
+        + [whole((piece_rows, width))] * 4,
+        [pl.BlockSpec((home_count, piece_rows), lambda i: (0, i))] * 2,
+        grid=(4,),
         name="expand", micros=20,
         order=[out_held[0]],
     )(mlp_in, in_bias_all, *in_pieces)
@@ -797,7 +856,7 @@
     stay = pl.BlockSpec((rows, home, width), lambda *_: (0, 0, 0))
     by_head = whole((heads, rows, home, share))
     grad_pre, pre_sum, block_home, stream_grad, grad_attn, grad_mixed, home_sums, attn_sum = call(
-        functools.partial(contract_kernel, link, quarter, steps),
+        functools.partial(contract_kernel, link, quarter),
         [
             shape_of((home_count, unit_count), low),
             shape_of((1, unit_count), full),
@@ -808,25 +867,37 @@
             shape_of((rows, 4, width), full),
             shape_of((1, width), full),
         ],
+        [SCALARS, whole((8, 6 * width)), whole((home_count, width)), whole((1, width))]
+        + [pl.BlockSpec(memory_space=pl.ANY)] * 14,
         [
-            whole((8, 6 * width)),
-            whole((home_count, width)),
-            tile_spec,
-            tile_spec,
-            whole((1, width)),
-            pl.BlockSpec((rows, home, width), lambda i, info_ref: (0, info_ref[1], 0)),
+            pl.BlockSpec(memory_space=pl.ANY),
+            whole((1, unit_count)),
+            by_head,
             stay,
             stay,
-            whole((width, width)),
-        ]
-        + [piece_spec(spot) for spot in range(4)] * 2,
-        [tile_spec, bias_spec, by_head, stay, stay, by_head, whole((rows, 4, width)), whole((1, width))],
-        grid=(4 * steps,),
-        prefetch=1,
-        scratch=[pltpu.VMEM((home_count, width), full)] * 2,
+            by_head,
+            whole((rows, 4, width)),
+            whole((1, width)),
+        ],
+        scratch=[
+            pltpu.VMEM((home_count, width), full),
+            pltpu.VMEM((home_count, width), full),
+            pltpu.VMEM((2, piece_rows, width), low),
+            pltpu.VMEM((2, piece_rows, width), low),
+            pltpu.VMEM((2, home_count, piece_rows), low),
+            pltpu.VMEM((2, home_count, piece_rows), low),
+            pltpu.VMEM((2, home_count, piece_rows), low),
+            pltpu.VMEM((rows, home, width), low),
+            pltpu.VMEM((rows, home, width), full),
+            pltpu.VMEM((rows, home, width), full),
+            pltpu.VMEM((width, width), low),
+            pltpu.SemaphoreType.DMA((4, 2)),
+            pltpu.SemaphoreType.DMA((2,)),
+            pltpu.SemaphoreType.DMA((4,)),
+        ],
         name="contract", micros=44,
         order=[out_parts[0]],
-    )(info, table, grad_mlp, hidden, slope, out_bias.astype(full)[None], grad_rows, stream, attn, proj_true,
+    )(info, table, grad_mlp, out_bias.astype(full)[None], hidden, slope, grad_rows, stream, attn, proj_true,
       *in_pieces, *out_pieces)
     mixed_sends = [link.send(grad_mixed[j], j) for j in range(1, heads)]
     out_near = link.reduce_cores(out_parts, grad_pre)
@@ -865,19 +936,19 @@
             [shape_of((heads, token_count, share), low), shape_of((4, 2, width), full)],
             [
                 whole((8, 6 * width)),
-                pl.BlockSpec((quarter, qkv_here), lambda i, _: (i, 0)),
+                pl.BlockSpec((2 * quarter, qkv_here), lambda i, _: (i, 0)),
                 whole((qkv_here, width)),
-                pl.BlockSpec((quarter, width), lambda i, info_ref, row=row: tokens_block(i + 4 * row, info_ref)),
+                pl.BlockSpec((2 * quarter, width), lambda i, info_ref, row=row: tokens_block(i + 2 * row, info_ref)),
                 pl.BlockSpec((1, home, width), lambda i, _, row=row: (row, 0, 0)),
             ]
             + [pl.BlockSpec(memory_space=pl.ANY)] * len(earlier),
             [
-                pl.BlockSpec((heads, quarter, share), lambda i, _, row=row: (0, i + 4 * row, 0)),
-                pl.BlockSpec((1, 2, width), lambda i, _: (i, 0, 0)),
+                pl.BlockSpec((heads, 2 * quarter, share), lambda i, _, row=row: (0, i + 2 * row, 0)),
+                pl.BlockSpec((2, 2, width), lambda i, _: (i, 0, 0)),
             ],
-            grid=(4,),
+            grid=(2,),
             prefetch=1,
-            scratch=[pltpu.VMEM((quarter, width), full)],
+            scratch=[pltpu.VMEM((2 * quarter, width), full)],
             name="leave", micros=9,
             aliases={6: 0} if earlier else {},
             order=order,

time: 615 us -> 599 us (0.974)
  Pallas kernels: 218 us -> 199 us
    pallas_call x18, Pallas kernels: 218 us -> 199 us  [call(): return lambda *arrays: run(*arrays, *order)]
  transfers between devices with their start and end apart: 66 -> 66, of which waited for: 25 -> 25; matrix products, arithmetic and copies ran while one was open for 23% -> 24% of each run, Pallas kernels for 36% -> 34%
where the time goes in v3:
time: 599 us; the launch traced here: 593 us
  Pallas kernels  199 us (33%)
  waiting for transfers between devices  114 us (19%)
  starting transfers between devices  106 us (18%)
  other arithmetic  84.9 us (14%)
  local copies, waits for them, and re-layouts  51.9 us (9%)
  matrix products  21.3 us (4%)
  between operations  15.4 us (3%)
    pallas_call x18, Pallas kernels, call(): return lambda *arrays: run(*arrays, *order)  199 us
    ppermute x15, starting transfers between devices, core_swap(): lax.ppermute(values, 'batch', [(i, i ^ 1) for i in range(self.batches)])  57 us
    ppermute x15, waiting for transfers between devices, send(): lax.ppermute(values, 'head', [(i, (i + distance) % count) for i in range(...  38.4 us
    ppermute x20, waiting for transfers between devices, link_swap(): return lax.ppermute(values, 'batch', pairs)  33.8 us
    ppermute x12, waiting for transfers between devices, fetch(): lax.ppermute(values, 'head', [((i + distance) % count, i) for i in range(...  22.2 us
    reduce_scatter x2, waiting for transfers between devices, head_sum(): return lax.psum_scatter(values, 'head', scatter_dimension=0, tiled=True)  19 us
    ppermute x20, starting transfers between devices, link_swap(): return lax.ppermute(values, 'batch', pairs)  17.8 us
    ppermute x15, starting transfers between devices, send(): lax.ppermute(values, 'head', [(i, (i + distance) % count) for i in range(...  17.6 us
  transfers between devices with their start and end apart: 66, of which 25 were waited for; matrix products, arithmetic and copies ran while one was open for 24% of the time, Pallas kernels for 34%

profile of v3, /device:TPU:9, one launch (start us, length us, event | category | flops | bytes accessed | tf_op | source)
XLA Modules:
  0.0 593.1 jit_solution(117428139115835895)
XLA Ops:
  30.8 11.6 %project.1 = (bf16[2048,1152]{1,0:T(8,128)(2,1)}, bf16[2048,864]{1,0:T(8,128)(2,1)}, f32[8,6912]{1,0:T(8,128)}) custom-call(s32[8]{0:T(128)} %get-tuple-element.51.info_ref.refs_0_, f32[4,8,1728]{2,1,0:T(8,128)} %pad_maximum_fusion.24.table_rel_ref.refs_1_, bf16[2048,1152]{1,0:T(8,128)(2,1)} %refs_4_.3, bf16[864,1152]{1,0:T(8,128)(2,1)} %bitcast.237, ...), custom_call_target="tpu_custom_call" | custom-call | flops 285999988736 | bytes 858000000 | tf_op jit(solution)/shard_map/project/pallas_call | solution.py:217
  51.4 7.4 %attend_split.1 = (bf16[4,2,256,288]{3,2,1,0:T(8,128)(2,1)}, f32[1,4,1024]{2,1,0:T(4,128)}) custom-call(bf16[2,1024,864]{2,1,0:T(8,128)(2,1)} %bitcast.187), custom_call_target="tpu_custom_call" | custom-call | flops 131999997952 | bytes 396000000 | tf_op jit(solution)/shard_map/attend_split/pallas_call | solution.py:217
  63.0 14.7 %attend_whole.1 = (bf16[4,2,256,288]{3,2,1,0:T(8,128)(2,1)}, f32[1,4,1024]{2,1,0:T(4,128)}) custom-call(bf16[2,1024,864]{2,1,0:T(8,128)(2,1)} %bitcast.188, bf16[4,2,256,288]{3,2,1,0:T(8,128)(2,1)} %get-tuple-element.55.refs_1_, bf16[576,1152]{1,0:T(8,128)(2,1)} %hold.31.refs_2_), custom_call_target="tpu_custom_call", output_to_operand_aliasing={{0}: (1, {})} | custom-call | flops 352000016384 | bytes 1056000000 | tf_op jit(solution)/shard_map/attend_whole/pallas_call | solution.py:217
  100.0 6.5 %collective-permute-done.10 = bf16[2,256,288]{2,1,0:T(8,128)(2,1)S(1)} collective-permute-done((bf16[2,256,288]{2,1,0:T(8,128)(2,1)S(1)}, bf16[2,256,288]{2,1,0:T(8,128)(2,1)S(1)}, u32[]{:S(2)}, u32[]{:S(2)}) %collective-permute-start.10) | collective-permute-done | bytes 294944 | tf_op jit(solution)/shard_map/ppermute | solution.py:252
  106.4 18.6 %collective-permute-start.15 = (bf16[1152,1152]{1,0:T(8,128)(2,1)}, bf16[1152,1152]{1,0:T(8,128)(2,1)}, u32[]{:S(2)}, u32[]{:S(2)}) collective-permute-start(bf16[1152,1152]{1,0:T(8,128)(2,1)} %pad_maximum_fusion.3.refs_1_.refs_2_.refs_10_), channel_id=1, source_target_pairs={{0,4},{4,0},{8,12},{12,8},{16,20},{20,16},{24,28},{28,24},{1,5},{5... | collective-permute-start | bytes 7962632 | tf_op jit(solution)/shard_map/ppermute | solution.py:281
  136.6 9.0 %enter.1 = (f32[2,256,1152]{2,1,0:T(8,128)}, f32[2,256,1152]{2,1,0:T(8,128)}, bf16[2,256,1152]{2,1,0:T(8,128)(2,1)}, bf16[2,256,1152]{2,1,0:T(8,128)(2,1)}, bf16...) custom-call(s32[8]{0:T(128)} %get-tuple-element.51.info_ref.refs_0_, ...), custom_call_target="tpu_custom_call" | custom-call | flops 198000001024 | bytes 594000000 | tf_op jit(solution)/shard_map/enter/pallas_call | solution.py:217
  152.9 14.0 %collective-permute-done.17.refs_15_ = bf16[1152,1152]{1,0:T(8,128)(2,1)} collective-permute-done((bf16[1152,1152]{1,0:T(8,128)(2,1)}, bf16[1152,1152]{1,0:T(8,128)(2,1)}, u32[]{:S(2)}, u32[]{:S(2)}) %collective-permute-start.17) | collective-permute-done | bytes 2654240 | tf_op jit(solution)/shard_map/ppermute | solution.py:285
  168.2 16.8 %expand.1 = (bf16[512,4608]{1,0:T(8,128)(2,1)}, bf16[512,4608]{1,0:T(8,128)(2,1)}) custom-call(bf16[512,1152]{1,0:T(8,128)(2,1)} %bitcast.214, f32[1,4608]{1,0:T(1,128)} %reshape.232.refs_1_, bf16[1152,1152]{1,0:T(8,128)(2,1)} %pad_maximum_fusion.3.refs_1_.refs_2_.refs_10_, bf16[1152,1152]{1,0:T(8,128)(2,1)} %hold.41.refs_3_.refs_11_, ...), custom_call_target="tpu_custom_call" | custom-call | flops 439999987712 | bytes 1320000000 | tf_op jit(solution)/shard_map/expand/pallas_call | solution.py:217
  185.0 15.1 %unit_grads.2 = (bf16[1152,1152]{1,0:T(8,128)(2,1)}, bf16[1152,1152]{1,0:T(8,128)(2,1)}, bf16[1152,1152]{1,0:T(8,128)(2,1)}, bf16[1152,1152]{1,0:T(8,128)(2,1)}) custom-call(bf16[512,4608]{1,0:T(8,128)(2,1)} %get-tuple-element.61.refs_0_.refs_4_, bf16[512,1152]{1,0:T(8,128)(2,1)} %bitcast.240, bf16[1152,1152]{1,0:T(8,128)(2,1)} %collective-permute-done.18.refs_2_.refs_16_), custom_call_target="tpu_custom_call" | custom-call | flops 307999997952 | bytes 924000000 | tf_op jit(solution)/shard_map/unit_grads/pallas_call | solution.py:217
  200.7 36.0 %contract.1 = (bf16[512,4608]{1,0:T(8,128)(2,1)}, f32[1,4608]{1,0:T(1,128)}, bf16[4,2,256,288]{3,2,1,0:T(8,128)(2,1)}, f32[2,256,1152]{2,1,0:T(8,128)}, bf16[2,2...) custom-call(s32[8]{0:T(128)} %get-tuple-element.51.info_ref.refs_0_, ...), custom_call_target="tpu_custom_call" | custom-call | flops 968000012288 | bytes 2904000000 | tf_op jit(solution)/shard_map/contract/pallas_call | solution.py:217
  251.0 15.1 %unit_grads.3 = (bf16[1152,1152]{1,0:T(8,128)(2,1)}, bf16[1152,1152]{1,0:T(8,128)(2,1)}, bf16[1152,1152]{1,0:T(8,128)(2,1)}, bf16[1152,1152]{1,0:T(8,128)(2,1)}) custom-call(bf16[512,4608]{1,0:T(8,128)(2,1)} %get-tuple-element.69.refs_1_.refs_0_, bf16[512,1152]{1,0:T(8,128)(2,1)} %bitcast.215, bf16[1152,1152]{1,0:T(8,128)(2,1)} %add_convert_fusion.5.refs_2_), custom_call_target="tpu_custom_call" | custom-call | flops 307999997952 | bytes 924000000 | tf_op jit(solution)/shard_map/unit_grads/pallas_call | solution.py:217
  268.3 7.2 %collective-permute-done.22.refs_0_ = bf16[2,256,288]{2,1,0:T(8,128)(2,1)} collective-permute-done((bf16[2,256,288]{2,1,0:T(8,128)(2,1)}, bf16[2,256,288]{2,1,0:T(8,128)(2,1)}, u32[]{:S(2)}, u32[]{:S(2)}) %collective-permute-start.22) | collective-permute-done | bytes 294944 | tf_op jit(solution)/shard_map/ppermute | solution.py:256
  280.5 8.1 %attend_back_split.1 = bf16[1,1024,864]{2,1,0:T(8,128)(2,1)} custom-call(bf16[2,1024,864]{2,1,0:T(8,128)(2,1)} %bitcast.189, f32[1,4,1024]{2,1,0:T(4,128)} %get-tuple-element.56.refs_1_.lse_ref, bf16[4,2,256,288]{3,2,1,0:T(8,128)(2,1)} %pad_maximum_fusion.8.refs_1_.pieces_ref.refs_2_), custom_call_target="tpu_custom_call" | custom-call | flops 176000008192 | bytes 528000000 | tf_op jit(solution)/shard_map/attend_back_split/pallas_call | solution.py:217
  307.8 10.1 %leave.2 = (bf16[4,2048,288]{2,1,0:T(8,128)(2,1)}, f32[4,2,1152]{2,1,0:T(2,128)}) custom-call(s32[8]{0:T(128)} %get-tuple-element.51.info_ref.refs_0_, f32[8,6912]{1,0:T(8,128)} %get-tuple-element.53.refs_1_, bf16[1024,864]{1,0:T(8,128)(2,1)} %bitcast.207, bf16[864,1152]{1,0:T(8,128)(2,1)} %bitcast.238, bf16[2048,1152]{1,0:T(8,128)(2,1)} %refs_4_.3, ...), custom_call_target="tpu_custom_call" | custom-call | flops 198000001024 | bytes 594000000 | tf_op jit(solution)/shard_map/leave/pallas_call | solution.py:217
  325.6 17.9 %attend_back_whole.1 = bf16[1,1024,864]{2,1,0:T(8,128)(2,1)} custom-call(bf16[2,1024,864]{2,1,0:T(8,128)(2,1)} %bitcast.190, f32[1,4,1024]{2,1,0:T(4,128)} %get-tuple-element.58.refs_1_, bf16[4,2,256,288]{3,2,1,0:T(8,128)(2,1)} %pad_maximum_fusion.8.refs_1_.pieces_ref.refs_2_, f32[4,2,1152]{2,1,0:T(2,128)} %get-tuple-element.78.refs_3_, ...), custom_call_target="tpu_custom_call" | custom-call | flops 527999991808 | bytes 1584000000 | tf_op jit(solution)/shard_map/attend_back_whole/pallas_call | solution.py:217
  379.2 10.1 %leave.3 = (bf16[4,2048,288]{2,1,0:T(8,128)(2,1)}, f32[4,2,1152]{2,1,0:T(2,128)}) custom-call(s32[8]{0:T(128)} %get-tuple-element.51.info_ref.refs_0_, f32[8,6912]{1,0:T(8,128)} %get-tuple-element.53.refs_1_, bf16[1024,864]{1,0:T(8,128)(2,1)} %bitcast.182, bf16[864,1152]{1,0:T(8,128)(2,1)} %bitcast.239, ...), custom_call_target="tpu_custom_call", output_to_operand_aliasing={{0}: (6, {})} | custom-call | flops 198000001024 | bytes 594000000 | tf_op jit(solution)/shard_map/leave/pallas_call | solution.py:217
  391.6 7.2 %collective-permute-done.31.refs_0_ = bf16[2,256,288]{2,1,0:T(8,128)(2,1)} collective-permute-done((bf16[2,256,288]{2,1,0:T(8,128)(2,1)}, bf16[2,256,288]{2,1,0:T(8,128)(2,1)}, u32[]{:S(2)}, u32[]{:S(2)}) %collective-permute-start.31) | collective-permute-done | bytes 294944 | tf_op jit(solution)/shard_map/ppermute | solution.py:256
  417.8 9.9 %convolution_convert_fusion = bf16[864,1152]{1,0:T(8,128)(2,1)} fusion(bf16[2048,864]{1,0:T(8,128)(2,1)} %hold.57, bf16[2048,1152]{1,0:T(8,128)(2,1)} %get-tuple-element.86), kind=kOutput, calls=%fused_computation.26 | convolution fusion | flops 4077858816 | bytes 10248192 | tf_op jit(solution)/shard_map/dot_general | solution.py:169
  438.6 6.8 %reduce-scatter.3.cloned.1.call-done.refs_1_ = bf16[144,1152]{1,0:T(8,128)(2,1)} async-done(((bf16[576,1152]{1,0:T(8,128)(2,1)}), bf16[144,1152]{1,0:T(8,128)(2,1)}) %reduce-scatter.3.cloned.1.call-update) | async-done | bytes 331792 | tf_op jit(solution)/shard_map/reduce_scatter | solution.py:912
  456.2 8.5 %collective-permute-done.38 = f32[2,8,1728]{2,1,0:T(8,128)S(1)} collective-permute-done((f32[2,8,1728]{2,1,0:T(8,128)S(1)}, f32[2,8,1728]{2,1,0:T(8,128)S(1)}, u32[]{:S(2)}, u32[]{:S(2)}) %collective-permute-start.38) | collective-permute-done | bytes 110624 | tf_op jit(solution)/shard_map/ppermute | solution.py:285
  487.7 10.8 %collective-permute-done.48 = bf16[40,1152]{1,0:T(8,128)(2,1)S(1)} collective-permute-done((bf16[40,1152]{1,0:T(8,128)(2,1)S(1)}, bf16[40,1152]{1,0:T(8,128)(2,1)S(1)}, u32[]{:S(2)}, u32[]{:S(2)}) %collective-permute-start.48) | collective-permute-done | bytes 92192 | tf_op jit(solution)/shard_map/ppermute | solution.py:256
  517.9 16.2 %collective-permute-start.55 = (bf16[4,144,1152]{2,1,0:T(8,128)(2,1)}, bf16[4,144,1152]{2,1,0:T(8,128)(2,1)}, u32[]{:S(2)}, u32[]{:S(2)}) collective-permute-start(bf16[4,144,1152]{2,1,0:T(8,128)(2,1)} %pad_maximum_fusion.12), channel_id=1, source_target_pairs={{0,4},{4,0},{8,12},{12,8},{16,20},{20,16},{24,28},{28,24},{1,5},{5... | collective-permute-start | bytes 3981320 | tf_op jit(solution)/shard_map/ppermute | solution.py:281
  548.5 7.4 %place_columns.1 = f32[1152,1152]{1,0:T(8,128)} custom-call(bf16[8,144,1152]{2,1,0:T(8,128)(2,1)} %pad_maximum_fusion.5.slices_ref), custom_call_target="tpu_custom_call" | custom-call | tf_op jit(solution)/shard_map/place_columns/pallas_call | solution.py:217
  568.2 12.2 %reduce-scatter.5.cloned.1.call-done = bf16[1,2048,288]{2,1,0:T(8,128)(2,1)} async-done(((bf16[4,2048,288]{2,1,0:T(8,128)(2,1)}), bf16[1,2048,288]{2,1,0:T(8,128)(2,1)}) %reduce-scatter.5.cloned.1.call-update) | async-done | bytes 1179664 | tf_op jit(solution)/shard_map/reduce_scatter | solution.py:912
  (456 shorter events, 280.3 us)
Async XLA Ops:
  7.2 55.6 %all-gather.3.cloned.1.call-start = ((), (), s32[]{:S(2)}) async-start(), calls=%async_computation.2 | async-start | bytes 1658880 | tf_op jit(solution)/shard_map/all_gather | solution.py:741
  10.2 80.5 %all-gather.5.cloned.1.call-start = ((), (), s32[]{:S(2)}) async-start(), calls=%async_computation.3 | async-start | bytes 1658880 | tf_op jit(solution)/shard_map/all_gather | solution.py:742
  22.0 423.4 %reduce-scatter.3.cloned.1.call-start = ((), (), s32[]{:S(2)}) async-start(), calls=%async_computation.4 | async-start | bytes 1658880 | tf_op jit(solution)/shard_map/reduce_scatter | solution.py:912
  90.7 41.7 %collective-permute-start.13 = (bf16[576,1152]{1,0:T(8,128)(2,1)}, bf16[576,1152]{1,0:T(8,128)(2,1)}, u32[]{:S(2)}, u32[]{:S(2)}) collective-permute-start(bf16[576,1152]{1,0:T(8,128)(2,1)} %hold.33.refs_1_), channel_id=1, source_target_pairs={{0,16},{4,12},{8,24},{12,4},{16,0},{20,28},{24,8},{28,20},{1,17},{... | collective-permute-start | bytes 3981320 | tf_op jit(solution)/shard_map/ppermute | solution.py:285
  97.1 33.7 %collective-permute-start.12 = (bf16[2,256,288]{2,1,0:T(8,128)(2,1)S(1)}, bf16[2,256,288]{2,1,0:T(8,128)(2,1)S(1)}, u32[]{:S(2)}, u32[]{:S(2)}) collective-permute-start(bf16[2,256,288]{2,1,0:T(8,128)(2,1)S(1)} %get-tuple-element.142), channel_id=1, source_target_pairs={{3,0},{0,1},{1,2},{2,3},{7,4},{4,5},{5,6},{6,7},{11,8},{8,9},{9,10... | collective-permute-start | bytes 884744 | tf_op jit(solution)/shard_map/ppermute | solution.py:252
  98.8 46.9 %collective-permute-start.14 = (bf16[1152,1152]{1,0:T(8,128)(2,1)}, bf16[1152,1152]{1,0:T(8,128)(2,1)}, u32[]{:S(2)}, u32[]{:S(2)}) collective-permute-start(bf16[1152,1152]{1,0:T(8,128)(2,1)} %pad_maximum_fusion.3.refs_1_.refs_2_.refs_10_), channel_id=1, source_target_pairs={{0,8},{4,20},{8,0},{12,28},{16,24},{20,4},{24,16},{28,12},{1,9},{5... | collective-permute-start | bytes 7962632 | tf_op jit(solution)/shard_map/ppermute | solution.py:285
  106.4 61.8 %collective-permute-start.15 = (bf16[1152,1152]{1,0:T(8,128)(2,1)}, bf16[1152,1152]{1,0:T(8,128)(2,1)}, u32[]{:S(2)}, u32[]{:S(2)}) collective-permute-start(bf16[1152,1152]{1,0:T(8,128)(2,1)} %pad_maximum_fusion.3.refs_1_.refs_2_.refs_10_), channel_id=1, source_target_pairs={{0,4},{4,0},{8,12},{12,8},{16,20},{20,16},{24,28},{28,24},{1,5},{5... | collective-permute-start | bytes 7962632 | tf_op jit(solution)/shard_map/ppermute | solution.py:281
  135.4 31.5 %collective-permute-start.17 = (bf16[1152,1152]{1,0:T(8,128)(2,1)}, bf16[1152,1152]{1,0:T(8,128)(2,1)}, u32[]{:S(2)}, u32[]{:S(2)}) collective-permute-start(bf16[1152,1152]{1,0:T(8,128)(2,1)} %pad_maximum_fusion.4.refs_7_.refs_6_.refs_14_), channel_id=1, source_target_pairs={{0,8},{4,20},{8,0},{12,28},{16,24},{20,4},{24,16},{28,12},{1,9},{5... | collective-permute-start | bytes 7962632 | tf_op jit(solution)/shard_map/ppermute | solution.py:285
  152.2 32.8 %collective-permute-start.18 = (bf16[1152,1152]{1,0:T(8,128)(2,1)}, bf16[1152,1152]{1,0:T(8,128)(2,1)}, u32[]{:S(2)}, u32[]{:S(2)}) collective-permute-start(bf16[1152,1152]{1,0:T(8,128)(2,1)} %pad_maximum_fusion.4.refs_7_.refs_6_.refs_14_), channel_id=1, source_target_pairs={{0,4},{4,0},{8,12},{12,8},{16,20},{20,16},{24,28},{28,24},{1,5},{5... | collective-permute-start | bytes 7962632 | tf_op jit(solution)/shard_map/ppermute | solution.py:281
  166.9 33.8 %collective-permute-start.19 = (bf16[1152,1152]{1,0:T(8,128)(2,1)}, bf16[1152,1152]{1,0:T(8,128)(2,1)}, u32[]{:S(2)}, u32[]{:S(2)}) collective-permute-start(bf16[1152,1152]{1,0:T(8,128)(2,1)} %collective-permute-done.17.refs_15_), channel_id=1, source_target_pairs={{0,4},{4,0},{8,12},{12,8},{16,20},{20,16},{24,28},{28,24},{1,5},{5... | collective-permute-start | bytes 7962632 | tf_op jit(solution)/shard_map/ppermute | solution.py:281
  200.1 88.5 %collective-permute-start.27 = (bf16[1152,1152]{1,0:T(8,128)(2,1)}, bf16[1152,1152]{1,0:T(8,128)(2,1)}, u32[]{:S(2)}, u32[]{:S(2)}) collective-permute-start(bf16[1152,1152]{1,0:T(8,128)(2,1)} %get-tuple-element.77), channel_id=1, source_target_pairs={{0,4},{4,0},{8,12},{12,8},{16,20},{20,16},{24,28},{28,24},{1,5},{5... | collective-permute-start | bytes 7962632 | tf_op jit(solution)/shard_map/ppermute | solution.py:281
  200.2 45.0 %collective-permute-start.21 = (bf16[1152,1152]{1,0:T(8,128)(2,1)}, bf16[1152,1152]{1,0:T(8,128)(2,1)}, u32[]{:S(2)}, u32[]{:S(2)}) collective-permute-start(bf16[1152,1152]{1,0:T(8,128)(2,1)} %get-tuple-element.71), channel_id=1, source_target_pairs={{0,4},{4,0},{8,12},{12,8},{16,20},{20,16},{24,28},{28,24},{1,5},{5... | collective-permute-start | bytes 7962632 | tf_op jit(solution)/shard_map/ppermute | solution.py:281
  241.5 34.1 %collective-permute-start.22 = (bf16[2,256,288]{2,1,0:T(8,128)(2,1)}, bf16[2,256,288]{2,1,0:T(8,128)(2,1)}, u32[]{:S(2)}, u32[]{:S(2)}) collective-permute-start(bf16[2,256,288]{2,1,0:T(8,128)(2,1)} %get-tuple-element.139), channel_id=1, source_target_pairs={{0,2},{1,3},{2,0},{3,1},{4,6},{5,7},{6,4},{7,5},{8,10},{9,11},{10,... | collective-permute-start | bytes 884744 | tf_op jit(solution)/shard_map/ppermute | solution.py:256
  243.8 33.9 %collective-permute-start.23 = (bf16[2,256,288]{2,1,0:T(8,128)(2,1)}, bf16[2,256,288]{2,1,0:T(8,128)(2,1)}, u32[]{:S(2)}, u32[]{:S(2)}) collective-permute-start(bf16[2,256,288]{2,1,0:T(8,128)(2,1)} %get-tuple-element.138), channel_id=1, source_target_pairs={{0,3},{1,0},{2,1},{3,2},{4,7},{5,4},{6,5},{7,6},{8,11},{9,8},{10,9... | collective-permute-start | bytes 884744 | tf_op jit(solution)/shard_map/ppermute | solution.py:256
  250.8 37.8 %collective-permute-start.28 = (bf16[1152,1152]{1,0:T(8,128)(2,1)}, bf16[1152,1152]{1,0:T(8,128)(2,1)}, u32[]{:S(2)}, u32[]{:S(2)}) collective-permute-start(bf16[1152,1152]{1,0:T(8,128)(2,1)} %add_convert_fusion.5.refs_2_), channel_id=1, source_target_pairs={{0,8},{4,20},{8,0},{12,28},{16,24},{20,4},{24,16},{28,12},{1,9},{5... | collective-permute-start | bytes 7962632 | tf_op jit(solution)/shard_map/ppermute | solution.py:285
  266.1 35.1 %collective-permute-start.26 = (bf16[1152,1152]{1,0:T(8,128)(2,1)}, bf16[1152,1152]{1,0:T(8,128)(2,1)}, u32[]{:S(2)}, u32[]{:S(2)}) collective-permute-start(bf16[1152,1152]{1,0:T(8,128)(2,1)} %get-tuple-element.76), channel_id=1, source_target_pairs={{0,4},{4,0},{8,12},{12,8},{16,20},{20,16},{24,28},{28,24},{1,5},{5... | collective-permute-start | bytes 7962632 | tf_op jit(solution)/shard_map/ppermute | solution.py:281
  307.0 68.3 %collective-permute-start.30 = (bf16[1152,1152]{1,0:T(8,128)(2,1)}, bf16[1152,1152]{1,0:T(8,128)(2,1)}, u32[]{:S(2)}, u32[]{:S(2)}) collective-permute-start(bf16[1152,1152]{1,0:T(8,128)(2,1)} %add_convert_fusion.3.refs_7_), channel_id=1, source_target_pairs={{0,8},{4,20},{8,0},{12,28},{16,24},{20,4},{24,16},{28,12},{1,9},{5... | collective-permute-start | bytes 7962632 | tf_op jit(solution)/shard_map/ppermute | solution.py:285
  366.1 32.7 %collective-permute-start.31 = (bf16[2,256,288]{2,1,0:T(8,128)(2,1)}, bf16[2,256,288]{2,1,0:T(8,128)(2,1)}, u32[]{:S(2)}, u32[]{:S(2)}) collective-permute-start(bf16[2,256,288]{2,1,0:T(8,128)(2,1)} %get-tuple-element.135), channel_id=1, source_target_pairs={{0,2},{1,3},{2,0},{3,1},{4,6},{5,7},{6,4},{7,5},{8,10},{9,11},{10,... | collective-permute-start | bytes 884744 | tf_op jit(solution)/shard_map/ppermute | solution.py:256
  366.1 34.1 %collective-permute-start.32 = (bf16[2,256,288]{2,1,0:T(8,128)(2,1)}, bf16[2,256,288]{2,1,0:T(8,128)(2,1)}, u32[]{:S(2)}, u32[]{:S(2)}) collective-permute-start(bf16[2,256,288]{2,1,0:T(8,128)(2,1)} %get-tuple-element.134), channel_id=1, source_target_pairs={{0,3},{1,0},{2,1},{3,2},{4,7},{5,4},{6,5},{7,6},{8,11},{9,8},{10,9... | collective-permute-start | bytes 884744 | tf_op jit(solution)/shard_map/ppermute | solution.py:256
  373.1 75.7 %collective-permute-start.61 = (bf16[4,144,1152]{2,1,0:T(8,128)(2,1)}, bf16[4,144,1152]{2,1,0:T(8,128)(2,1)}, u32[]{:S(2)}, u32[]{:S(2)}) collective-permute-start(bf16[4,144,1152]{2,1,0:T(8,128)(2,1)} %pad_maximum_fusion.13), channel_id=1, source_target_pairs={{0,4},{4,0},{8,12},{12,8},{16,20},{20,16},{24,28},{28,24},{1,5},{5... | collective-permute-start | bytes 3981320 | tf_op jit(solution)/shard_map/ppermute | solution.py:281
  412.8 167.5 %reduce-scatter.5.cloned.1.call-start = ((), (), s32[]{:S(2)}) async-start(), calls=%async_computation.5 | async-start | bytes 7864320 | tf_op jit(solution)/shard_map/reduce_scatter | solution.py:912
  482.9 57.9 %collective-permute-start.40 = (bf16[72,1152]{1,0:T(8,128)(2,1)S(1)}, bf16[72,1152]{1,0:T(8,128)(2,1)S(1)}, u32[]{:S(2)}, u32[]{:S(2)}) collective-permute-start(bf16[72,1152]{1,0:T(8,128)(2,1)S(1)} %maximum_maximum_fusion.1), channel_id=1, source_target_pairs={{1,0},{2,1},{3,2},{0,3},{5,4},{6,5},{7,6},{4,7},{9,8},{10,9},{11,1... | collective-permute-start | bytes 497672 | tf_op jit(solution)/shard_map/ppermute | solution.py:252
  484.4 56.3 %collective-permute-start.41 = (bf16[72,1152]{1,0:T(8,128)(2,1)S(1)}, bf16[72,1152]{1,0:T(8,128)(2,1)S(1)}, u32[]{:S(2)}, u32[]{:S(2)}) collective-permute-start(bf16[72,1152]{1,0:T(8,128)(2,1)S(1)} %maximum_maximum_fusion.1), channel_id=1, source_target_pairs={{2,0},{3,1},{0,2},{1,3},{6,4},{7,5},{4,6},{5,7},{10,8},{11,9},{8,1... | collective-permute-start | bytes 497672 | tf_op jit(solution)/shard_map/ppermute | solution.py:252
  485.9 54.8 %collective-permute-start.42 = (bf16[72,1152]{1,0:T(8,128)(2,1)S(1)}, bf16[72,1152]{1,0:T(8,128)(2,1)S(1)}, u32[]{:S(2)}, u32[]{:S(2)}) collective-permute-start(bf16[72,1152]{1,0:T(8,128)(2,1)S(1)} %maximum_maximum_fusion.1), channel_id=1, source_target_pairs={{3,0},{0,1},{1,2},{2,3},{7,4},{4,5},{5,6},{6,7},{11,8},{8,9},{9,10... | collective-permute-start | bytes 497672 | tf_op jit(solution)/shard_map/ppermute | solution.py:252
  (107 other events, 1135.4 us)
Sparse Core Ops, SparseCore 0:
  10.3 42.7 all-gather.2
  54.7 33.9 all-gather.4
  413.0 32.4 reduce-scatter.2
  447.6 132.6 reduce-scatter.4

commit v4 on v3

--- a/solution.py
+++ b/solution.py
@@ -602,11 +602,9 @@
         rows = pl.ds(pl.multiple_of(start % (2 * quarter), 8), home)
         term_ref[rows, :] += stream_grad_ref[0]
 
-    for half in range(2):
-        here = slice(half * quarter, (half + 1) * quarter)
-        low = term_ref[here, :].astype(jnp.bfloat16)
-        for head in range(heads):
-            shares_ref[head, here, :] = low[:, head * share : (head + 1) * share]
+    turned = term_ref[...].T
+    for head in range(heads):
+        shares_ref[head] = turned[head * share : (head + 1) * share, :].astype(jnp.bfloat16)
 
 
 def unit_grads_kernel(steps, left_ref, right_ref, *outs):
@@ -933,7 +931,7 @@
         kernel = functools.partial(leave_kernel, link, quarter, row)
         shares, sums_row = call(
             kernel if row == 0 else lambda *refs: kernel(*refs[:6], *refs[7:]),
-            [shape_of((heads, token_count, share), low), shape_of((4, 2, width), full)],
+            [shape_of((heads, share, token_count), low), shape_of((4, 2, width), full)],
             [
                 whole((8, 6 * width)),
                 pl.BlockSpec((2 * quarter, qkv_here), lambda i, _: (i, 0)),
@@ -943,7 +941,7 @@
             ]
             + [pl.BlockSpec(memory_space=pl.ANY)] * len(earlier),
             [
-                pl.BlockSpec((heads, 2 * quarter, share), lambda i, _, row=row: (0, i + 2 * row, 0)),
+                pl.BlockSpec((heads, share, 2 * quarter), lambda i, _, row=row: (0, 0, i + 2 * row)),
                 pl.BlockSpec((2, 2, width), lambda i, _: (i, 0, 0)),
             ],
             grid=(2,),
@@ -965,8 +963,8 @@
     in_slice_sum = head_sum(in_slice)
     shares = head_sum(hold(shares, in_slice_sum))[0]
     tokens_grad = jnp.where(
-        info[0] == 0, shares, jnp.concatenate([shares[SEQ:], shares[:SEQ]], axis=0)
-    )
+        info[0] == 0, shares, jnp.concatenate([shares[:, SEQ:], shares[:, :SEQ]], axis=1)
+    ).T
 
     block_home = hold(block_home, grad_mixed)
     block_home = jnp.stack(

time: 599 us -> 581 us (0.970)
  starting transfers between devices: 106 us -> 94.5 us
    ppermute x15, starting transfers between devices: 57 us -> 43.8 us  [core_swap(): lax.ppermute(values, 'batch', [(i, i ^ 1) for i in range(self.batches)])]
    reduce_scatter x2, waiting for transfers between devices: 19 us -> 6.95 us  [head_sum(): return lax.psum_scatter(values, 'head', scatter_dimension=0, tiled=True)]
    ppermute x20, waiting for transfers between devices: 33.8 us -> 39.9 us  [link_swap(): return lax.ppermute(values, 'batch', pairs)]
    unnamed x151 -> x150, local copies, waits for them, and re-layouts: 17 us -> 14.5 us
  transfers between devices with their start and end apart: 66 -> 66, of which waited for: 25 -> 24; matrix products, arithmetic and copies ran while one was open for 24% -> 24% of each run, Pallas kernels for 34% -> 35%
where the time goes in v4:
time: 581 us; the launch traced here: 573 us
  Pallas kernels  198 us (34%)
  waiting for transfers between devices  110 us (19%)
  starting transfers between devices  94.5 us (16%)
  other arithmetic  84.7 us (15%)
  local copies, waits for them, and re-layouts  49.2 us (8%)
  matrix products  21.3 us (4%)
  between operations  15.5 us (3%)
    pallas_call x18, Pallas kernels, call(): return lambda *arrays: run(*arrays, *order)  198 us
    ppermute x15, starting transfers between devices, core_swap(): lax.ppermute(values, 'batch', [(i, i ^ 1) for i in range(self.batches)])  43.8 us
    ppermute x20, waiting for transfers between devices, link_swap(): return lax.ppermute(values, 'batch', pairs)  39.9 us
    ppermute x15, waiting for transfers between devices, send(): lax.ppermute(values, 'head', [(i, (i + distance) % count) for i in range(...  39.6 us
    ppermute x12, waiting for transfers between devices, fetch(): lax.ppermute(values, 'head', [((i + distance) % count, i) for i in range(...  22.2 us
    ppermute x15, starting transfers between devices, send(): lax.ppermute(values, 'head', [(i, (i + distance) % count) for i in range(...  17.9 us
    dot_general x3, matrix products, tn(): lax.dot_general(left_side, right_side, (((0,), (0,)), ((), ())), preferre...  17.4 us
    ppermute x12, starting transfers between devices, fetch(): lax.ppermute(values, 'head', [((i + distance) % count, i) for i in range(...  16.9 us
  transfers between devices with their start and end apart: 66, of which 24 were waited for; matrix products, arithmetic and copies ran while one was open for 24% of the time, Pallas kernels for 35%

profile of v4, /device:TPU:9, one launch (start us, length us, event | category | flops | bytes accessed | tf_op | source)
XLA Modules:
  0.0 572.9 jit_solution(13447232232749457674)
XLA Ops:
  30.8 11.6 %project.1 = (bf16[2048,1152]{1,0:T(8,128)(2,1)}, bf16[2048,864]{1,0:T(8,128)(2,1)}, f32[8,6912]{1,0:T(8,128)}) custom-call(s32[8]{0:T(128)} %get-tuple-element.51.info_ref.refs_0_, f32[4,8,1728]{2,1,0:T(8,128)} %pad_maximum_fusion.24.table_rel_ref.refs_1_, bf16[2048,1152]{1,0:T(8,128)(2,1)} %refs_4_.3, bf16[864,1152]{1,0:T(8,128)(2,1)} %bitcast.236, ...), custom_call_target="tpu_custom_call" | custom-call | flops 285999988736 | bytes 858000000 | tf_op jit(solution)/shard_map/project/pallas_call | solution.py:217
  51.4 7.4 %attend_split.1 = (bf16[4,2,256,288]{3,2,1,0:T(8,128)(2,1)}, f32[1,4,1024]{2,1,0:T(4,128)}) custom-call(bf16[2,1024,864]{2,1,0:T(8,128)(2,1)} %bitcast.185), custom_call_target="tpu_custom_call" | custom-call | flops 131999997952 | bytes 396000000 | tf_op jit(solution)/shard_map/attend_split/pallas_call | solution.py:217
  63.0 14.7 %attend_whole.1 = (bf16[4,2,256,288]{3,2,1,0:T(8,128)(2,1)}, f32[1,4,1024]{2,1,0:T(4,128)}) custom-call(bf16[2,1024,864]{2,1,0:T(8,128)(2,1)} %bitcast.186, bf16[4,2,256,288]{3,2,1,0:T(8,128)(2,1)} %get-tuple-element.55.refs_1_, bf16[576,1152]{1,0:T(8,128)(2,1)} %hold.31.refs_2_), custom_call_target="tpu_custom_call", output_to_operand_aliasing={{0}: (1, {})} | custom-call | flops 352000016384 | bytes 1056000000 | tf_op jit(solution)/shard_map/attend_whole/pallas_call | solution.py:217
  100.0 6.5 %collective-permute-done.10 = bf16[2,256,288]{2,1,0:T(8,128)(2,1)S(1)} collective-permute-done((bf16[2,256,288]{2,1,0:T(8,128)(2,1)S(1)}, bf16[2,256,288]{2,1,0:T(8,128)(2,1)S(1)}, u32[]{:S(2)}, u32[]{:S(2)}) %collective-permute-start.10) | collective-permute-done | bytes 294944 | tf_op jit(solution)/shard_map/ppermute | solution.py:252
  106.4 18.6 %collective-permute-start.15 = (bf16[1152,1152]{1,0:T(8,128)(2,1)}, bf16[1152,1152]{1,0:T(8,128)(2,1)}, u32[]{:S(2)}, u32[]{:S(2)}) collective-permute-start(bf16[1152,1152]{1,0:T(8,128)(2,1)} %pad_maximum_fusion.3.refs_1_.refs_2_.refs_10_), channel_id=1, source_target_pairs={{0,4},{4,0},{8,12},{12,8},{16,20},{20,16},{24,28},{28,24},{1,5},{5... | collective-permute-start | bytes 7962632 | tf_op jit(solution)/shard_map/ppermute | solution.py:281
  125.1 5.8 %collective-permute-done.12 = bf16[2,256,288]{2,1,0:T(8,128)(2,1)S(1)} collective-permute-done((bf16[2,256,288]{2,1,0:T(8,128)(2,1)S(1)}, bf16[2,256,288]{2,1,0:T(8,128)(2,1)S(1)}, u32[]{:S(2)}, u32[]{:S(2)}) %collective-permute-start.12) | collective-permute-done | bytes 294944 | tf_op jit(solution)/shard_map/ppermute | solution.py:252
  136.6 9.0 %enter.1 = (f32[2,256,1152]{2,1,0:T(8,128)}, f32[2,256,1152]{2,1,0:T(8,128)}, bf16[2,256,1152]{2,1,0:T(8,128)(2,1)}, bf16[2,256,1152]{2,1,0:T(8,128)(2,1)}, bf16...) custom-call(s32[8]{0:T(128)} %get-tuple-element.51.info_ref.refs_0_, ...), custom_call_target="tpu_custom_call" | custom-call | flops 198000001024 | bytes 594000000 | tf_op jit(solution)/shard_map/enter/pallas_call | solution.py:217
  152.9 14.0 %collective-permute-done.17.refs_15_ = bf16[1152,1152]{1,0:T(8,128)(2,1)} collective-permute-done((bf16[1152,1152]{1,0:T(8,128)(2,1)}, bf16[1152,1152]{1,0:T(8,128)(2,1)}, u32[]{:S(2)}, u32[]{:S(2)}) %collective-permute-start.17) | collective-permute-done | bytes 2654240 | tf_op jit(solution)/shard_map/ppermute | solution.py:285
  168.2 16.8 %expand.1 = (bf16[512,4608]{1,0:T(8,128)(2,1)}, bf16[512,4608]{1,0:T(8,128)(2,1)}) custom-call(bf16[512,1152]{1,0:T(8,128)(2,1)} %bitcast.213, f32[1,4608]{1,0:T(1,128)} %reshape.230.refs_1_, bf16[1152,1152]{1,0:T(8,128)(2,1)} %pad_maximum_fusion.3.refs_1_.refs_2_.refs_10_, bf16[1152,1152]{1,0:T(8,128)(2,1)} %hold.41.refs_3_.refs_11_, ...), custom_call_target="tpu_custom_call" | custom-call | flops 439999987712 | bytes 1320000000 | tf_op jit(solution)/shard_map/expand/pallas_call | solution.py:217
  185.0 15.1 %unit_grads.2 = (bf16[1152,1152]{1,0:T(8,128)(2,1)}, bf16[1152,1152]{1,0:T(8,128)(2,1)}, bf16[1152,1152]{1,0:T(8,128)(2,1)}, bf16[1152,1152]{1,0:T(8,128)(2,1)}) custom-call(bf16[512,4608]{1,0:T(8,128)(2,1)} %get-tuple-element.61.refs_0_.refs_4_, bf16[512,1152]{1,0:T(8,128)(2,1)} %bitcast.239, bf16[1152,1152]{1,0:T(8,128)(2,1)} %collective-permute-done.18.refs_2_.refs_16_), custom_call_target="tpu_custom_call" | custom-call | flops 307999997952 | bytes 924000000 | tf_op jit(solution)/shard_map/unit_grads/pallas_call | solution.py:217
  200.7 36.0 %contract.1 = (bf16[512,4608]{1,0:T(8,128)(2,1)}, f32[1,4608]{1,0:T(1,128)}, bf16[4,2,256,288]{3,2,1,0:T(8,128)(2,1)}, f32[2,256,1152]{2,1,0:T(8,128)}, bf16[2,2...) custom-call(s32[8]{0:T(128)} %get-tuple-element.51.info_ref.refs_0_, ...), custom_call_target="tpu_custom_call" | custom-call | flops 968000012288 | bytes 2904000000 | tf_op jit(solution)/shard_map/contract/pallas_call | solution.py:217
  251.0 15.1 %unit_grads.3 = (bf16[1152,1152]{1,0:T(8,128)(2,1)}, bf16[1152,1152]{1,0:T(8,128)(2,1)}, bf16[1152,1152]{1,0:T(8,128)(2,1)}, bf16[1152,1152]{1,0:T(8,128)(2,1)}) custom-call(bf16[512,4608]{1,0:T(8,128)(2,1)} %get-tuple-element.69.refs_1_.refs_0_, bf16[512,1152]{1,0:T(8,128)(2,1)} %bitcast.214, bf16[1152,1152]{1,0:T(8,128)(2,1)} %add_convert_fusion.5.refs_2_), custom_call_target="tpu_custom_call" | custom-call | flops 307999997952 | bytes 924000000 | tf_op jit(solution)/shard_map/unit_grads/pallas_call | solution.py:217
  268.3 7.2 %collective-permute-done.22.refs_0_ = bf16[2,256,288]{2,1,0:T(8,128)(2,1)} collective-permute-done((bf16[2,256,288]{2,1,0:T(8,128)(2,1)}, bf16[2,256,288]{2,1,0:T(8,128)(2,1)}, u32[]{:S(2)}, u32[]{:S(2)}) %collective-permute-start.22) | collective-permute-done | bytes 294944 | tf_op jit(solution)/shard_map/ppermute | solution.py:256
  280.5 8.1 %attend_back_split.1 = bf16[1,1024,864]{2,1,0:T(8,128)(2,1)} custom-call(bf16[2,1024,864]{2,1,0:T(8,128)(2,1)} %bitcast.187, f32[1,4,1024]{2,1,0:T(4,128)} %get-tuple-element.56.refs_1_.lse_ref, bf16[4,2,256,288]{3,2,1,0:T(8,128)(2,1)} %pad_maximum_fusion.8.refs_1_.pieces_ref.refs_2_), custom_call_target="tpu_custom_call" | custom-call | flops 176000008192 | bytes 528000000 | tf_op jit(solution)/shard_map/attend_back_split/pallas_call | solution.py:217
  307.8 9.8 %leave.2 = (bf16[4,288,2048]{2,1,0:T(8,128)(2,1)}, f32[4,2,1152]{2,1,0:T(2,128)}) custom-call(s32[8]{0:T(128)} %get-tuple-element.51.info_ref.refs_0_, f32[8,6912]{1,0:T(8,128)} %get-tuple-element.53.refs_1_, bf16[1024,864]{1,0:T(8,128)(2,1)} %bitcast.206, bf16[864,1152]{1,0:T(8,128)(2,1)} %bitcast.237, bf16[2048,1152]{1,0:T(8,128)(2,1)} %refs_4_.3, ...), custom_call_target="tpu_custom_call" | custom-call | flops 198000001024 | bytes 594000000 | tf_op jit(solution)/shard_map/leave/pallas_call | solution.py:217
  325.3 17.9 %attend_back_whole.1 = bf16[1,1024,864]{2,1,0:T(8,128)(2,1)} custom-call(bf16[2,1024,864]{2,1,0:T(8,128)(2,1)} %bitcast.188, f32[1,4,1024]{2,1,0:T(4,128)} %get-tuple-element.58.refs_1_, bf16[4,2,256,288]{3,2,1,0:T(8,128)(2,1)} %pad_maximum_fusion.8.refs_1_.pieces_ref.refs_2_, f32[4,2,1152]{2,1,0:T(2,128)} %get-tuple-element.78.refs_3_, ...), custom_call_target="tpu_custom_call" | custom-call | flops 527999991808 | bytes 1584000000 | tf_op jit(solution)/shard_map/attend_back_whole/pallas_call | solution.py:217
  378.9 9.8 %leave.3 = (bf16[4,288,2048]{2,1,0:T(8,128)(2,1)}, f32[4,2,1152]{2,1,0:T(2,128)}) custom-call(s32[8]{0:T(128)} %get-tuple-element.51.info_ref.refs_0_, f32[8,6912]{1,0:T(8,128)} %get-tuple-element.53.refs_1_, bf16[1024,864]{1,0:T(8,128)(2,1)} %bitcast.180, bf16[864,1152]{1,0:T(8,128)(2,1)} %bitcast.238, ...), custom_call_target="tpu_custom_call", output_to_operand_aliasing={{0}: (6, {})} | custom-call | flops 198000001024 | bytes 594000000 | tf_op jit(solution)/shard_map/leave/pallas_call | solution.py:217
  391.0 7.5 %collective-permute-done.31.refs_0_ = bf16[2,256,288]{2,1,0:T(8,128)(2,1)} collective-permute-done((bf16[2,256,288]{2,1,0:T(8,128)(2,1)}, bf16[2,256,288]{2,1,0:T(8,128)(2,1)}, u32[]{:S(2)}, u32[]{:S(2)}) %collective-permute-start.31) | collective-permute-done | bytes 294944 | tf_op jit(solution)/shard_map/ppermute | solution.py:256
  417.3 9.9 %convolution_convert_fusion = bf16[864,1152]{1,0:T(8,128)(2,1)} fusion(bf16[2048,864]{1,0:T(8,128)(2,1)} %hold.57, bf16[2048,1152]{1,0:T(8,128)(2,1)} %get-tuple-element.86), kind=kOutput, calls=%fused_computation.26 | convolution fusion | flops 4077858816 | bytes 10248192 | tf_op jit(solution)/shard_map/dot_general | solution.py:169
  438.2 6.9 %reduce-scatter.3.cloned.1.call-done.refs_1_ = bf16[144,1152]{1,0:T(8,128)(2,1)} async-done(((bf16[576,1152]{1,0:T(8,128)(2,1)}), bf16[144,1152]{1,0:T(8,128)(2,1)}) %reduce-scatter.3.cloned.1.call-update) | async-done | bytes 331792 | tf_op jit(solution)/shard_map/reduce_scatter | solution.py:910
  455.9 8.5 %collective-permute-done.38 = f32[2,8,1728]{2,1,0:T(8,128)S(1)} collective-permute-done((f32[2,8,1728]{2,1,0:T(8,128)S(1)}, f32[2,8,1728]{2,1,0:T(8,128)S(1)}, u32[]{:S(2)}, u32[]{:S(2)}) %collective-permute-start.38) | collective-permute-done | bytes 110624 | tf_op jit(solution)/shard_map/ppermute | solution.py:285
  491.9 10.9 %collective-permute-done.48 = bf16[40,1152]{1,0:T(8,128)(2,1)S(1)} collective-permute-done((bf16[40,1152]{1,0:T(8,128)(2,1)S(1)}, bf16[40,1152]{1,0:T(8,128)(2,1)S(1)}, u32[]{:S(2)}, u32[]{:S(2)}) %collective-permute-start.48) | collective-permute-done | bytes 92192 | tf_op jit(solution)/shard_map/ppermute | solution.py:256
  518.3 5.9 %collective-permute-done.54 = bf16[2,144,1152]{2,1,0:T(8,128)(2,1)S(1)} collective-permute-done((bf16[2,144,1152]{2,1,0:T(8,128)(2,1)S(1)}, bf16[2,144,1152]{2,1,0:T(8,128)(2,1)S(1)}, u32[]{:S(2)}, u32[]{:S(2)}) %collective-permute-start.54) | collective-permute-done | bytes 663584 | tf_op jit(solution)/shard_map/ppermute | solution.py:285
  543.4 7.5 %place_columns.1 = f32[1152,1152]{1,0:T(8,128)} custom-call(bf16[8,144,1152]{2,1,0:T(8,128)(2,1)} %pad_maximum_fusion.5.slices_ref), custom_call_target="tpu_custom_call" | custom-call | tf_op jit(solution)/shard_map/place_columns/pallas_call | solution.py:217
  (455 shorter events, 276.9 us)
Async XLA Ops:
  7.2 55.6 %all-gather.3.cloned.1.call-start = ((), (), s32[]{:S(2)}) async-start(), calls=%async_computation.2 | async-start | bytes 1658880 | tf_op jit(solution)/shard_map/all_gather | solution.py:739
  10.2 80.5 %all-gather.5.cloned.1.call-start = ((), (), s32[]{:S(2)}) async-start(), calls=%async_computation.3 | async-start | bytes 1658880 | tf_op jit(solution)/shard_map/all_gather | solution.py:740
  22.0 423.1 %reduce-scatter.3.cloned.1.call-start = ((), (), s32[]{:S(2)}) async-start(), calls=%async_computation.4 | async-start | bytes 1658880 | tf_op jit(solution)/shard_map/reduce_scatter | solution.py:910
  90.7 41.7 %collective-permute-start.13 = (bf16[576,1152]{1,0:T(8,128)(2,1)}, bf16[576,1152]{1,0:T(8,128)(2,1)}, u32[]{:S(2)}, u32[]{:S(2)}) collective-permute-start(bf16[576,1152]{1,0:T(8,128)(2,1)} %hold.33.refs_1_), channel_id=1, source_target_pairs={{0,16},{4,12},{8,24},{12,4},{16,0},{20,28},{24,8},{28,20},{1,17},{... | collective-permute-start | bytes 3981320 | tf_op jit(solution)/shard_map/ppermute | solution.py:285
  97.1 33.7 %collective-permute-start.12 = (bf16[2,256,288]{2,1,0:T(8,128)(2,1)S(1)}, bf16[2,256,288]{2,1,0:T(8,128)(2,1)S(1)}, u32[]{:S(2)}, u32[]{:S(2)}) collective-permute-start(bf16[2,256,288]{2,1,0:T(8,128)(2,1)S(1)} %get-tuple-element.140), channel_id=1, source_target_pairs={{3,0},{0,1},{1,2},{2,3},{7,4},{4,5},{5,6},{6,7},{11,8},{8,9},{9,10... | collective-permute-start | bytes 884744 | tf_op jit(solution)/shard_map/ppermute | solution.py:252
  98.8 46.9 %collective-permute-start.14 = (bf16[1152,1152]{1,0:T(8,128)(2,1)}, bf16[1152,1152]{1,0:T(8,128)(2,1)}, u32[]{:S(2)}, u32[]{:S(2)}) collective-permute-start(bf16[1152,1152]{1,0:T(8,128)(2,1)} %pad_maximum_fusion.3.refs_1_.refs_2_.refs_10_), channel_id=1, source_target_pairs={{0,8},{4,20},{8,0},{12,28},{16,24},{20,4},{24,16},{28,12},{1,9},{5... | collective-permute-start | bytes 7962632 | tf_op jit(solution)/shard_map/ppermute | solution.py:285
  106.4 61.8 %collective-permute-start.15 = (bf16[1152,1152]{1,0:T(8,128)(2,1)}, bf16[1152,1152]{1,0:T(8,128)(2,1)}, u32[]{:S(2)}, u32[]{:S(2)}) collective-permute-start(bf16[1152,1152]{1,0:T(8,128)(2,1)} %pad_maximum_fusion.3.refs_1_.refs_2_.refs_10_), channel_id=1, source_target_pairs={{0,4},{4,0},{8,12},{12,8},{16,20},{20,16},{24,28},{28,24},{1,5},{5... | collective-permute-start | bytes 7962632 | tf_op jit(solution)/shard_map/ppermute | solution.py:281
  135.4 31.5 %collective-permute-start.17 = (bf16[1152,1152]{1,0:T(8,128)(2,1)}, bf16[1152,1152]{1,0:T(8,128)(2,1)}, u32[]{:S(2)}, u32[]{:S(2)}) collective-permute-start(bf16[1152,1152]{1,0:T(8,128)(2,1)} %pad_maximum_fusion.4.refs_7_.refs_6_.refs_14_), channel_id=1, source_target_pairs={{0,8},{4,20},{8,0},{12,28},{16,24},{20,4},{24,16},{28,12},{1,9},{5... | collective-permute-start | bytes 7962632 | tf_op jit(solution)/shard_map/ppermute | solution.py:285
  152.2 32.8 %collective-permute-start.18 = (bf16[1152,1152]{1,0:T(8,128)(2,1)}, bf16[1152,1152]{1,0:T(8,128)(2,1)}, u32[]{:S(2)}, u32[]{:S(2)}) collective-permute-start(bf16[1152,1152]{1,0:T(8,128)(2,1)} %pad_maximum_fusion.4.refs_7_.refs_6_.refs_14_), channel_id=1, source_target_pairs={{0,4},{4,0},{8,12},{12,8},{16,20},{20,16},{24,28},{28,24},{1,5},{5... | collective-permute-start | bytes 7962632 | tf_op jit(solution)/shard_map/ppermute | solution.py:281
  166.9 33.8 %collective-permute-start.19 = (bf16[1152,1152]{1,0:T(8,128)(2,1)}, bf16[1152,1152]{1,0:T(8,128)(2,1)}, u32[]{:S(2)}, u32[]{:S(2)}) collective-permute-start(bf16[1152,1152]{1,0:T(8,128)(2,1)} %collective-permute-done.17.refs_15_), channel_id=1, source_target_pairs={{0,4},{4,0},{8,12},{12,8},{16,20},{20,16},{24,28},{28,24},{1,5},{5... | collective-permute-start | bytes 7962632 | tf_op jit(solution)/shard_map/ppermute | solution.py:281
  200.1 88.5 %collective-permute-start.27 = (bf16[1152,1152]{1,0:T(8,128)(2,1)}, bf16[1152,1152]{1,0:T(8,128)(2,1)}, u32[]{:S(2)}, u32[]{:S(2)}) collective-permute-start(bf16[1152,1152]{1,0:T(8,128)(2,1)} %get-tuple-element.77), channel_id=1, source_target_pairs={{0,4},{4,0},{8,12},{12,8},{16,20},{20,16},{24,28},{28,24},{1,5},{5... | collective-permute-start | bytes 7962632 | tf_op jit(solution)/shard_map/ppermute | solution.py:281
  200.2 45.0 %collective-permute-start.21 = (bf16[1152,1152]{1,0:T(8,128)(2,1)}, bf16[1152,1152]{1,0:T(8,128)(2,1)}, u32[]{:S(2)}, u32[]{:S(2)}) collective-permute-start(bf16[1152,1152]{1,0:T(8,128)(2,1)} %get-tuple-element.71), channel_id=1, source_target_pairs={{0,4},{4,0},{8,12},{12,8},{16,20},{20,16},{24,28},{28,24},{1,5},{5... | collective-permute-start | bytes 7962632 | tf_op jit(solution)/shard_map/ppermute | solution.py:281
  241.5 34.1 %collective-permute-start.22 = (bf16[2,256,288]{2,1,0:T(8,128)(2,1)}, bf16[2,256,288]{2,1,0:T(8,128)(2,1)}, u32[]{:S(2)}, u32[]{:S(2)}) collective-permute-start(bf16[2,256,288]{2,1,0:T(8,128)(2,1)} %get-tuple-element.137), channel_id=1, source_target_pairs={{0,2},{1,3},{2,0},{3,1},{4,6},{5,7},{6,4},{7,5},{8,10},{9,11},{10,... | collective-permute-start | bytes 884744 | tf_op jit(solution)/shard_map/ppermute | solution.py:256
  243.8 33.9 %collective-permute-start.23 = (bf16[2,256,288]{2,1,0:T(8,128)(2,1)}, bf16[2,256,288]{2,1,0:T(8,128)(2,1)}, u32[]{:S(2)}, u32[]{:S(2)}) collective-permute-start(bf16[2,256,288]{2,1,0:T(8,128)(2,1)} %get-tuple-element.136), channel_id=1, source_target_pairs={{0,3},{1,0},{2,1},{3,2},{4,7},{5,4},{6,5},{7,6},{8,11},{9,8},{10,9... | collective-permute-start | bytes 884744 | tf_op jit(solution)/shard_map/ppermute | solution.py:256
  250.8 37.8 %collective-permute-start.28 = (bf16[1152,1152]{1,0:T(8,128)(2,1)}, bf16[1152,1152]{1,0:T(8,128)(2,1)}, u32[]{:S(2)}, u32[]{:S(2)}) collective-permute-start(bf16[1152,1152]{1,0:T(8,128)(2,1)} %add_convert_fusion.5.refs_2_), channel_id=1, source_target_pairs={{0,8},{4,20},{8,0},{12,28},{16,24},{20,4},{24,16},{28,12},{1,9},{5... | collective-permute-start | bytes 7962632 | tf_op jit(solution)/shard_map/ppermute | solution.py:285
  266.1 35.1 %collective-permute-start.26 = (bf16[1152,1152]{1,0:T(8,128)(2,1)}, bf16[1152,1152]{1,0:T(8,128)(2,1)}, u32[]{:S(2)}, u32[]{:S(2)}) collective-permute-start(bf16[1152,1152]{1,0:T(8,128)(2,1)} %get-tuple-element.76), channel_id=1, source_target_pairs={{0,4},{4,0},{8,12},{12,8},{16,20},{20,16},{24,28},{28,24},{1,5},{5... | collective-permute-start | bytes 7962632 | tf_op jit(solution)/shard_map/ppermute | solution.py:281
  307.0 68.0 %collective-permute-start.30 = (bf16[1152,1152]{1,0:T(8,128)(2,1)}, bf16[1152,1152]{1,0:T(8,128)(2,1)}, u32[]{:S(2)}, u32[]{:S(2)}) collective-permute-start(bf16[1152,1152]{1,0:T(8,128)(2,1)} %add_convert_fusion.3.refs_7_), channel_id=1, source_target_pairs={{0,8},{4,20},{8,0},{12,28},{16,24},{20,4},{24,16},{28,12},{1,9},{5... | collective-permute-start | bytes 7962632 | tf_op jit(solution)/shard_map/ppermute | solution.py:285
  365.8 32.7 %collective-permute-start.31 = (bf16[2,256,288]{2,1,0:T(8,128)(2,1)}, bf16[2,256,288]{2,1,0:T(8,128)(2,1)}, u32[]{:S(2)}, u32[]{:S(2)}) collective-permute-start(bf16[2,256,288]{2,1,0:T(8,128)(2,1)} %get-tuple-element.133), channel_id=1, source_target_pairs={{0,2},{1,3},{2,0},{3,1},{4,6},{5,7},{6,4},{7,5},{8,10},{9,11},{10,... | collective-permute-start | bytes 884744 | tf_op jit(solution)/shard_map/ppermute | solution.py:256
  365.8 33.7 %collective-permute-start.32 = (bf16[2,256,288]{2,1,0:T(8,128)(2,1)}, bf16[2,256,288]{2,1,0:T(8,128)(2,1)}, u32[]{:S(2)}, u32[]{:S(2)}) collective-permute-start(bf16[2,256,288]{2,1,0:T(8,128)(2,1)} %get-tuple-element.132), channel_id=1, source_target_pairs={{0,3},{1,0},{2,1},{3,2},{4,7},{5,4},{6,5},{7,6},{8,11},{9,8},{10,9... | collective-permute-start | bytes 884744 | tf_op jit(solution)/shard_map/ppermute | solution.py:256
  372.8 75.7 %collective-permute-start.61 = (bf16[4,144,1152]{2,1,0:T(8,128)(2,1)}, bf16[4,144,1152]{2,1,0:T(8,128)(2,1)}, u32[]{:S(2)}, u32[]{:S(2)}) collective-permute-start(bf16[4,144,1152]{2,1,0:T(8,128)(2,1)} %pad_maximum_fusion.13), channel_id=1, source_target_pairs={{0,4},{4,0},{8,12},{12,8},{16,20},{20,16},{24,28},{28,24},{1,5},{5... | collective-permute-start | bytes 3981320 | tf_op jit(solution)/shard_map/ppermute | solution.py:281
  412.1 150.9 %reduce-scatter.5.cloned.1.call-start = ((), (), s32[]{:S(2)}) async-start(), calls=%async_computation.5 | async-start | bytes 5898240 | tf_op jit(solution)/shard_map/reduce_scatter | solution.py:910
  482.5 53.1 %collective-permute-start.40 = (bf16[72,1152]{1,0:T(8,128)(2,1)S(1)}, bf16[72,1152]{1,0:T(8,128)(2,1)S(1)}, u32[]{:S(2)}, u32[]{:S(2)}) collective-permute-start(bf16[72,1152]{1,0:T(8,128)(2,1)S(1)} %maximum_maximum_fusion.1), channel_id=1, source_target_pairs={{1,0},{2,1},{3,2},{0,3},{5,4},{6,5},{7,6},{4,7},{9,8},{10,9},{11,1... | collective-permute-start | bytes 497672 | tf_op jit(solution)/shard_map/ppermute | solution.py:252
  483.9 51.7 %collective-permute-start.41 = (bf16[72,1152]{1,0:T(8,128)(2,1)S(1)}, bf16[72,1152]{1,0:T(8,128)(2,1)S(1)}, u32[]{:S(2)}, u32[]{:S(2)}) collective-permute-start(bf16[72,1152]{1,0:T(8,128)(2,1)S(1)} %maximum_maximum_fusion.1), channel_id=1, source_target_pairs={{2,0},{3,1},{0,2},{1,3},{6,4},{7,5},{4,6},{5,7},{10,8},{11,9},{8,1... | collective-permute-start | bytes 497672 | tf_op jit(solution)/shard_map/ppermute | solution.py:252
  487.1 48.6 %collective-permute-start.42 = (bf16[72,1152]{1,0:T(8,128)(2,1)S(1)}, bf16[72,1152]{1,0:T(8,128)(2,1)S(1)}, u32[]{:S(2)}, u32[]{:S(2)}) collective-permute-start(bf16[72,1152]{1,0:T(8,128)(2,1)S(1)} %maximum_maximum_fusion.1), channel_id=1, source_target_pairs={{3,0},{0,1},{1,2},{2,3},{7,4},{4,5},{5,6},{6,7},{11,8},{8,9},{9,10... | collective-permute-start | bytes 497672 | tf_op jit(solution)/shard_map/ppermute | solution.py:252
  (107 other events, 1123.4 us)
Sparse Core Ops, SparseCore 0:
  10.3 42.7 all-gather.2
  54.7 33.9 all-gather.4
  412.2 32.8 reduce-scatter.2
  447.3 107.1 reduce-scatter.4

commit v5 on v4

--- a/solution.py
+++ b/solution.py
@@ -42,15 +42,15 @@
         total = jnp.sum(weights, axis=0, keepdims=True)
         mixed_t = nn(value_rows.T, weights.astype(jnp.bfloat16)) / total
         lse_ref[0, head : head + 1, rows] = peak * (KEY_SCALE * LOG2E) + jnp.log2(total)
-        return mixed_t.T
+        return mixed_t
 
     def step(index, _):
         start = pl.multiple_of(index * chunk, chunk)
         outs = [part(head, start) for head in range(heads)]
-        outs = jnp.concatenate(outs, axis=1).astype(jnp.bfloat16)
+        outs = jnp.concatenate(outs, axis=0).astype(jnp.bfloat16)
         for spot in range(chunk // home):
             target = index * (chunk // home) + spot
-            mixed_ref[(group - target + groups) % groups, 0] = outs[spot * home : (spot + 1) * home]
+            mixed_ref[(group - target + groups) % groups, 0] = outs[:, spot * home : (spot + 1) * home]
         return 0
 
     lax.fori_loop(0, seq // chunk, step, 0, unroll=True)
@@ -64,12 +64,12 @@
     return call(
         kernel if mixed is None else lambda p, _, *refs: kernel(p, *refs),
         [
-            shape_of((groups, 2, seq // groups, heads * HEAD_DIM), jnp.bfloat16),
+            shape_of((groups, 2, heads * HEAD_DIM, seq // groups), jnp.bfloat16),
             shape_of((1, heads, seq), jnp.float32),
         ],
         [pl.BlockSpec((1, seq, width), lambda i: (row, 0, 0))] + [pl.BlockSpec(memory_space=pl.ANY)] * len(earlier),
         [
-            pl.BlockSpec((groups, 1, seq // groups, heads * HEAD_DIM), lambda i: (0, row, 0, 0)),
+            pl.BlockSpec((groups, 1, heads * HEAD_DIM, seq // groups), lambda i: (0, row, 0, 0)),
             pl.BlockSpec((1, heads, seq), lambda i: (0, 0, 0)),
         ],
         grid=(1,),
@@ -87,7 +87,8 @@
     width = 3 * HEAD_DIM
     key_count = chunk if split else seq
     for spot in range(groups):
-        grad_ref[spot * home : (spot + 1) * home, :] = pieces_ref[(group - spot + groups) % groups, 0]
+        piece = pieces_ref[(group - spot + groups) % groups, 0].astype(jnp.float32).T
+        grad_ref[spot * home : (spot + 1) * home, :] = piece.astype(jnp.bfloat16)
 
     def part(head, start, key_turned=None):
         at = head * width
@@ -147,7 +148,7 @@
         [
             pl.BlockSpec((1, seq, width), lambda i: (row, 0, 0)),
             pl.BlockSpec((1, heads, seq), lambda i: (0, 0, 0)),
-            pl.BlockSpec((groups, 1, seq // groups, heads * HEAD_DIM), lambda i: (0, row, 0, 0)),
+            pl.BlockSpec((groups, 1, heads * HEAD_DIM, seq // groups), lambda i: (0, row, 0, 0)),
         ],
         pl.BlockSpec((1, seq, width), lambda i: (0, 0, 0)),
         grid=(1,),
@@ -432,8 +433,8 @@
                     proj_true_ref[at : at + count, :] = piece[:count]
 
     for spot in range(heads):
-        piece = mixed_ref[(spot - head + heads) % heads, 0]
-        mixed_home_ref[0, :, spot * share : (spot + 1) * share] = piece
+        piece = mixed_ref[(spot - head + heads) % heads, 0].astype(jnp.float32).T
+        mixed_home_ref[0, :, spot * share : (spot + 1) * share] = piece.astype(jnp.bfloat16)
     spot = home_row(info_ref, row, home, quarter)
 
     def mod(group):
@@ -566,9 +567,9 @@
         grad_attn = (rounded * mod(2)).astype(jnp.bfloat16)
         grad_attn_ref[row] = grad_attn
         attn_sum += jnp.sum(grad_attn.astype(jnp.float32), axis=0, keepdims=True)
-        grad_mixed = nt(grad_attn, proj_buf[...]).astype(jnp.bfloat16)
+        grad_mixed = nt(proj_buf[...], grad_attn).astype(jnp.bfloat16)
         for other in range(heads):
-            grad_mixed_ref[(other - head + heads) % heads, row] = grad_mixed[:, other * share : (other + 1) * share]
+            grad_mixed_ref[(other - head + heads) % heads, row] = grad_mixed[other * share : (other + 1) * share]
     attn_sum_ref[...] = attn_sum
     for piece in range(count - 2, count):
         pre_copy(piece).wait()
@@ -809,7 +810,7 @@
         ],
         [
             whole((8, 6 * width)),
-            pl.BlockSpec((heads, 1, home, share), lambda i, _: (0, i, 0, 0)),
+            pl.BlockSpec((heads, 1, share, home), lambda i, _: (0, i, 0, 0)),
             whole(proj_all.shape),
             home_spec,
             home_spec,
@@ -861,7 +862,7 @@
             shape_of((heads, rows, home, share), low),
             shape_of((rows, home, width), full),
             shape_of((rows, home, width), low),
-            shape_of((heads, rows, home, share), low),
+            shape_of((heads, rows, share, home), low),
             shape_of((rows, 4, width), full),
             shape_of((1, width), full),
         ],
@@ -873,7 +874,7 @@
             by_head,
             stay,
             stay,
-            by_head,
+            whole((heads, rows, share, home)),
             whole((rows, 4, width)),
             whole((1, width)),
         ],

time: 581 us -> 568 us (0.978)
  starting transfers between devices: 94.5 us -> 84.4 us
    ppermute x20, waiting for transfers between devices: 39.9 us -> 48.7 us  [link_swap(): return lax.ppermute(values, 'batch', pairs)]
    ppermute x15, waiting for transfers between devices: 39.6 us -> 32.3 us  [send(): lax.ppermute(values, 'head', [(i, (i + distance) % count) for i in range(...]
  transfers between devices with their start and end apart: 66 -> 66, of which waited for: 24 -> 25; matrix products, arithmetic and copies ran while one was open for 24% -> 25% of each run, Pallas kernels for 35% -> 35%
where the time goes in v5:
time: 568 us; the launch traced here: 558 us
  Pallas kernels  198 us (35%)
  waiting for transfers between devices  107 us (19%)
  starting transfers between devices  84.4 us (15%)
  other arithmetic  83.9 us (15%)
  local copies, waits for them, and re-layouts  48.5 us (9%)
  matrix products  21.2 us (4%)
  between operations  15.4 us (3%)
    pallas_call x18, Pallas kernels, call(): return lambda *arrays: run(*arrays, *order)  198 us
    ppermute x20, waiting for transfers between devices, link_swap(): return lax.ppermute(values, 'batch', pairs)  48.7 us
    ppermute x15, starting transfers between devices, core_swap(): lax.ppermute(values, 'batch', [(i, i ^ 1) for i in range(self.batches)])  39.1 us
    ppermute x15, waiting for transfers between devices, send(): lax.ppermute(values, 'head', [(i, (i + distance) % count) for i in range(...  32.3 us
    ppermute x12, waiting for transfers between devices, fetch(): lax.ppermute(values, 'head', [((i + distance) % count, i) for i in range(...  18.3 us
    dot_general x3, matrix products, tn(): lax.dot_general(left_side, right_side, (((0,), (0,)), ((), ())), preferre...  17.2 us
    ppermute x20, starting transfers between devices, link_swap(): return lax.ppermute(values, 'batch', pairs)  16.3 us
    ppermute x12, starting transfers between devices, fetch(): lax.ppermute(values, 'head', [((i + distance) % count, i) for i in range(...  16.1 us
  transfers between devices with their start and end apart: 66, of which 25 were waited for; matrix products, arithmetic and copies ran while one was open for 25% of the time, Pallas kernels for 35%

profile of v5, /device:TPU:9, one launch (start us, length us, event | category | flops | bytes accessed | tf_op | source)
XLA Modules:
  0.0 558.4 jit_solution(16621819362064499524)
XLA Ops:
  30.8 11.6 %project.1 = (bf16[2048,1152]{1,0:T(8,128)(2,1)}, bf16[2048,864]{1,0:T(8,128)(2,1)}, f32[8,6912]{1,0:T(8,128)}) custom-call(s32[8]{0:T(128)} %get-tuple-element.51.info_ref.refs_0_, f32[4,8,1728]{2,1,0:T(8,128)} %pad_maximum_fusion.24.table_rel_ref.refs_1_, bf16[2048,1152]{1,0:T(8,128)(2,1)} %refs_4_.3, bf16[864,1152]{1,0:T(8,128)(2,1)} %bitcast.236, ...), custom_call_target="tpu_custom_call" | custom-call | flops 285999988736 | bytes 858000000 | tf_op jit(solution)/shard_map/project/pallas_call | solution.py:218
  44.2 4.9 collective-permute-done.4.refs_0_
  51.4 7.2 %attend_split.1 = (bf16[4,2,288,256]{3,2,1,0:T(8,128)(2,1)}, f32[1,4,1024]{2,1,0:T(4,128)}) custom-call(bf16[2,1024,864]{2,1,0:T(8,128)(2,1)} %bitcast.185), custom_call_target="tpu_custom_call" | custom-call | flops 131999997952 | bytes 396000000 | tf_op jit(solution)/shard_map/attend_split/pallas_call | solution.py:218
  62.8 14.5 %attend_whole.1 = (bf16[4,2,288,256]{3,2,1,0:T(8,128)(2,1)}, f32[1,4,1024]{2,1,0:T(4,128)}) custom-call(bf16[2,1024,864]{2,1,0:T(8,128)(2,1)} %bitcast.186, bf16[4,2,288,256]{3,2,1,0:T(8,128)(2,1)} %get-tuple-element.55.refs_1_, bf16[576,1152]{1,0:T(8,128)(2,1)} %hold.31.refs_2_), custom_call_target="tpu_custom_call", output_to_operand_aliasing={{0}: (1, {})} | custom-call | flops 352000016384 | bytes 1056000000 | tf_op jit(solution)/shard_map/attend_whole/pallas_call | solution.py:218
  79.7 5.6 collective-permute-start.9
  104.2 14.1 %collective-permute-start.15 = (bf16[1152,1152]{1,0:T(8,128)(2,1)}, bf16[1152,1152]{1,0:T(8,128)(2,1)}, u32[]{:S(2)}, u32[]{:S(2)}) collective-permute-start(bf16[1152,1152]{1,0:T(8,128)(2,1)} %pad_maximum_fusion.3.refs_1_.refs_2_.refs_10_), channel_id=1, source_target_pairs={{0,4},{4,0},{8,12},{12,8},{16,20},{20,16},{24,28},{28,24},{1,5},{5... | collective-permute-start | bytes 7962632 | tf_op jit(solution)/shard_map/ppermute | solution.py:282
  127.7 10.0 %enter.1 = (f32[2,256,1152]{2,1,0:T(8,128)}, f32[2,256,1152]{2,1,0:T(8,128)}, bf16[2,256,1152]{2,1,0:T(8,128)(2,1)}, bf16[2,256,1152]{2,1,0:T(8,128)(2,1)}, bf16...) custom-call(s32[8]{0:T(128)} %get-tuple-element.51.info_ref.refs_0_, ...), custom_call_target="tpu_custom_call" | custom-call | flops 198000001024 | bytes 594000000 | tf_op jit(solution)/shard_map/enter/pallas_call | solution.py:218
  144.9 19.4 %collective-permute-done.17.refs_15_ = bf16[1152,1152]{1,0:T(8,128)(2,1)} collective-permute-done((bf16[1152,1152]{1,0:T(8,128)(2,1)}, bf16[1152,1152]{1,0:T(8,128)(2,1)}, u32[]{:S(2)}, u32[]{:S(2)}) %collective-permute-start.17) | collective-permute-done | bytes 2654240 | tf_op jit(solution)/shard_map/ppermute | solution.py:286
  165.1 16.8 %expand.1 = (bf16[512,4608]{1,0:T(8,128)(2,1)}, bf16[512,4608]{1,0:T(8,128)(2,1)}) custom-call(bf16[512,1152]{1,0:T(8,128)(2,1)} %bitcast.213, f32[1,4608]{1,0:T(1,128)} %reshape.230.refs_1_, bf16[1152,1152]{1,0:T(8,128)(2,1)} %pad_maximum_fusion.3.refs_1_.refs_2_.refs_10_, bf16[1152,1152]{1,0:T(8,128)(2,1)} %hold.41.refs_3_.refs_11_, ...), custom_call_target="tpu_custom_call" | custom-call | flops 439999987712 | bytes 1320000000 | tf_op jit(solution)/shard_map/expand/pallas_call | solution.py:218
  181.9 15.1 %unit_grads.2 = (bf16[1152,1152]{1,0:T(8,128)(2,1)}, bf16[1152,1152]{1,0:T(8,128)(2,1)}, bf16[1152,1152]{1,0:T(8,128)(2,1)}, bf16[1152,1152]{1,0:T(8,128)(2,1)}) custom-call(bf16[512,4608]{1,0:T(8,128)(2,1)} %get-tuple-element.61.refs_0_.refs_4_, bf16[512,1152]{1,0:T(8,128)(2,1)} %bitcast.239, bf16[1152,1152]{1,0:T(8,128)(2,1)} %collective-permute-done.18.refs_2_.refs_16_), custom_call_target="tpu_custom_call" | custom-call | flops 307999997952 | bytes 924000000 | tf_op jit(solution)/shard_map/unit_grads/pallas_call | solution.py:218
  197.6 35.0 %contract.1 = (bf16[512,4608]{1,0:T(8,128)(2,1)}, f32[1,4608]{1,0:T(1,128)}, bf16[4,2,256,288]{3,2,1,0:T(8,128)(2,1)}, f32[2,256,1152]{2,1,0:T(8,128)}, bf16[2,2...) custom-call(s32[8]{0:T(128)} %get-tuple-element.51.info_ref.refs_0_, ...), custom_call_target="tpu_custom_call" | custom-call | flops 968000012288 | bytes 2904000000 | tf_op jit(solution)/shard_map/contract/pallas_call | solution.py:218
  245.1 15.3 %unit_grads.3 = (bf16[1152,1152]{1,0:T(8,128)(2,1)}, bf16[1152,1152]{1,0:T(8,128)(2,1)}, bf16[1152,1152]{1,0:T(8,128)(2,1)}, bf16[1152,1152]{1,0:T(8,128)(2,1)}) custom-call(bf16[512,4608]{1,0:T(8,128)(2,1)} %get-tuple-element.69.refs_1_.refs_0_, bf16[512,1152]{1,0:T(8,128)(2,1)} %bitcast.214, bf16[1152,1152]{1,0:T(8,128)(2,1)} %add_convert_fusion.5.refs_2_), custom_call_target="tpu_custom_call" | custom-call | flops 307999997952 | bytes 924000000 | tf_op jit(solution)/shard_map/unit_grads/pallas_call | solution.py:218
  266.2 8.2 %attend_back_split.1 = bf16[1,1024,864]{2,1,0:T(8,128)(2,1)} custom-call(bf16[2,1024,864]{2,1,0:T(8,128)(2,1)} %bitcast.187, f32[1,4,1024]{2,1,0:T(4,128)} %get-tuple-element.56.refs_1_.lse_ref, bf16[4,2,288,256]{3,2,1,0:T(8,128)(2,1)} %pad_maximum_fusion.17.refs_1_.pieces_ref.refs_2_), custom_call_target="tpu_custom_call" | custom-call | flops 176000008192 | bytes 528000000 | tf_op jit(solution)/shard_map/attend_back_split/pallas_call | solution.py:218
  294.9 9.8 %leave.2 = (bf16[4,288,2048]{2,1,0:T(8,128)(2,1)}, f32[4,2,1152]{2,1,0:T(2,128)}) custom-call(s32[8]{0:T(128)} %get-tuple-element.51.info_ref.refs_0_, f32[8,6912]{1,0:T(8,128)} %get-tuple-element.53.refs_1_, bf16[1024,864]{1,0:T(8,128)(2,1)} %bitcast.206, bf16[864,1152]{1,0:T(8,128)(2,1)} %bitcast.237, bf16[2048,1152]{1,0:T(8,128)(2,1)} %refs_4_.3, ...), custom_call_target="tpu_custom_call" | custom-call | flops 198000001024 | bytes 594000000 | tf_op jit(solution)/shard_map/leave/pallas_call | solution.py:218
  311.1 17.8 %attend_back_whole.1 = bf16[1,1024,864]{2,1,0:T(8,128)(2,1)} custom-call(bf16[2,1024,864]{2,1,0:T(8,128)(2,1)} %bitcast.188, f32[1,4,1024]{2,1,0:T(4,128)} %get-tuple-element.58.refs_1_, bf16[4,2,288,256]{3,2,1,0:T(8,128)(2,1)} %pad_maximum_fusion.17.refs_1_.pieces_ref.refs_2_, f32[4,2,1152]{2,1,0:T(2,128)} %get-tuple-element.78.refs_3_, ...), custom_call_target="tpu_custom_call" | custom-call | flops 527999991808 | bytes 1584000000 | tf_op jit(solution)/shard_map/attend_back_whole/pallas_call | solution.py:218
  328.9 5.8 %collective-permute-done.57.refs_0_ = bf16[144,1152]{1,0:T(8,128)(2,1)} collective-permute-done((bf16[144,1152]{1,0:T(8,128)(2,1)}, bf16[144,1152]{1,0:T(8,128)(2,1)}, u32[]{:S(2)}, u32[]{:S(2)}) %collective-permute-start.57) | collective-permute-done | bytes 331808 | tf_op jit(solution)/shard_map/ppermute | solution.py:257
  359.3 5.5 collective-permute-start.61
  368.6 9.8 %leave.3 = (bf16[4,288,2048]{2,1,0:T(8,128)(2,1)}, f32[4,2,1152]{2,1,0:T(2,128)}) custom-call(s32[8]{0:T(128)} %get-tuple-element.51.info_ref.refs_0_, f32[8,6912]{1,0:T(8,128)} %get-tuple-element.53.refs_1_, bf16[1024,864]{1,0:T(8,128)(2,1)} %bitcast.180, bf16[864,1152]{1,0:T(8,128)(2,1)} %bitcast.238, ...), custom_call_target="tpu_custom_call", output_to_operand_aliasing={{0}: (6, {})} | custom-call | flops 198000001024 | bytes 594000000 | tf_op jit(solution)/shard_map/leave/pallas_call | solution.py:218
  403.6 9.7 %convolution_convert_fusion = bf16[864,1152]{1,0:T(8,128)(2,1)} fusion(bf16[2048,864]{1,0:T(8,128)(2,1)} %hold.57, bf16[2048,1152]{1,0:T(8,128)(2,1)} %get-tuple-element.86), kind=kOutput, calls=%fused_computation.26 | convolution fusion | flops 4077858816 | bytes 10248192 | tf_op jit(solution)/shard_map/dot_general | solution.py:170
  425.4 7.0 %reduce-scatter.3.cloned.1.call-done.refs_1_ = bf16[144,1152]{1,0:T(8,128)(2,1)} async-done(((bf16[576,1152]{1,0:T(8,128)(2,1)}), bf16[144,1152]{1,0:T(8,128)(2,1)}) %reduce-scatter.3.cloned.1.call-update) | async-done | bytes 331792 | tf_op jit(solution)/shard_map/reduce_scatter | solution.py:911
  443.2 8.5 %collective-permute-done.38 = f32[2,8,1728]{2,1,0:T(8,128)S(1)} collective-permute-done((f32[2,8,1728]{2,1,0:T(8,128)S(1)}, f32[2,8,1728]{2,1,0:T(8,128)S(1)}, u32[]{:S(2)}, u32[]{:S(2)}) %collective-permute-start.38) | collective-permute-done | bytes 110624 | tf_op jit(solution)/shard_map/ppermute | solution.py:286
  479.6 11.0 %collective-permute-done.48 = bf16[40,1152]{1,0:T(8,128)(2,1)S(1)} collective-permute-done((bf16[40,1152]{1,0:T(8,128)(2,1)S(1)}, bf16[40,1152]{1,0:T(8,128)(2,1)S(1)}, u32[]{:S(2)}, u32[]{:S(2)}) %collective-permute-start.48) | collective-permute-done | bytes 92192 | tf_op jit(solution)/shard_map/ppermute | solution.py:257
  505.5 5.3 collective-permute-done.54
  529.0 7.4 %place_columns.1 = f32[1152,1152]{1,0:T(8,128)} custom-call(bf16[8,144,1152]{2,1,0:T(8,128)(2,1)} %pad_maximum_fusion.5.slices_ref), custom_call_target="tpu_custom_call" | custom-call | tf_op jit(solution)/shard_map/place_columns/pallas_call | solution.py:218
  (455 shorter events, 267.8 us)
Async XLA Ops:
  7.2 55.4 %all-gather.3.cloned.1.call-start = ((), (), s32[]{:S(2)}) async-start(), calls=%async_computation.2 | async-start | bytes 1658880 | tf_op jit(solution)/shard_map/all_gather | solution.py:740
  10.2 80.4 %all-gather.5.cloned.1.call-start = ((), (), s32[]{:S(2)}) async-start(), calls=%async_computation.3 | async-start | bytes 1658880 | tf_op jit(solution)/shard_map/all_gather | solution.py:741
  22.0 410.4 %reduce-scatter.3.cloned.1.call-start = ((), (), s32[]{:S(2)}) async-start(), calls=%async_computation.4 | async-start | bytes 1658880 | tf_op jit(solution)/shard_map/reduce_scatter | solution.py:911
  90.6 32.9 %collective-permute-start.13 = (bf16[576,1152]{1,0:T(8,128)(2,1)}, bf16[576,1152]{1,0:T(8,128)(2,1)}, u32[]{:S(2)}, u32[]{:S(2)}) collective-permute-start(bf16[576,1152]{1,0:T(8,128)(2,1)} %hold.33.refs_1_), channel_id=1, source_target_pairs={{0,16},{4,12},{8,24},{12,4},{16,0},{20,28},{24,8},{28,20},{1,17},{... | collective-permute-start | bytes 3981320 | tf_op jit(solution)/shard_map/ppermute | solution.py:286
  98.6 39.1 %collective-permute-start.14 = (bf16[1152,1152]{1,0:T(8,128)(2,1)}, bf16[1152,1152]{1,0:T(8,128)(2,1)}, u32[]{:S(2)}, u32[]{:S(2)}) collective-permute-start(bf16[1152,1152]{1,0:T(8,128)(2,1)} %pad_maximum_fusion.3.refs_1_.refs_2_.refs_10_), channel_id=1, source_target_pairs={{0,8},{4,20},{8,0},{12,28},{16,24},{20,4},{24,16},{28,12},{1,9},{5... | collective-permute-start | bytes 7962632 | tf_op jit(solution)/shard_map/ppermute | solution.py:286
  104.2 60.9 %collective-permute-start.15 = (bf16[1152,1152]{1,0:T(8,128)(2,1)}, bf16[1152,1152]{1,0:T(8,128)(2,1)}, u32[]{:S(2)}, u32[]{:S(2)}) collective-permute-start(bf16[1152,1152]{1,0:T(8,128)(2,1)} %pad_maximum_fusion.3.refs_1_.refs_2_.refs_10_), channel_id=1, source_target_pairs={{0,4},{4,0},{8,12},{12,8},{16,20},{20,16},{24,28},{28,24},{1,5},{5... | collective-permute-start | bytes 7962632 | tf_op jit(solution)/shard_map/ppermute | solution.py:282
  126.5 37.9 %collective-permute-start.17 = (bf16[1152,1152]{1,0:T(8,128)(2,1)}, bf16[1152,1152]{1,0:T(8,128)(2,1)}, u32[]{:S(2)}, u32[]{:S(2)}) collective-permute-start(bf16[1152,1152]{1,0:T(8,128)(2,1)} %pad_maximum_fusion.4.refs_7_.refs_6_.refs_14_), channel_id=1, source_target_pairs={{0,8},{4,20},{8,0},{12,28},{16,24},{20,4},{24,16},{28,12},{1,9},{5... | collective-permute-start | bytes 7962632 | tf_op jit(solution)/shard_map/ppermute | solution.py:286
  144.2 37.6 %collective-permute-start.18 = (bf16[1152,1152]{1,0:T(8,128)(2,1)}, bf16[1152,1152]{1,0:T(8,128)(2,1)}, u32[]{:S(2)}, u32[]{:S(2)}) collective-permute-start(bf16[1152,1152]{1,0:T(8,128)(2,1)} %pad_maximum_fusion.4.refs_7_.refs_6_.refs_14_), channel_id=1, source_target_pairs={{0,4},{4,0},{8,12},{12,8},{16,20},{20,16},{24,28},{28,24},{1,5},{5... | collective-permute-start | bytes 7962632 | tf_op jit(solution)/shard_map/ppermute | solution.py:282
  164.4 33.2 %collective-permute-start.19 = (bf16[1152,1152]{1,0:T(8,128)(2,1)}, bf16[1152,1152]{1,0:T(8,128)(2,1)}, u32[]{:S(2)}, u32[]{:S(2)}) collective-permute-start(bf16[1152,1152]{1,0:T(8,128)(2,1)} %collective-permute-done.17.refs_15_), channel_id=1, source_target_pairs={{0,4},{4,0},{8,12},{12,8},{16,20},{20,16},{24,28},{28,24},{1,5},{5... | collective-permute-start | bytes 7962632 | tf_op jit(solution)/shard_map/ppermute | solution.py:282
  197.0 77.4 %collective-permute-start.27 = (bf16[1152,1152]{1,0:T(8,128)(2,1)}, bf16[1152,1152]{1,0:T(8,128)(2,1)}, u32[]{:S(2)}, u32[]{:S(2)}) collective-permute-start(bf16[1152,1152]{1,0:T(8,128)(2,1)} %get-tuple-element.77), channel_id=1, source_target_pairs={{0,4},{4,0},{8,12},{12,8},{16,20},{20,16},{24,28},{28,24},{1,5},{5... | collective-permute-start | bytes 7962632 | tf_op jit(solution)/shard_map/ppermute | solution.py:282
  197.1 41.4 %collective-permute-start.21 = (bf16[1152,1152]{1,0:T(8,128)(2,1)}, bf16[1152,1152]{1,0:T(8,128)(2,1)}, u32[]{:S(2)}, u32[]{:S(2)}) collective-permute-start(bf16[1152,1152]{1,0:T(8,128)(2,1)} %get-tuple-element.71), channel_id=1, source_target_pairs={{0,4},{4,0},{8,12},{12,8},{16,20},{20,16},{24,28},{28,24},{1,5},{5... | collective-permute-start | bytes 7962632 | tf_op jit(solution)/shard_map/ppermute | solution.py:282
  244.1 31.5 %collective-permute-start.28 = (bf16[1152,1152]{1,0:T(8,128)(2,1)}, bf16[1152,1152]{1,0:T(8,128)(2,1)}, u32[]{:S(2)}, u32[]{:S(2)}) collective-permute-start(bf16[1152,1152]{1,0:T(8,128)(2,1)} %add_convert_fusion.5.refs_2_), channel_id=1, source_target_pairs={{0,8},{4,20},{8,0},{12,28},{16,24},{20,4},{24,16},{28,12},{1,9},{5... | collective-permute-start | bytes 7962632 | tf_op jit(solution)/shard_map/ppermute | solution.py:286
  260.4 27.8 %collective-permute-start.26 = (bf16[1152,1152]{1,0:T(8,128)(2,1)}, bf16[1152,1152]{1,0:T(8,128)(2,1)}, u32[]{:S(2)}, u32[]{:S(2)}) collective-permute-start(bf16[1152,1152]{1,0:T(8,128)(2,1)} %get-tuple-element.76), channel_id=1, source_target_pairs={{0,4},{4,0},{8,12},{12,8},{16,20},{20,16},{24,28},{28,24},{1,5},{5... | collective-permute-start | bytes 7962632 | tf_op jit(solution)/shard_map/ppermute | solution.py:282
  294.0 70.8 %collective-permute-start.30 = (bf16[1152,1152]{1,0:T(8,128)(2,1)}, bf16[1152,1152]{1,0:T(8,128)(2,1)}, u32[]{:S(2)}, u32[]{:S(2)}) collective-permute-start(bf16[1152,1152]{1,0:T(8,128)(2,1)} %add_convert_fusion.3.refs_7_), channel_id=1, source_target_pairs={{0,8},{4,20},{8,0},{12,28},{16,24},{20,4},{24,16},{28,12},{1,9},{5... | collective-permute-start | bytes 7962632 | tf_op jit(solution)/shard_map/ppermute | solution.py:286
  310.9 28.2 %collective-permute-start.58 = (bf16[144,1152]{1,0:T(8,128)(2,1)}, bf16[144,1152]{1,0:T(8,128)(2,1)}, u32[]{:S(2)}, u32[]{:S(2)}) collective-permute-start(bf16[144,1152]{1,0:T(8,128)(2,1)} %get-tuple-element.136), channel_id=1, source_target_pairs={{0,3},{1,0},{2,1},{3,2},{4,7},{5,4},{6,5},{7,6},{8,11},{9,8},{10,9... | collective-permute-start | bytes 995336 | tf_op jit(solution)/shard_map/ppermute | solution.py:257
  352.1 27.7 %collective-permute-start.24 = (bf16[2,256,288]{2,1,0:T(8,128)(2,1)}, bf16[2,256,288]{2,1,0:T(8,128)(2,1)}, u32[]{:S(2)}, u32[]{:S(2)}) collective-permute-start(bf16[2,256,288]{2,1,0:T(8,128)(2,1)} %get-tuple-element.134), channel_id=1, source_target_pairs={{0,1},{1,2},{2,3},{3,0},{4,5},{5,6},{6,7},{7,4},{8,9},{9,10},{10,1... | collective-permute-start | bytes 884744 | tf_op jit(solution)/shard_map/ppermute | solution.py:257
  352.1 31.4 %collective-permute-start.31 = (bf16[2,256,288]{2,1,0:T(8,128)(2,1)}, bf16[2,256,288]{2,1,0:T(8,128)(2,1)}, u32[]{:S(2)}, u32[]{:S(2)}) collective-permute-start(bf16[2,256,288]{2,1,0:T(8,128)(2,1)} %get-tuple-element.133), channel_id=1, source_target_pairs={{0,2},{1,3},{2,0},{3,1},{4,6},{5,7},{6,4},{7,5},{8,10},{9,11},{10,... | collective-permute-start | bytes 884744 | tf_op jit(solution)/shard_map/ppermute | solution.py:257
  352.1 33.4 %collective-permute-start.32 = (bf16[2,256,288]{2,1,0:T(8,128)(2,1)}, bf16[2,256,288]{2,1,0:T(8,128)(2,1)}, u32[]{:S(2)}, u32[]{:S(2)}) collective-permute-start(bf16[2,256,288]{2,1,0:T(8,128)(2,1)} %get-tuple-element.132), channel_id=1, source_target_pairs={{0,3},{1,0},{2,1},{3,2},{4,7},{5,4},{6,5},{7,6},{8,11},{9,8},{10,9... | collective-permute-start | bytes 884744 | tf_op jit(solution)/shard_map/ppermute | solution.py:257
  359.3 76.5 %collective-permute-start.61 = (bf16[4,144,1152]{2,1,0:T(8,128)(2,1)}, bf16[4,144,1152]{2,1,0:T(8,128)(2,1)}, u32[]{:S(2)}, u32[]{:S(2)}) collective-permute-start(bf16[4,144,1152]{2,1,0:T(8,128)(2,1)} %pad_maximum_fusion.11), channel_id=1, source_target_pairs={{0,4},{4,0},{8,12},{12,8},{16,20},{20,16},{24,28},{28,24},{1,5},{5... | collective-permute-start | bytes 3981320 | tf_op jit(solution)/shard_map/ppermute | solution.py:282
  399.7 148.9 %reduce-scatter.5.cloned.1.call-start = ((), (), s32[]{:S(2)}) async-start(), calls=%async_computation.5 | async-start | bytes 5898240 | tf_op jit(solution)/shard_map/reduce_scatter | solution.py:911
  423.7 31.2 %collective-permute-start.43 = (bf16[544,1152]{1,0:T(8,128)(2,1)}, bf16[544,1152]{1,0:T(8,128)(2,1)}, u32[]{:S(2)}, u32[]{:S(2)}) collective-permute-start(bf16[544,1152]{1,0:T(8,128)(2,1)} %bitcast.212), channel_id=1, source_target_pairs={{0,4},{4,0},{8,12},{12,8},{16,20},{20,16},{24,28},{28,24},{1,5},{5... | collective-permute-start | bytes 3760136 | tf_op jit(solution)/shard_map/ppermute | solution.py:282
  469.7 51.6 %collective-permute-start.40 = (bf16[72,1152]{1,0:T(8,128)(2,1)S(1)}, bf16[72,1152]{1,0:T(8,128)(2,1)S(1)}, u32[]{:S(2)}, u32[]{:S(2)}) collective-permute-start(bf16[72,1152]{1,0:T(8,128)(2,1)S(1)} %maximum_maximum_fusion.1), channel_id=1, source_target_pairs={{1,0},{2,1},{3,2},{0,3},{5,4},{6,5},{7,6},{4,7},{9,8},{10,9},{11,1... | collective-permute-start | bytes 497672 | tf_op jit(solution)/shard_map/ppermute | solution.py:253
  471.2 50.1 %collective-permute-start.41 = (bf16[72,1152]{1,0:T(8,128)(2,1)S(1)}, bf16[72,1152]{1,0:T(8,128)(2,1)S(1)}, u32[]{:S(2)}, u32[]{:S(2)}) collective-permute-start(bf16[72,1152]{1,0:T(8,128)(2,1)S(1)} %maximum_maximum_fusion.1), channel_id=1, source_target_pairs={{2,0},{3,1},{0,2},{1,3},{6,4},{7,5},{4,6},{5,7},{10,8},{11,9},{8,1... | collective-permute-start | bytes 497672 | tf_op jit(solution)/shard_map/ppermute | solution.py:253
  475.9 45.4 %collective-permute-start.42 = (bf16[72,1152]{1,0:T(8,128)(2,1)S(1)}, bf16[72,1152]{1,0:T(8,128)(2,1)S(1)}, u32[]{:S(2)}, u32[]{:S(2)}) collective-permute-start(bf16[72,1152]{1,0:T(8,128)(2,1)S(1)} %maximum_maximum_fusion.1), channel_id=1, source_target_pairs={{3,0},{0,1},{1,2},{2,3},{7,4},{4,5},{5,6},{6,7},{11,8},{8,9},{9,10... | collective-permute-start | bytes 497672 | tf_op jit(solution)/shard_map/ppermute | solution.py:253
  (107 other events, 1087.8 us)
Sparse Core Ops, SparseCore 0:
  10.3 42.8 all-gather.2
  54.7 33.9 all-gather.4
  399.8 32.5 reduce-scatter.2
  434.5 106.6 reduce-scatter.4

commit v6 on v5

--- a/solution.py
+++ b/solution.py
@@ -552,9 +552,9 @@
         grad_out = tokens_buf[row_at(row, info_ref)].astype(jnp.float32)
         stream = stream_buf[row]
         mlp = mlp_acc[here, :] + out_bias_ref[...]
-        block = (stream + mod(5) * mlp).astype(jnp.bfloat16)
+        block = (stream + mod(5) * mlp).T.astype(jnp.bfloat16)
         for other in range(heads):
-            block_ref[(other - head + heads) % heads, row] = block[:, other * share : (other + 1) * share]
+            block_ref[(other - head + heads) % heads, row] = block[other * share : (other + 1) * share]
         normed, inverse = row_norm(stream.astype(jnp.bfloat16).astype(jnp.float32))
         grad_in = grad_acc[here, :]
         sums_ref[row, 1:2] = jnp.sum(grad_in, axis=0, keepdims=True)
@@ -680,11 +680,16 @@
 
 
 def lay_home_kernel(heads, info_ref, blocks_ref, out_ref):
-    home = blocks_ref.shape[2]
+    home = blocks_ref.shape[3]
     head = lax.axis_index("head")
-    for spot in range(heads):
-        for row in range(2):
-            out_ref[row_at(row, info_ref), spot * home : (spot + 1) * home, :] = blocks_ref[(head - spot + heads) % heads, row]
+    for split_row in range(2):
+
+        @pl.when(info_ref[0] == split_row)
+        def _(split_row=split_row):
+            for spot in range(heads):
+                for row in range(2):
+                    at = (split_row ^ row) * SEQ + spot * home
+                    out_ref[:, at : at + home] = blocks_ref[(head - spot + heads) % heads, row]
 
 
 def shards(
@@ -859,7 +864,7 @@
         [
             shape_of((home_count, unit_count), low),
             shape_of((1, unit_count), full),
-            shape_of((heads, rows, home, share), low),
+            shape_of((heads, rows, share, home), low),
             shape_of((rows, home, width), full),
             shape_of((rows, home, width), low),
             shape_of((heads, rows, share, home), low),
@@ -871,7 +876,7 @@
         [
             pl.BlockSpec(memory_space=pl.ANY),
             whole((1, unit_count)),
-            by_head,
+            whole((heads, rows, share, home)),
             stay,
             stay,
             whole((heads, rows, share, home)),
@@ -973,13 +978,13 @@
     )
     block_out = call(
         functools.partial(lay_home_kernel, heads),
-        shape_of((rows, SEQ, share), low),
-        [whole((heads, rows, home, share))],
-        whole((rows, SEQ, share)),
+        shape_of((share, token_count), low),
+        [whole((heads, rows, share, home))],
+        whole((share, token_count)),
         prefetch=1,
         name="lay_home", micros=0,
         order=[sums_row],
-    )(info, block_home).reshape(token_count, share)
+    )(info, block_home).T
 
     home_quarter = lax.axis_index("head") * home // quarter
     seg_spots = lax.broadcasted_iota(jnp.int32, (5, 1), 0)

time: 568 us -> 567 us (level)
    ppermute x15, waiting for transfers between devices: 32.3 us -> 26 us  [send(): lax.ppermute(values, 'head', [(i, (i + distance) % count) for i in range(...]
    ppermute x20, waiting for transfers between devices: 48.7 us -> 55 us  [link_swap(): return lax.ppermute(values, 'batch', pairs)]
    unnamed x150 -> x149, local copies, waits for them, and re-layouts: 14.2 us -> 11.7 us
  transfers between devices with their start and end apart: 66 -> 66, of which waited for: 25 -> 22; matrix products, arithmetic and copies ran while one was open for 25% -> 24% of each run, Pallas kernels for 35% -> 35%
where the time goes in v6:
time: 567 us; the launch traced here: 559 us
  Pallas kernels  197 us (35%)
  waiting for transfers between devices  108 us (19%)
  starting transfers between devices  88 us (16%)
  other arithmetic  83.5 us (15%)
  local copies, waits for them, and re-layouts  45.8 us (8%)
  matrix products  21.4 us (4%)
  between operations  15.4 us (3%)
    pallas_call x18, Pallas kernels, call(): return lambda *arrays: run(*arrays, *order)  197 us
    ppermute x20, waiting for transfers between devices, link_swap(): return lax.ppermute(values, 'batch', pairs)  55 us
    ppermute x15, starting transfers between devices, core_swap(): lax.ppermute(values, 'batch', [(i, i ^ 1) for i in range(self.batches)])  42 us
    ppermute x15, waiting for transfers between devices, send(): lax.ppermute(values, 'head', [(i, (i + distance) % count) for i in range(...  26 us
    ppermute x12, waiting for transfers between devices, fetch(): lax.ppermute(values, 'head', [((i + distance) % count, i) for i in range(...  18.3 us
    dot_general x3, matrix products, tn(): lax.dot_general(left_side, right_side, (((0,), (0,)), ((), ())), preferre...  17.4 us
    ppermute x20, starting transfers between devices, link_swap(): return lax.ppermute(values, 'batch', pairs)  17.4 us
    ppermute x12, starting transfers between devices, fetch(): lax.ppermute(values, 'head', [((i + distance) % count, i) for i in range(...  16 us
  transfers between devices with their start and end apart: 66, of which 22 were waited for; matrix products, arithmetic and copies ran while one was open for 24% of the time, Pallas kernels for 35%

profile of v6, /device:TPU:9, one launch (start us, length us, event | category | flops | bytes accessed | tf_op | source)
XLA Modules:
  0.0 559.3 jit_solution(17895537842466113188)
XLA Ops:
  30.8 11.6 %project.1 = (bf16[2048,1152]{1,0:T(8,128)(2,1)}, bf16[2048,864]{1,0:T(8,128)(2,1)}, f32[8,6912]{1,0:T(8,128)}) custom-call(s32[8]{0:T(128)} %get-tuple-element.51.info_ref.refs_0_, f32[4,8,1728]{2,1,0:T(8,128)} %pad_maximum_fusion.24.table_rel_ref.refs_1_, bf16[2048,1152]{1,0:T(8,128)(2,1)} %refs_4_.3, bf16[864,1152]{1,0:T(8,128)(2,1)} %bitcast.236, ...), custom_call_target="tpu_custom_call" | custom-call | flops 285999988736 | bytes 858000000 | tf_op jit(solution)/shard_map/project/pallas_call | solution.py:218
  51.4 7.2 %attend_split.1 = (bf16[4,2,288,256]{3,2,1,0:T(8,128)(2,1)}, f32[1,4,1024]{2,1,0:T(4,128)}) custom-call(bf16[2,1024,864]{2,1,0:T(8,128)(2,1)} %bitcast.185), custom_call_target="tpu_custom_call" | custom-call | flops 131999997952 | bytes 396000000 | tf_op jit(solution)/shard_map/attend_split/pallas_call | solution.py:218
  62.8 14.5 %attend_whole.1 = (bf16[4,2,288,256]{3,2,1,0:T(8,128)(2,1)}, f32[1,4,1024]{2,1,0:T(4,128)}) custom-call(bf16[2,1024,864]{2,1,0:T(8,128)(2,1)} %bitcast.186, bf16[4,2,288,256]{3,2,1,0:T(8,128)(2,1)} %get-tuple-element.55.refs_1_, bf16[576,1152]{1,0:T(8,128)(2,1)} %hold.31.refs_2_), custom_call_target="tpu_custom_call", output_to_operand_aliasing={{0}: (1, {})} | custom-call | flops 352000016384 | bytes 1056000000 | tf_op jit(solution)/shard_map/attend_whole/pallas_call | solution.py:218
  79.7 5.6 collective-permute-start.9
  104.2 14.1 %collective-permute-start.15 = (bf16[1152,1152]{1,0:T(8,128)(2,1)}, bf16[1152,1152]{1,0:T(8,128)(2,1)}, u32[]{:S(2)}, u32[]{:S(2)}) collective-permute-start(bf16[1152,1152]{1,0:T(8,128)(2,1)} %pad_maximum_fusion.3.refs_1_.refs_2_.refs_10_), channel_id=1, source_target_pairs={{0,4},{4,0},{8,12},{12,8},{16,20},{20,16},{24,28},{28,24},{1,5},{5... | collective-permute-start | bytes 7962632 | tf_op jit(solution)/shard_map/ppermute | solution.py:282
  127.7 10.0 %enter.1 = (f32[2,256,1152]{2,1,0:T(8,128)}, f32[2,256,1152]{2,1,0:T(8,128)}, bf16[2,256,1152]{2,1,0:T(8,128)(2,1)}, bf16[2,256,1152]{2,1,0:T(8,128)(2,1)}, bf16...) custom-call(s32[8]{0:T(128)} %get-tuple-element.51.info_ref.refs_0_, ...), custom_call_target="tpu_custom_call" | custom-call | flops 198000001024 | bytes 594000000 | tf_op jit(solution)/shard_map/enter/pallas_call | solution.py:218
  145.0 19.4 %collective-permute-done.17.refs_15_ = bf16[1152,1152]{1,0:T(8,128)(2,1)} collective-permute-done((bf16[1152,1152]{1,0:T(8,128)(2,1)}, bf16[1152,1152]{1,0:T(8,128)(2,1)}, u32[]{:S(2)}, u32[]{:S(2)}) %collective-permute-start.17) | collective-permute-done | bytes 2654240 | tf_op jit(solution)/shard_map/ppermute | solution.py:286
  165.1 16.8 %expand.1 = (bf16[512,4608]{1,0:T(8,128)(2,1)}, bf16[512,4608]{1,0:T(8,128)(2,1)}) custom-call(bf16[512,1152]{1,0:T(8,128)(2,1)} %bitcast.212, f32[1,4608]{1,0:T(1,128)} %reshape.227.refs_1_, bf16[1152,1152]{1,0:T(8,128)(2,1)} %pad_maximum_fusion.3.refs_1_.refs_2_.refs_10_, bf16[1152,1152]{1,0:T(8,128)(2,1)} %hold.41.refs_3_.refs_11_, ...), custom_call_target="tpu_custom_call" | custom-call | flops 439999987712 | bytes 1320000000 | tf_op jit(solution)/shard_map/expand/pallas_call | solution.py:218
  181.9 15.1 %unit_grads.2 = (bf16[1152,1152]{1,0:T(8,128)(2,1)}, bf16[1152,1152]{1,0:T(8,128)(2,1)}, bf16[1152,1152]{1,0:T(8,128)(2,1)}, bf16[1152,1152]{1,0:T(8,128)(2,1)}) custom-call(bf16[512,4608]{1,0:T(8,128)(2,1)} %get-tuple-element.61.refs_0_.refs_4_, bf16[512,1152]{1,0:T(8,128)(2,1)} %bitcast.239, bf16[1152,1152]{1,0:T(8,128)(2,1)} %collective-permute-done.18.refs_2_.refs_16_), custom_call_target="tpu_custom_call" | custom-call | flops 307999997952 | bytes 924000000 | tf_op jit(solution)/shard_map/unit_grads/pallas_call | solution.py:218
  197.6 34.8 %contract.1 = (bf16[512,4608]{1,0:T(8,128)(2,1)}, f32[1,4608]{1,0:T(1,128)}, bf16[4,2,288,256]{3,2,1,0:T(8,128)(2,1)}, f32[2,256,1152]{2,1,0:T(8,128)}, bf16[2,2...) custom-call(s32[8]{0:T(128)} %get-tuple-element.51.info_ref.refs_0_, ...), custom_call_target="tpu_custom_call" | custom-call | flops 968000012288 | bytes 2904000000 | tf_op jit(solution)/shard_map/contract/pallas_call | solution.py:218
  244.9 15.3 %unit_grads.3 = (bf16[1152,1152]{1,0:T(8,128)(2,1)}, bf16[1152,1152]{1,0:T(8,128)(2,1)}, bf16[1152,1152]{1,0:T(8,128)(2,1)}, bf16[1152,1152]{1,0:T(8,128)(2,1)}) custom-call(bf16[512,4608]{1,0:T(8,128)(2,1)} %get-tuple-element.69.refs_1_.refs_0_, bf16[512,1152]{1,0:T(8,128)(2,1)} %bitcast.213, bf16[1152,1152]{1,0:T(8,128)(2,1)} %add_convert_fusion.5.refs_2_), custom_call_target="tpu_custom_call" | custom-call | flops 307999997952 | bytes 924000000 | tf_op jit(solution)/shard_map/unit_grads/pallas_call | solution.py:218
  266.0 8.2 %attend_back_split.1 = bf16[1,1024,864]{2,1,0:T(8,128)(2,1)} custom-call(bf16[2,1024,864]{2,1,0:T(8,128)(2,1)} %bitcast.187, f32[1,4,1024]{2,1,0:T(4,128)} %get-tuple-element.56.refs_1_.lse_ref, bf16[4,2,288,256]{3,2,1,0:T(8,128)(2,1)} %pad_maximum_fusion.16.refs_1_.pieces_ref.refs_2_), custom_call_target="tpu_custom_call" | custom-call | flops 176000008192 | bytes 528000000 | tf_op jit(solution)/shard_map/attend_back_split/pallas_call | solution.py:218
  294.7 9.8 %leave.2 = (bf16[4,288,2048]{2,1,0:T(8,128)(2,1)}, f32[4,2,1152]{2,1,0:T(2,128)}) custom-call(s32[8]{0:T(128)} %get-tuple-element.51.info_ref.refs_0_, f32[8,6912]{1,0:T(8,128)} %get-tuple-element.53.refs_1_, bf16[1024,864]{1,0:T(8,128)(2,1)} %bitcast.205, bf16[864,1152]{1,0:T(8,128)(2,1)} %bitcast.237, bf16[2048,1152]{1,0:T(8,128)(2,1)} %refs_4_.3, ...), custom_call_target="tpu_custom_call" | custom-call | flops 198000001024 | bytes 594000000 | tf_op jit(solution)/shard_map/leave/pallas_call | solution.py:218
  310.9 17.8 %attend_back_whole.1 = bf16[1,1024,864]{2,1,0:T(8,128)(2,1)} custom-call(bf16[2,1024,864]{2,1,0:T(8,128)(2,1)} %bitcast.188, f32[1,4,1024]{2,1,0:T(4,128)} %get-tuple-element.58.refs_1_, bf16[4,2,288,256]{3,2,1,0:T(8,128)(2,1)} %pad_maximum_fusion.16.refs_1_.pieces_ref.refs_2_, f32[4,2,1152]{2,1,0:T(2,128)} %get-tuple-element.78.refs_3_, ...), custom_call_target="tpu_custom_call" | custom-call | flops 527999991808 | bytes 1584000000 | tf_op jit(solution)/shard_map/attend_back_whole/pallas_call | solution.py:218
  328.6 5.9 %collective-permute-done.57.refs_0_ = bf16[144,1152]{1,0:T(8,128)(2,1)} collective-permute-done((bf16[144,1152]{1,0:T(8,128)(2,1)}, bf16[144,1152]{1,0:T(8,128)(2,1)}, u32[]{:S(2)}, u32[]{:S(2)}) %collective-permute-start.57) | collective-permute-done | bytes 331808 | tf_op jit(solution)/shard_map/ppermute | solution.py:257
  359.0 5.2 collective-permute-start.61
  368.2 9.8 %leave.3 = (bf16[4,288,2048]{2,1,0:T(8,128)(2,1)}, f32[4,2,1152]{2,1,0:T(2,128)}) custom-call(s32[8]{0:T(128)} %get-tuple-element.51.info_ref.refs_0_, f32[8,6912]{1,0:T(8,128)} %get-tuple-element.53.refs_1_, bf16[1024,864]{1,0:T(8,128)(2,1)} %bitcast.180, bf16[864,1152]{1,0:T(8,128)(2,1)} %bitcast.238, ...), custom_call_target="tpu_custom_call", output_to_operand_aliasing={{0}: (6, {})} | custom-call | flops 198000001024 | bytes 594000000 | tf_op jit(solution)/shard_map/leave/pallas_call | solution.py:218
  386.1 10.4 %collective-permute-done.33.refs_0_ = bf16[576,1152]{1,0:T(8,128)(2,1)} collective-permute-done((bf16[576,1152]{1,0:T(8,128)(2,1)}, bf16[576,1152]{1,0:T(8,128)(2,1)}, u32[]{:S(2)}, u32[]{:S(2)}) %collective-permute-start.33) | collective-permute-done | bytes 1327136 | tf_op jit(solution)/shard_map/ppermute | solution.py:286
  403.1 9.9 %convolution_convert_fusion = bf16[864,1152]{1,0:T(8,128)(2,1)} fusion(bf16[2048,864]{1,0:T(8,128)(2,1)} %hold.57, bf16[2048,1152]{1,0:T(8,128)(2,1)} %get-tuple-element.86), kind=kOutput, calls=%fused_computation.26 | convolution fusion | flops 4077858816 | bytes 10248192 | tf_op jit(solution)/shard_map/dot_general | solution.py:170
  424.2 7.7 %reduce-scatter.3.cloned.1.call-done.refs_1_ = bf16[144,1152]{1,0:T(8,128)(2,1)} async-done(((bf16[576,1152]{1,0:T(8,128)(2,1)}), bf16[144,1152]{1,0:T(8,128)(2,1)}) %reduce-scatter.3.cloned.1.call-update) | async-done | bytes 331792 | tf_op jit(solution)/shard_map/reduce_scatter | solution.py:916
  442.8 8.5 %collective-permute-done.38 = f32[2,8,1728]{2,1,0:T(8,128)S(1)} collective-permute-done((f32[2,8,1728]{2,1,0:T(8,128)S(1)}, f32[2,8,1728]{2,1,0:T(8,128)S(1)}, u32[]{:S(2)}, u32[]{:S(2)}) %collective-permute-start.38) | collective-permute-done | bytes 110624 | tf_op jit(solution)/shard_map/ppermute | solution.py:286
  478.0 11.0 %collective-permute-done.48 = bf16[40,1152]{1,0:T(8,128)(2,1)S(1)} collective-permute-done((bf16[40,1152]{1,0:T(8,128)(2,1)S(1)}, bf16[40,1152]{1,0:T(8,128)(2,1)S(1)}, u32[]{:S(2)}, u32[]{:S(2)}) %collective-permute-start.48) | collective-permute-done | bytes 92192 | tf_op jit(solution)/shard_map/ppermute | solution.py:257
  511.3 6.3 %collective-permute-start.55 = (bf16[4,144,1152]{2,1,0:T(8,128)(2,1)}, bf16[4,144,1152]{2,1,0:T(8,128)(2,1)}, u32[]{:S(2)}, u32[]{:S(2)}) collective-permute-start(bf16[4,144,1152]{2,1,0:T(8,128)(2,1)} %pad_maximum_fusion.9), channel_id=1, source_target_pairs={{0,4},{4,0},{8,12},{12,8},{16,20},{20,16},{24,28},{28,24},{1,5},{5... | collective-permute-start | bytes 3981320 | tf_op jit(solution)/shard_map/ppermute | solution.py:282
  529.9 7.5 %place_columns.1 = f32[1152,1152]{1,0:T(8,128)} custom-call(bf16[8,144,1152]{2,1,0:T(8,128)(2,1)} %pad_maximum_fusion.5.slices_ref), custom_call_target="tpu_custom_call" | custom-call | tf_op jit(solution)/shard_map/place_columns/pallas_call | solution.py:218
  (454 shorter events, 261.7 us)
Async XLA Ops:
  7.2 55.4 %all-gather.3.cloned.1.call-start = ((), (), s32[]{:S(2)}) async-start(), calls=%async_computation.2 | async-start | bytes 1658880 | tf_op jit(solution)/shard_map/all_gather | solution.py:745
  10.2 80.4 %all-gather.5.cloned.1.call-start = ((), (), s32[]{:S(2)}) async-start(), calls=%async_computation.3 | async-start | bytes 1658880 | tf_op jit(solution)/shard_map/all_gather | solution.py:746
  22.0 409.9 %reduce-scatter.3.cloned.1.call-start = ((), (), s32[]{:S(2)}) async-start(), calls=%async_computation.4 | async-start | bytes 1658880 | tf_op jit(solution)/shard_map/reduce_scatter | solution.py:916
  90.6 32.9 %collective-permute-start.13 = (bf16[576,1152]{1,0:T(8,128)(2,1)}, bf16[576,1152]{1,0:T(8,128)(2,1)}, u32[]{:S(2)}, u32[]{:S(2)}) collective-permute-start(bf16[576,1152]{1,0:T(8,128)(2,1)} %hold.33.refs_1_), channel_id=1, source_target_pairs={{0,16},{4,12},{8,24},{12,4},{16,0},{20,28},{24,8},{28,20},{1,17},{... | collective-permute-start | bytes 3981320 | tf_op jit(solution)/shard_map/ppermute | solution.py:286
  98.6 39.1 %collective-permute-start.14 = (bf16[1152,1152]{1,0:T(8,128)(2,1)}, bf16[1152,1152]{1,0:T(8,128)(2,1)}, u32[]{:S(2)}, u32[]{:S(2)}) collective-permute-start(bf16[1152,1152]{1,0:T(8,128)(2,1)} %pad_maximum_fusion.3.refs_1_.refs_2_.refs_10_), channel_id=1, source_target_pairs={{0,8},{4,20},{8,0},{12,28},{16,24},{20,4},{24,16},{28,12},{1,9},{5... | collective-permute-start | bytes 7962632 | tf_op jit(solution)/shard_map/ppermute | solution.py:286
  104.2 60.9 %collective-permute-start.15 = (bf16[1152,1152]{1,0:T(8,128)(2,1)}, bf16[1152,1152]{1,0:T(8,128)(2,1)}, u32[]{:S(2)}, u32[]{:S(2)}) collective-permute-start(bf16[1152,1152]{1,0:T(8,128)(2,1)} %pad_maximum_fusion.3.refs_1_.refs_2_.refs_10_), channel_id=1, source_target_pairs={{0,4},{4,0},{8,12},{12,8},{16,20},{20,16},{24,28},{28,24},{1,5},{5... | collective-permute-start | bytes 7962632 | tf_op jit(solution)/shard_map/ppermute | solution.py:282
  126.5 37.9 %collective-permute-start.17 = (bf16[1152,1152]{1,0:T(8,128)(2,1)}, bf16[1152,1152]{1,0:T(8,128)(2,1)}, u32[]{:S(2)}, u32[]{:S(2)}) collective-permute-start(bf16[1152,1152]{1,0:T(8,128)(2,1)} %pad_maximum_fusion.4.refs_7_.refs_6_.refs_14_), channel_id=1, source_target_pairs={{0,8},{4,20},{8,0},{12,28},{16,24},{20,4},{24,16},{28,12},{1,9},{5... | collective-permute-start | bytes 7962632 | tf_op jit(solution)/shard_map/ppermute | solution.py:286
  144.3 37.6 %collective-permute-start.18 = (bf16[1152,1152]{1,0:T(8,128)(2,1)}, bf16[1152,1152]{1,0:T(8,128)(2,1)}, u32[]{:S(2)}, u32[]{:S(2)}) collective-permute-start(bf16[1152,1152]{1,0:T(8,128)(2,1)} %pad_maximum_fusion.4.refs_7_.refs_6_.refs_14_), channel_id=1, source_target_pairs={{0,4},{4,0},{8,12},{12,8},{16,20},{20,16},{24,28},{28,24},{1,5},{5... | collective-permute-start | bytes 7962632 | tf_op jit(solution)/shard_map/ppermute | solution.py:282
  164.4 33.2 %collective-permute-start.19 = (bf16[1152,1152]{1,0:T(8,128)(2,1)}, bf16[1152,1152]{1,0:T(8,128)(2,1)}, u32[]{:S(2)}, u32[]{:S(2)}) collective-permute-start(bf16[1152,1152]{1,0:T(8,128)(2,1)} %collective-permute-done.17.refs_15_), channel_id=1, source_target_pairs={{0,4},{4,0},{8,12},{12,8},{16,20},{20,16},{24,28},{28,24},{1,5},{5... | collective-permute-start | bytes 7962632 | tf_op jit(solution)/shard_map/ppermute | solution.py:282
  197.0 77.2 %collective-permute-start.27 = (bf16[1152,1152]{1,0:T(8,128)(2,1)}, bf16[1152,1152]{1,0:T(8,128)(2,1)}, u32[]{:S(2)}, u32[]{:S(2)}) collective-permute-start(bf16[1152,1152]{1,0:T(8,128)(2,1)} %get-tuple-element.77), channel_id=1, source_target_pairs={{0,4},{4,0},{8,12},{12,8},{16,20},{20,16},{24,28},{28,24},{1,5},{5... | collective-permute-start | bytes 7962632 | tf_op jit(solution)/shard_map/ppermute | solution.py:282
  197.1 41.2 %collective-permute-start.21 = (bf16[1152,1152]{1,0:T(8,128)(2,1)}, bf16[1152,1152]{1,0:T(8,128)(2,1)}, u32[]{:S(2)}, u32[]{:S(2)}) collective-permute-start(bf16[1152,1152]{1,0:T(8,128)(2,1)} %get-tuple-element.71), channel_id=1, source_target_pairs={{0,4},{4,0},{8,12},{12,8},{16,20},{20,16},{24,28},{28,24},{1,5},{5... | collective-permute-start | bytes 7962632 | tf_op jit(solution)/shard_map/ppermute | solution.py:282
  243.9 31.5 %collective-permute-start.28 = (bf16[1152,1152]{1,0:T(8,128)(2,1)}, bf16[1152,1152]{1,0:T(8,128)(2,1)}, u32[]{:S(2)}, u32[]{:S(2)}) collective-permute-start(bf16[1152,1152]{1,0:T(8,128)(2,1)} %add_convert_fusion.5.refs_2_), channel_id=1, source_target_pairs={{0,8},{4,20},{8,0},{12,28},{16,24},{20,4},{24,16},{28,12},{1,9},{5... | collective-permute-start | bytes 7962632 | tf_op jit(solution)/shard_map/ppermute | solution.py:286
  260.2 27.8 %collective-permute-start.26 = (bf16[1152,1152]{1,0:T(8,128)(2,1)}, bf16[1152,1152]{1,0:T(8,128)(2,1)}, u32[]{:S(2)}, u32[]{:S(2)}) collective-permute-start(bf16[1152,1152]{1,0:T(8,128)(2,1)} %get-tuple-element.76), channel_id=1, source_target_pairs={{0,4},{4,0},{8,12},{12,8},{16,20},{20,16},{24,28},{28,24},{1,5},{5... | collective-permute-start | bytes 7962632 | tf_op jit(solution)/shard_map/ppermute | solution.py:282
  293.8 70.5 %collective-permute-start.30 = (bf16[1152,1152]{1,0:T(8,128)(2,1)}, bf16[1152,1152]{1,0:T(8,128)(2,1)}, u32[]{:S(2)}, u32[]{:S(2)}) collective-permute-start(bf16[1152,1152]{1,0:T(8,128)(2,1)} %add_convert_fusion.3.refs_7_), channel_id=1, source_target_pairs={{0,8},{4,20},{8,0},{12,28},{16,24},{20,4},{24,16},{28,12},{1,9},{5... | collective-permute-start | bytes 7962632 | tf_op jit(solution)/shard_map/ppermute | solution.py:286
  310.7 28.2 %collective-permute-start.58 = (bf16[144,1152]{1,0:T(8,128)(2,1)}, bf16[144,1152]{1,0:T(8,128)(2,1)}, u32[]{:S(2)}, u32[]{:S(2)}) collective-permute-start(bf16[144,1152]{1,0:T(8,128)(2,1)} %get-tuple-element.106), channel_id=1, source_target_pairs={{0,3},{1,0},{2,1},{3,2},{4,7},{5,4},{6,5},{7,6},{8,11},{9,8},{10,9... | collective-permute-start | bytes 995336 | tf_op jit(solution)/shard_map/ppermute | solution.py:257
  351.7 27.6 %collective-permute-start.24 = (bf16[2,288,256]{2,1,0:T(8,128)(2,1)}, bf16[2,288,256]{2,1,0:T(8,128)(2,1)}, u32[]{:S(2)}, u32[]{:S(2)}) collective-permute-start(bf16[2,288,256]{2,1,0:T(8,128)(2,1)} %get-tuple-element.113), channel_id=1, source_target_pairs={{0,1},{1,2},{2,3},{3,0},{4,5},{5,6},{6,7},{7,4},{8,9},{9,10},{10,1... | collective-permute-start | bytes 884744 | tf_op jit(solution)/shard_map/ppermute | solution.py:257
  351.7 27.7 %collective-permute-start.31 = (bf16[2,288,256]{2,1,0:T(8,128)(2,1)}, bf16[2,288,256]{2,1,0:T(8,128)(2,1)}, u32[]{:S(2)}, u32[]{:S(2)}) collective-permute-start(bf16[2,288,256]{2,1,0:T(8,128)(2,1)} %get-tuple-element.112), channel_id=1, source_target_pairs={{0,2},{1,3},{2,0},{3,1},{4,6},{5,7},{6,4},{7,5},{8,10},{9,11},{10,... | collective-permute-start | bytes 884744 | tf_op jit(solution)/shard_map/ppermute | solution.py:257
  351.7 27.7 %collective-permute-start.32 = (bf16[2,288,256]{2,1,0:T(8,128)(2,1)}, bf16[2,288,256]{2,1,0:T(8,128)(2,1)}, u32[]{:S(2)}, u32[]{:S(2)}) collective-permute-start(bf16[2,288,256]{2,1,0:T(8,128)(2,1)} %get-tuple-element.111), channel_id=1, source_target_pairs={{0,3},{1,0},{2,1},{3,2},{4,7},{5,4},{6,5},{7,6},{8,11},{9,8},{10,9... | collective-permute-start | bytes 884744 | tf_op jit(solution)/shard_map/ppermute | solution.py:257
  359.0 76.3 %collective-permute-start.61 = (bf16[4,144,1152]{2,1,0:T(8,128)(2,1)}, bf16[4,144,1152]{2,1,0:T(8,128)(2,1)}, u32[]{:S(2)}, u32[]{:S(2)}) collective-permute-start(bf16[4,144,1152]{2,1,0:T(8,128)(2,1)} %pad_maximum_fusion.10), channel_id=1, source_target_pairs={{0,4},{4,0},{8,12},{12,8},{16,20},{20,16},{24,28},{28,24},{1,5},{5... | collective-permute-start | bytes 3981320 | tf_op jit(solution)/shard_map/ppermute | solution.py:282
  399.2 150.3 %reduce-scatter.5.cloned.1.call-start = ((), (), s32[]{:S(2)}) async-start(), calls=%async_computation.5 | async-start | bytes 5898240 | tf_op jit(solution)/shard_map/reduce_scatter | solution.py:916
  423.2 31.2 %collective-permute-start.43 = (bf16[544,1152]{1,0:T(8,128)(2,1)}, bf16[544,1152]{1,0:T(8,128)(2,1)}, u32[]{:S(2)}, u32[]{:S(2)}) collective-permute-start(bf16[544,1152]{1,0:T(8,128)(2,1)} %bitcast.211), channel_id=1, source_target_pairs={{0,4},{4,0},{8,12},{12,8},{16,20},{20,16},{24,28},{28,24},{1,5},{5... | collective-permute-start | bytes 3760136 | tf_op jit(solution)/shard_map/ppermute | solution.py:282
  468.8 53.3 %collective-permute-start.40 = (bf16[72,1152]{1,0:T(8,128)(2,1)S(1)}, bf16[72,1152]{1,0:T(8,128)(2,1)S(1)}, u32[]{:S(2)}, u32[]{:S(2)}) collective-permute-start(bf16[72,1152]{1,0:T(8,128)(2,1)S(1)} %maximum_maximum_fusion.1), channel_id=1, source_target_pairs={{1,0},{2,1},{3,2},{0,3},{5,4},{6,5},{7,6},{4,7},{9,8},{10,9},{11,1... | collective-permute-start | bytes 497672 | tf_op jit(solution)/shard_map/ppermute | solution.py:253
  470.3 51.9 %collective-permute-start.41 = (bf16[72,1152]{1,0:T(8,128)(2,1)S(1)}, bf16[72,1152]{1,0:T(8,128)(2,1)S(1)}, u32[]{:S(2)}, u32[]{:S(2)}) collective-permute-start(bf16[72,1152]{1,0:T(8,128)(2,1)S(1)} %maximum_maximum_fusion.1), channel_id=1, source_target_pairs={{2,0},{3,1},{0,2},{1,3},{6,4},{7,5},{4,6},{5,7},{10,8},{11,9},{8,1... | collective-permute-start | bytes 497672 | tf_op jit(solution)/shard_map/ppermute | solution.py:253
  474.4 47.8 %collective-permute-start.42 = (bf16[72,1152]{1,0:T(8,128)(2,1)S(1)}, bf16[72,1152]{1,0:T(8,128)(2,1)S(1)}, u32[]{:S(2)}, u32[]{:S(2)}) collective-permute-start(bf16[72,1152]{1,0:T(8,128)(2,1)S(1)} %maximum_maximum_fusion.1), channel_id=1, source_target_pairs={{3,0},{0,1},{1,2},{2,3},{7,4},{4,5},{5,6},{6,7},{11,8},{8,9},{9,10... | collective-permute-start | bytes 497672 | tf_op jit(solution)/shard_map/ppermute | solution.py:253
  (107 other events, 1119.8 us)
Sparse Core Ops, SparseCore 0:
  10.3 42.8 all-gather.2
  54.7 33.9 all-gather.4
  399.3 32.5 reduce-scatter.2
  434.1 106.6 reduce-scatter.4
